TPU v7x, 32 devices: a whole 2x2x4 slice. The times are simulated.
32 devices in a mesh: outer: 16 (over z, y, core), inner: 2 (over x).
Axes of the slice: x: 2, y: 2, z: 4, core: 2. Of those that a mesh axis runs over, the one named last changes fastest.
Arguments:
- queries: bfloat16 [4096, 1024], P(('outer', 'inner')), may hold values from -9 to 9
- keys: bfloat16 [4096, 128], P(('outer', 'inner')), may hold values from -9 to 9
- values: bfloat16 [4096, 128], P(('outer', 'inner')), may hold values from -6 to 6
- grad_out: bfloat16 [4096, 1024], P(('outer', 'inner')), may hold values from -6 to 6
- doc_lengths: int32 [16], replicated, may hold values from 1 to 1024, 4096 in all
Outputs:
- grad_queries: bfloat16 [4096, 1024], P(('outer', 'inner'))
- grad_keys: bfloat16 [4096, 128], P(('outer', 'inner'))
- grad_values: bfloat16 [4096, 128], P(('outer', 'inner'))
Inputs may be any that keep to these rules, and one draw needn't show every extreme that they name: `doc_lengths`: the lengths sum to 4096; the longest document has exactly 1024 tokens.
All inputs are finite; a program needn't handle non-finite values.
Results may differ from a plain program's by a relative error of at most 0.0074.
Values may be sent and summed in bfloat16 or wider, within the bound.
No kernel may reach another device: no remote copies, remote signals or barrier semaphores. Data moves between devices by JAX's collectives and lax.ppermute only.
A program may use at most 128 MiB of HBM per device.

v0:
```python
import math

import jax
import jax.numpy as jnp
from jax import lax
from jax.sharding import PartitionSpec as P

REACH = 4


NEG = -1e30


def shifted(value, axis, steps):
    count = lax.axis_size(axis)
    first, last = (max(0, -steps), min(count, count - steps))
    return lax.ppermute(value, axis, [(source, source + steps) for source in range(first, last)])


def doc_of(positions, doc_lengths):
    ends = jnp.cumsum(doc_lengths)
    return jnp.sum((positions[:, None] >= ends[None, :]).astype(jnp.int32), axis=1)


def allowed(query_pos, key_pos, doc_lengths):
    same = doc_of(query_pos, doc_lengths)[:, None] == doc_of(key_pos, doc_lengths)[None, :]
    return (same & (key_pos[None, :] <= query_pos[:, None]) & (key_pos[None, :] >= 0))[:, None, :]


def score_block(query_blk, key_grp, scale):
    return jnp.einsum("thd,kd->thk", query_blk, key_grp, preferred_element_type=jnp.float32) * scale


def partial_forward(scores, mask3, val_grp):
    peak = jnp.max(jnp.where(mask3, scores, NEG), axis=-1)
    weights = jnp.where(mask3, jnp.exp(scores - peak[..., None]), 0.0)
    total = jnp.sum(weights, axis=-1)
    summed = jnp.einsum(
        "thk,kd->thd", weights, val_grp.astype(jnp.float32), precision=lax.Precision.HIGHEST
    )
    return (peak, total, summed)


def combine_stats(partials, grad_rows):
    peak = partials[0][0]
    for entry in partials[1:]:
        peak = jnp.maximum(peak, entry[0])
    total = jnp.zeros_like(peak)
    summed = jnp.zeros(grad_rows.shape, jnp.float32)
    for entry in partials:
        factor = jnp.exp(entry[0] - peak)
        total = total + entry[1] * factor
        summed = summed + entry[2] * factor[..., None]
    lse = peak + jnp.log(total)
    attended = summed / total[..., None]
    delta = jnp.sum(grad_rows.astype(jnp.float32) * attended, axis=-1)
    return (lse, delta)


def backward_block(scores, mask3, lse, delta, query_blk, grad_blk, key_grp, val_grp):
    probs = jnp.where(mask3, jnp.exp(scores - lse[..., None]), 0.0)
    probs_low = probs.astype(jnp.bfloat16)
    dv_part = jnp.einsum("thk,thd->kd", probs_low, grad_blk, preferred_element_type=jnp.float32)
    dprobs = jnp.einsum("thd,kd->thk", grad_blk, val_grp, preferred_element_type=jnp.float32)
    dscores = (probs * (dprobs - delta[..., None])).astype(jnp.bfloat16)
    dq_part = jnp.einsum("thk,kd->thd", dscores, key_grp, preferred_element_type=jnp.float32)
    dk_part = jnp.einsum("thk,thd->kd", dscores, query_blk, preferred_element_type=jnp.float32)
    return (dq_part, dk_part, dv_part)


def gather_group(keys, values):
    return (
        lax.all_gather(keys, "inner", axis=0, tiled=True),
        lax.all_gather(values, "inner", axis=0, tiled=True),
    )


def visit_later(query_blk, grad_blk, step):
    return shifted((query_blk, grad_blk), "outer", -step)


def return_stats(peak, total, summed, step):
    return shifted((peak, total, summed), "outer", step)


def forward_stats(lse, delta, step):
    return shifted((lse, delta), "outer", -step)


def return_query_grads(dq_part, step):
    return shifted(dq_part, "outer", step)


def on_device(queries, keys, values, grad_out, doc_lengths):
    tokens, head_dim = keys.shape
    heads = queries.shape[1] // head_dim
    scale = 1.0 / math.sqrt(head_dim)
    n_inner = lax.axis_size("inner")
    outer_at = lax.axis_index("outer")
    inner_at = lax.axis_index("inner")
    group = tokens * n_inner
    offsets = jnp.arange(tokens, dtype=jnp.int32)
    group_offsets = jnp.arange(group, dtype=jnp.int32)
    own_query = queries.reshape(tokens, heads, head_dim)
    own_grad = grad_out.reshape(tokens, heads, head_dim)
    own_pos = (outer_at * n_inner + inner_at) * tokens + offsets
    key_grp, val_grp = gather_group(keys, values)
    key_pos = outer_at * group + group_offsets
    blocks = []
    for step in range(REACH + 1):
        if step == 0:
            query_blk, grad_blk = (own_query, own_grad)
        else:
            query_blk, grad_blk = visit_later(own_query, own_grad, step)
        mask3 = allowed(own_pos + step * group, key_pos, doc_lengths)
        scores = score_block(query_blk, key_grp, scale)
        blocks.append((query_blk, grad_blk, mask3, scores, partial_forward(scores, mask3, val_grp)))
    partials = [blocks[0][4]]
    for step in range(1, REACH + 1):
        peak, total, summed = return_stats(
            blocks[step][4][0], blocks[step][4][1], blocks[step][4][2], step
        )
        peak = jnp.where(outer_at - step >= 0, peak, NEG)
        partials.append((peak, total, summed))
    lse, delta = combine_stats(partials, own_grad)
    dq_total = jnp.zeros((tokens, heads, head_dim), jnp.float32)
    dk_acc = jnp.zeros((group, head_dim), jnp.float32)
    dv_acc = jnp.zeros((group, head_dim), jnp.float32)
    for step in range(REACH + 1):
        query_blk, grad_blk, mask3, scores, unused = blocks[step]
        if step == 0:
            lse_blk, delta_blk = (lse, delta)
        else:
            lse_blk, delta_blk = forward_stats(lse, delta, step)
        dq_part, dk_part, dv_part = backward_block(
            scores, mask3, lse_blk, delta_blk, query_blk, grad_blk, key_grp, val_grp
        )
        dk_acc = dk_acc + dk_part
        dv_acc = dv_acc + dv_part
        if step == 0:
            dq_total = dq_part
        else:
            dq_total = dq_total + return_query_grads(dq_part, step)
    dk_own, dv_own = (
        lax.psum_scatter(dk_acc, "inner", scatter_dimension=0, tiled=True),
        lax.psum_scatter(dv_acc, "inner", scatter_dimension=0, tiled=True),
    )
    grad_queries = (dq_total * scale).astype(jnp.bfloat16).reshape(tokens, heads * head_dim)
    grad_keys = (dk_own * scale).astype(jnp.bfloat16)
    grad_values = dv_own.astype(jnp.bfloat16)
    return (grad_queries, grad_keys, grad_values)


def solution(mesh):
    in_specs = (
        P(("outer", "inner"), None),
        P(("outer", "inner"), None),
        P(("outer", "inner"), None),
        P(("outer", "inner"), None),
        P(),
    )
    out_specs = (
        P(("outer", "inner"), None),
        P(("outer", "inner"), None),
        P(("outer", "inner"), None),
    )
    return jax.shard_map(
        on_device, mesh=mesh, in_specs=in_specs, out_specs=out_specs, check_vma=False
    )
```

profile of v0, /device:TPU:27, one launch (start us, length us, event | category | flops | bytes accessed | tf_op | source)
XLA Modules:
  0.0 211.2 jit_solution(2241900543734723677)
XLA Ops:
  9.2 2.9 %collective-permute-start.6 = (bf16[128,8,128]{2,0,1:T(8,128)(2,1)}, bf16[128,8,128]{2,0,1:T(8,128)(2,1)}, u32[]{:S(2)}, u32[]{:S(2)}) collective-permute-start(bf16[128,8,128]{2,0,1:T(8,128)(2,1)} %copy.84), channel_id=1, source_target_pairs={{8,0},{10,2},{12,4},{14,6},{16,8},{18,10},{20,12},{22,14},{24,16},... | collective-permute-start | bytes 786440 | tf_op jit(solution)/shard_map/ppermute | solution.py:17
  12.1 3.2 %collective-permute-start.4 = (bf16[128,8,128]{2,0,1:T(8,128)(2,1)}, bf16[128,8,128]{2,0,1:T(8,128)(2,1)S(1)}, u32[]{:S(2)}, u32[]{:S(2)}) collective-permute-start(bf16[128,8,128]{2,0,1:T(8,128)(2,1)} %copy.84), channel_id=1, source_target_pairs={{6,0},{8,2},{10,4},{12,6},{14,8},{16,10},{18,12},{20,14},{22,16},{... | collective-permute-start | bytes 786440 | tf_op jit(solution)/shard_map/ppermute | solution.py:17
  15.3 2.1 %collective-permute-start.2 = (bf16[128,8,128]{2,0,1:T(8,128)(2,1)}, bf16[128,8,128]{2,0,1:T(8,128)(2,1)S(1)}, u32[]{:S(2)}, u32[]{:S(2)}) collective-permute-start(bf16[128,8,128]{2,0,1:T(8,128)(2,1)} %copy.84), channel_id=1, source_target_pairs={{4,0},{6,2},{8,4},{10,6},{12,8},{14,10},{16,12},{18,14},{20,16},{2... | collective-permute-start | bytes 786440 | tf_op jit(solution)/shard_map/ppermute | solution.py:17
  17.4 2.1 collective-permute-start
  19.9 3.7 %all_gather.6 = bf16[256,128]{1,0:T(8,128)(2,1)S(1)} all-gather(bf16[128,128]{1,0:T(8,128)(2,1)S(1)} %copy-done.37), channel_id=1, replica_groups=mesh['outer'=16,'inner'=2] {'inner'}, dimensions={0}, use_global_device_ids=true | all-gather | bytes 98304 | tf_op jit(solution)/shard_map/all_gather | solution.py:73
  26.5 3.4 %all_gather.7 = bf16[256,128]{1,0:T(8,128)(2,1)S(1)} all-gather(bf16[128,128]{1,0:T(8,128)(2,1)S(1)} %copy-done.38), channel_id=1, replica_groups=mesh['outer'=16,'inner'=2] {'inner'}, dimensions={0}, use_global_device_ids=true | all-gather | bytes 98304 | tf_op jit(solution)/shard_map/all_gather | solution.py:74
  31.0 5.5 %collective-permute-start.1 = (f32[128,8]{0,1:T(8,128)S(1)}, f32[128,8]{0,1:T(8,128)S(1)}, u32[]{:S(2)}, u32[]{:S(2)}) collective-permute-start(f32[128,8]{0,1:T(8,128)S(1)} %get-tuple-element.35), channel_id=1, source_target_pairs={{0,2},{2,4},{4,6},{6,8},{8,10},{10,12},{12,14},{14,16},{16,18},{18... | collective-permute-start | bytes 12296 | tf_op jit(solution)/shard_map/ppermute | solution.py:17
  36.9 1.9 collective-permute-start.8
  38.8 1.7 fusion.25
  41.3 1.9 collective-permute-start.3
  43.6 1.7 fusion.27
  46.0 1.4 select_reduce_fusion.1
  49.1 1.7 fusion.29
  50.8 1.9 collective-permute-start.9
  52.8 1.4 select_reduce_fusion
  54.6 1.4 collective-permute-start.7
  56.0 1.3 collective-permute-start.10
  57.3 1.3 collective-permute-start.11
  58.6 1.7 fusion.31
  60.4 7.2 %collective-permute-start.29 = (bf16[128,8,128]{0,2,1:T(8,128)(2,1)S(1)}, bf16[128,8,128]{0,2,1:T(8,128)(2,1)S(1)}, u32[]{:S(2)}, u32[]{:S(2)}) collective-permute-start(bf16[128,8,128]{0,2,1:T(8,128)(2,1)S(1)} %bitcast.131), channel_id=1, source_target_pairs={{8,0},{10,2},{12,4},{14,6},{16,8},{18,10},{20,12},{22,14},{24,16},... | collective-permute-start | bytes 786440 | tf_op jit(solution)/shard_map/ppermute | solution.py:17
  67.6 5.2 %collective-permute-start.25 = (bf16[128,8,128]{0,2,1:T(8,128)(2,1)S(1)}, bf16[128,8,128]{0,2,1:T(8,128)(2,1)S(1)}, u32[]{:S(2)}, u32[]{:S(2)}) collective-permute-start(bf16[128,8,128]{0,2,1:T(8,128)(2,1)S(1)} %bitcast.132), channel_id=1, source_target_pairs={{6,0},{8,2},{10,4},{12,6},{14,8},{16,10},{18,12},{20,14},{22,16},{... | collective-permute-start | bytes 786440 | tf_op jit(solution)/shard_map/ppermute | solution.py:17
  72.7 3.0 %collective-permute-start.21 = (bf16[128,8,128]{0,2,1:T(8,128)(2,1)S(1)}, bf16[128,8,128]{0,2,1:T(8,128)(2,1)S(1)}, u32[]{:S(2)}, u32[]{:S(2)}) collective-permute-start(bf16[128,8,128]{0,2,1:T(8,128)(2,1)S(1)} %bitcast.133), channel_id=1, source_target_pairs={{4,0},{6,2},{8,4},{10,6},{12,8},{14,10},{16,12},{18,14},{20,16},{2... | collective-permute-start | bytes 786440 | tf_op jit(solution)/shard_map/ppermute | solution.py:17
  75.7 2.1 collective-permute-start.17
  78.4 3.7 %collective-permute-start.20 = (f32[128,8]{0,1:T(8,128)S(1)}, f32[128,8]{0,1:T(8,128)S(1)}, u32[]{:S(2)}, u32[]{:S(2)}) collective-permute-start(f32[128,8]{0,1:T(8,128)S(1)} %get-tuple-element.17), channel_id=1, source_target_pairs={{4,0},{6,2},{8,4},{10,6},{12,8},{14,10},{16,12},{18,14},{20,16},{2... | collective-permute-start | bytes 12296 | tf_op jit(solution)/shard_map/ppermute | solution.py:17
  82.7 1.8 collective-permute-done.21
  84.5 2.2 %collective-permute-start.12 = (f32[128,8,128]{0,2,1:T(8,128)}, f32[128,8,128]{0,2,1:T(8,128)}, u32[]{:S(2)}, u32[]{:S(2)}) collective-permute-start(f32[128,8,128]{0,2,1:T(8,128)} %fusion.25), channel_id=1, source_target_pairs={{0,2},{2,4},{4,6},{6,8},{8,10},{10,12},{12,14},{14,16},{16,18},{18... | collective-permute-start | bytes 1572872 | tf_op jit(solution)/shard_map/ppermute | solution.py:17
  86.7 6.3 %collective-permute-start.24 = (f32[128,8]{0,1:T(8,128)S(1)}, f32[128,8]{0,1:T(8,128)S(1)}, u32[]{:S(2)}, u32[]{:S(2)}) collective-permute-start(f32[128,8]{0,1:T(8,128)S(1)} %get-tuple-element.17), channel_id=1, source_target_pairs={{6,0},{8,2},{10,4},{12,6},{14,8},{16,10},{18,12},{20,14},{22,16},{... | collective-permute-start | bytes 12296 | tf_op jit(solution)/shard_map/ppermute | solution.py:17
  93.6 1.9 collective-permute-start.13
  95.6 1.3 collective-permute-start.14
  96.9 1.3 collective-permute-start.15
  98.2 5.6 %collective-permute-start.28 = (f32[128,8]{0,1:T(8,128)S(1)}, f32[128,8]{0,1:T(8,128)S(1)}, u32[]{:S(2)}, u32[]{:S(2)}) collective-permute-start(f32[128,8]{0,1:T(8,128)S(1)} %get-tuple-element.17), channel_id=1, source_target_pairs={{8,0},{10,2},{12,4},{14,6},{16,8},{18,10},{20,12},{22,14},{24,16},... | collective-permute-start | bytes 12296 | tf_op jit(solution)/shard_map/ppermute | solution.py:17
  104.5 3.4 %collective-permute-start.16 = (f32[128,8]{0,1:T(8,128)S(1)}, f32[128,8]{0,1:T(8,128)S(1)}, u32[]{:S(2)}, u32[]{:S(2)}) collective-permute-start(f32[128,8]{0,1:T(8,128)S(1)} %get-tuple-element.17), channel_id=1, source_target_pairs={{2,0},{4,2},{6,4},{8,6},{10,8},{12,10},{14,12},{16,14},{18,16},{20... | collective-permute-start | bytes 12296 | tf_op jit(solution)/shard_map/ppermute | solution.py:17
  108.5 1.8 collective-permute-done.16
  111.7 10.1 %collective-permute-done.14 = f32[128,8,128]{0,2,1:T(8,128)} collective-permute-done((f32[128,8,128]{0,2,1:T(8,128)}, f32[128,8,128]{0,2,1:T(8,128)}, u32[]{:S(2)}, u32[]{:S(2)}) %collective-permute-start.14) | collective-permute-done | bytes 524320 | tf_op jit(solution)/shard_map/ppermute | solution.py:17
  122.5 3.2 %multiply_reduce_fusion = f32[128,8]{0,1:T(8,128)S(1)} fusion(f32[128,8,128]{0,2,1:T(8,128)} %collective-permute-done.15, f32[128,8,128]{0,2,1:T(8,128)} %collective-permute-done.14, f32[128,8,128]{0,2,1:T(8,128)} %collective-permute-done.13, f32[128,8,128]{0,2,1:T(8,128)} %collective-permute-done.12, bf16[128,8,128]{0,2,1:T(8,128)(2,1)} %bitcast.130, ...), kind=kOutput, calls=%fused_computation.78 | convolution fusion | flops 404880384 | bytes 3538944 | tf_op jit(solution)/shard_map/thk,kd->thd/dot_general | solution.py:38
  125.7 4.3 %collective-permute-start.30 = (f32[128,8]{0,1:T(8,128)S(1)}, f32[128,8]{0,1:T(8,128)S(1)}, u32[]{:S(2)}, u32[]{:S(2)}) collective-permute-start(f32[128,8]{0,1:T(8,128)S(1)} %multiply_reduce_fusion), channel_id=1, source_target_pairs={{8,0},{10,2},{12,4},{14,6},{16,8},{18,10},{20,12},{22,14},{24,16},... | collective-permute-start | bytes 12296 | tf_op jit(solution)/shard_map/ppermute | solution.py:17
  130.0 15.2 %collective-permute-start.26 = (f32[128,8]{0,1:T(8,128)S(1)}, f32[128,8]{0,1:T(8,128)S(1)}, u32[]{:S(2)}, u32[]{:S(2)}) collective-permute-start(f32[128,8]{0,1:T(8,128)S(1)} %multiply_reduce_fusion), channel_id=1, source_target_pairs={{6,0},{8,2},{10,4},{12,6},{14,8},{16,10},{18,12},{20,14},{22,16},{... | collective-permute-start | bytes 12296 | tf_op jit(solution)/shard_map/ppermute | solution.py:17
  145.2 1.9 collective-permute-start.22
  147.2 2.3 %collective-permute-start.18 = (f32[128,8]{0,1:T(8,128)S(1)}, f32[128,8]{0,1:T(8,128)S(1)}, u32[]{:S(2)}, u32[]{:S(2)}) collective-permute-start(f32[128,8]{0,1:T(8,128)S(1)} %multiply_reduce_fusion), channel_id=1, source_target_pairs={{2,0},{4,2},{6,4},{8,6},{10,8},{12,10},{14,12},{16,14},{18,16},{20... | collective-permute-start | bytes 12296 | tf_op jit(solution)/shard_map/ppermute | solution.py:17
  156.3 3.4 %collective-permute-start.19 = (f32[128,8,128]{0,2,1:T(8,128)S(1)}, f32[128,8,128]{0,2,1:T(8,128)S(1)}, u32[]{:S(2)}, u32[]{:S(2)}) collective-permute-start(f32[128,8,128]{0,2,1:T(8,128)S(1)} %fusion.92), channel_id=1, source_target_pairs={{0,2},{2,4},{4,6},{6,8},{8,10},{10,12},{12,14},{14,16},{16,18},{18... | collective-permute-start | bytes 1572872 | tf_op jit(solution)/shard_map/ppermute | solution.py:17
  162.3 1.9 collective-permute-start.23
  164.9 1.3 convolution_bitcast_fusion.5
  167.3 1.5 convert_element_type.88
  168.8 11.5 %reduce-scatter.3.cloned.1.call-done = f32[128,128]{1,0:T(8,128)} async-done(((f32[256,128]{1,0:T(8,128)}), f32[128,128]{1,0:T(8,128)}) %reduce-scatter.3.cloned.1.call-update) | async-done | bytes 65552 | tf_op jit(solution)/shard_map/reduce_scatter | solution.py:145
  180.3 1.5 multiply_convert_fusion
  181.8 5.1 %collective-permute-done.27 = f32[128,8,128]{0,2,1:T(8,128)} collective-permute-done((f32[128,8,128]{0,2,1:T(8,128)S(1)}, f32[128,8,128]{0,2,1:T(8,128)}, u32[]{:S(2)}, u32[]{:S(2)}) %collective-permute-start.27) | collective-permute-done | bytes 524320 | tf_op jit(solution)/shard_map/ppermute | solution.py:17
  186.9 14.9 %collective-permute-done.23 = f32[128,8,128]{0,2,1:T(8,128)} collective-permute-done((f32[128,8,128]{0,2,1:T(8,128)S(1)}, f32[128,8,128]{0,2,1:T(8,128)}, u32[]{:S(2)}, u32[]{:S(2)}) %collective-permute-start.23) | collective-permute-done | bytes 524320 | tf_op jit(solution)/shard_map/ppermute | solution.py:17
  201.8 1.7 fusion.14
  (169 shorter events, 27.4 us)
Async XLA Ops:
  7.2 160.1 %reduce-scatter.5.cloned.1.call-start = ((), (), s32[]{:S(2)}) async-start(), calls=%async_computation.3 | async-start | bytes 196608 | tf_op jit(solution)/shard_map/reduce_scatter | solution.py:146
  8.3 11.3 %copy-start.45 = (s32[16]{0:T(128)S(1)}, s32[16]{0:T(128)}, u32[]{:S(2)}) copy-start(s32[16]{0:T(128)} %param.9) | copy-start | bytes 196
  9.2 10.7 %copy-start.37 = (bf16[128,128]{1,0:T(8,128)(2,1)S(1)}, bf16[128,128]{1,0:T(8,128)(2,1)}, u32[]{:S(2)}) copy-start(bf16[128,128]{1,0:T(8,128)(2,1)} %param.6) | copy-start | bytes 98308
  9.2 41.6 %collective-permute-start.6 = (bf16[128,8,128]{2,0,1:T(8,128)(2,1)}, bf16[128,8,128]{2,0,1:T(8,128)(2,1)}, u32[]{:S(2)}, u32[]{:S(2)}) collective-permute-start(bf16[128,8,128]{2,0,1:T(8,128)(2,1)} %copy.84), channel_id=1, source_target_pairs={{8,0},{10,2},{12,4},{14,6},{16,8},{18,10},{20,12},{22,14},{24,16},... | collective-permute-start | bytes 786440 | tf_op jit(solution)/shard_map/ppermute | solution.py:17
  12.1 33.2 %collective-permute-start.4 = (bf16[128,8,128]{2,0,1:T(8,128)(2,1)}, bf16[128,8,128]{2,0,1:T(8,128)(2,1)S(1)}, u32[]{:S(2)}, u32[]{:S(2)}) collective-permute-start(bf16[128,8,128]{2,0,1:T(8,128)(2,1)} %copy.84), channel_id=1, source_target_pairs={{6,0},{8,2},{10,4},{12,6},{14,8},{16,10},{18,12},{20,14},{22,16},{... | collective-permute-start | bytes 786440 | tf_op jit(solution)/shard_map/ppermute | solution.py:17
  15.3 25.3 %collective-permute-start.2 = (bf16[128,8,128]{2,0,1:T(8,128)(2,1)}, bf16[128,8,128]{2,0,1:T(8,128)(2,1)S(1)}, u32[]{:S(2)}, u32[]{:S(2)}) collective-permute-start(bf16[128,8,128]{2,0,1:T(8,128)(2,1)} %copy.84), channel_id=1, source_target_pairs={{4,0},{6,2},{8,4},{10,6},{12,8},{14,10},{16,12},{18,14},{20,16},{2... | collective-permute-start | bytes 786440 | tf_op jit(solution)/shard_map/ppermute | solution.py:17
  17.4 12.9 %collective-permute-start = (bf16[128,8,128]{2,0,1:T(8,128)(2,1)}, bf16[128,8,128]{2,0,1:T(8,128)(2,1)S(1)}, u32[]{:S(2)}, u32[]{:S(2)}) collective-permute-start(bf16[128,8,128]{2,0,1:T(8,128)(2,1)} %copy.84), channel_id=1, source_target_pairs={{2,0},{4,2},{6,4},{8,6},{10,8},{12,10},{14,12},{16,14},{18,16},{20... | collective-permute-start | bytes 786440 | tf_op jit(solution)/shard_map/ppermute | solution.py:17
  24.6 14.2 %copy-start.7 = (pred[128,256]{1,0:T(8,128)(4,1)}, pred[128,256]{1,0:T(8,128)(4,1)S(1)}, u32[]{:S(2)}) copy-start(pred[128,256]{1,0:T(8,128)(4,1)S(1)} %get-tuple-element.28) | copy-start | bytes 98308
  24.6 19.0 %copy-start.24 = (pred[128,256]{1,0:T(8,128)(4,1)}, pred[128,256]{1,0:T(8,128)(4,1)S(1)}, u32[]{:S(2)}) copy-start(pred[128,256]{1,0:T(8,128)(4,1)S(1)} %get-tuple-element.25) | copy-start | bytes 98308
  31.0 25.0 %collective-permute-start.1 = (f32[128,8]{0,1:T(8,128)S(1)}, f32[128,8]{0,1:T(8,128)S(1)}, u32[]{:S(2)}, u32[]{:S(2)}) collective-permute-start(f32[128,8]{0,1:T(8,128)S(1)} %get-tuple-element.35), channel_id=1, source_target_pairs={{0,2},{2,4},{4,6},{6,8},{8,10},{10,12},{12,14},{14,16},{16,18},{18... | collective-permute-start | bytes 12296 | tf_op jit(solution)/shard_map/ppermute | solution.py:17
  36.9 17.7 %collective-permute-start.8 = (f32[128,8]{0,1:T(8,128)S(1)}, f32[128,8]{0,1:T(8,128)S(1)}, u32[]{:S(2)}, u32[]{:S(2)}) collective-permute-start(f32[128,8]{0,1:T(8,128)S(1)} %fusion.26), channel_id=1, source_target_pairs={{0,2},{2,4},{4,6},{6,8},{8,10},{10,12},{12,14},{14,16},{16,18},{18... | collective-permute-start | bytes 12296 | tf_op jit(solution)/shard_map/ppermute | solution.py:17
  41.3 19.1 %collective-permute-start.3 = (f32[128,8]{0,1:T(8,128)S(1)}, f32[128,8]{0,1:T(8,128)S(1)}, u32[]{:S(2)}, u32[]{:S(2)}) collective-permute-start(f32[128,8]{0,1:T(8,128)S(1)} %get-tuple-element.33), channel_id=1, source_target_pairs={{0,4},{2,6},{4,8},{6,10},{8,12},{10,14},{12,16},{14,18},{16,20},{1... | collective-permute-start | bytes 12296 | tf_op jit(solution)/shard_map/ppermute | solution.py:17
  47.4 25.3 %collective-permute-start.5 = (f32[128,8]{0,1:T(8,128)S(1)}, f32[128,8]{0,1:T(8,128)S(1)}, u32[]{:S(2)}, u32[]{:S(2)}) collective-permute-start(f32[128,8]{0,1:T(8,128)S(1)} %get-tuple-element.31), channel_id=1, source_target_pairs={{0,6},{2,8},{4,10},{6,12},{8,14},{10,16},{12,18},{14,20},{16,22},{... | collective-permute-start | bytes 12296 | tf_op jit(solution)/shard_map/ppermute | solution.py:17
  50.8 6.5 %collective-permute-start.9 = (f32[128,8]{0,1:T(8,128)S(1)}, f32[128,8]{0,1:T(8,128)S(1)}, u32[]{:S(2)}, u32[]{:S(2)}) collective-permute-start(f32[128,8]{0,1:T(8,128)S(1)} %fusion.28), channel_id=1, source_target_pairs={{0,4},{2,6},{4,8},{6,10},{8,12},{10,14},{12,16},{14,18},{16,20},{1... | collective-permute-start | bytes 12296 | tf_op jit(solution)/shard_map/ppermute | solution.py:17
  54.1 53.8 %copy-start = (f32[128,8,256]{2,0,1:T(8,128)}, f32[128,8,256]{2,0,1:T(8,128)S(1)}, u32[]{:S(2)}) copy-start(f32[128,8,256]{2,0,1:T(8,128)S(1)} %get-tuple-element.30) | copy-start | bytes 3145732
  54.6 27.6 %copy-start.3 = (f32[128,8,256]{2,0,1:T(8,128)S(1)}, f32[128,8,256]{2,0,1:T(8,128)}, u32[]{:S(2)}) copy-start(f32[128,8,256]{2,0,1:T(8,128)} %copy-done.2) | copy-start | bytes 3145732
  54.6 23.2 %collective-permute-start.7 = (f32[128,8]{0,1:T(8,128)S(1)}, f32[128,8]{0,1:T(8,128)S(1)}, u32[]{:S(2)}, u32[]{:S(2)}) collective-permute-start(f32[128,8]{0,1:T(8,128)S(1)} %get-tuple-element.29), channel_id=1, source_target_pairs={{0,8},{2,10},{4,12},{6,14},{8,16},{10,18},{12,20},{14,22},{16,24},... | collective-permute-start | bytes 12296 | tf_op jit(solution)/shard_map/ppermute | solution.py:17
  56.0 11.5 %collective-permute-start.10 = (f32[128,8]{0,1:T(8,128)S(1)}, f32[128,8]{0,1:T(8,128)S(1)}, u32[]{:S(2)}, u32[]{:S(2)}) collective-permute-start(f32[128,8]{0,1:T(8,128)S(1)} %fusion.30), channel_id=1, source_target_pairs={{0,6},{2,8},{4,10},{6,12},{8,14},{10,16},{12,18},{14,20},{16,22},{... | collective-permute-start | bytes 12296 | tf_op jit(solution)/shard_map/ppermute | solution.py:17
  57.3 18.4 %collective-permute-start.11 = (f32[128,8]{0,1:T(8,128)S(1)}, f32[128,8]{0,1:T(8,128)S(1)}, u32[]{:S(2)}, u32[]{:S(2)}) collective-permute-start(f32[128,8]{0,1:T(8,128)S(1)} %fusion.32), channel_id=1, source_target_pairs={{0,8},{2,10},{4,12},{6,14},{8,16},{10,18},{12,20},{14,22},{16,24},... | collective-permute-start | bytes 12296 | tf_op jit(solution)/shard_map/ppermute | solution.py:17
  60.4 21.8 %copy-start.28 = (pred[128,256]{1,0:T(8,128)(4,1)S(1)}, pred[128,256]{1,0:T(8,128)(4,1)}, u32[]{:S(2)}) copy-start(pred[128,256]{1,0:T(8,128)(4,1)} %copy-done.27) | copy-start | bytes 98308
  60.4 33.3 %collective-permute-start.29 = (bf16[128,8,128]{0,2,1:T(8,128)(2,1)S(1)}, bf16[128,8,128]{0,2,1:T(8,128)(2,1)S(1)}, u32[]{:S(2)}, u32[]{:S(2)}) collective-permute-start(bf16[128,8,128]{0,2,1:T(8,128)(2,1)S(1)} %bitcast.131), channel_id=1, source_target_pairs={{8,0},{10,2},{12,4},{14,6},{16,8},{18,10},{20,12},{22,14},{24,16},... | collective-permute-start | bytes 786440 | tf_op jit(solution)/shard_map/ppermute | solution.py:17
  67.6 28.0 %collective-permute-start.25 = (bf16[128,8,128]{0,2,1:T(8,128)(2,1)S(1)}, bf16[128,8,128]{0,2,1:T(8,128)(2,1)S(1)}, u32[]{:S(2)}, u32[]{:S(2)}) collective-permute-start(bf16[128,8,128]{0,2,1:T(8,128)(2,1)S(1)} %bitcast.132), channel_id=1, source_target_pairs={{6,0},{8,2},{10,4},{12,6},{14,8},{16,10},{18,12},{20,14},{22,16},{... | collective-permute-start | bytes 786440 | tf_op jit(solution)/shard_map/ppermute | solution.py:17
  72.7 11.8 %collective-permute-start.21 = (bf16[128,8,128]{0,2,1:T(8,128)(2,1)S(1)}, bf16[128,8,128]{0,2,1:T(8,128)(2,1)S(1)}, u32[]{:S(2)}, u32[]{:S(2)}) collective-permute-start(bf16[128,8,128]{0,2,1:T(8,128)(2,1)S(1)} %bitcast.133), channel_id=1, source_target_pairs={{4,0},{6,2},{8,4},{10,6},{12,8},{14,10},{16,12},{18,14},{20,16},{2... | collective-permute-start | bytes 786440 | tf_op jit(solution)/shard_map/ppermute | solution.py:17
  75.7 21.2 %collective-permute-start.17 = (bf16[128,8,128]{0,2,1:T(8,128)(2,1)S(1)}, bf16[128,8,128]{0,2,1:T(8,128)(2,1)S(1)}, u32[]{:S(2)}, u32[]{:S(2)}) collective-permute-start(bf16[128,8,128]{0,2,1:T(8,128)(2,1)S(1)} %bitcast.134), channel_id=1, source_target_pairs={{2,0},{4,2},{6,4},{8,6},{10,8},{12,10},{14,12},{16,14},{18,16},{20... | collective-permute-start | bytes 786440 | tf_op jit(solution)/shard_map/ppermute | solution.py:17
  78.4 14.6 %copy-start.25 = (pred[128,256]{1,0:T(8,128)(4,1)S(1)}, pred[128,256]{1,0:T(8,128)(4,1)}, u32[]{:S(2)}) copy-start(pred[128,256]{1,0:T(8,128)(4,1)} %copy-done.24) | copy-start | bytes 98308
  78.4 8.3 %collective-permute-start.20 = (f32[128,8]{0,1:T(8,128)S(1)}, f32[128,8]{0,1:T(8,128)S(1)}, u32[]{:S(2)}, u32[]{:S(2)}) collective-permute-start(f32[128,8]{0,1:T(8,128)S(1)} %get-tuple-element.17), channel_id=1, source_target_pairs={{4,0},{6,2},{8,4},{10,6},{12,8},{14,10},{16,12},{18,14},{20,16},{2... | collective-permute-start | bytes 12296 | tf_op jit(solution)/shard_map/ppermute | solution.py:17
  84.5 27.2 %collective-permute-start.12 = (f32[128,8,128]{0,2,1:T(8,128)}, f32[128,8,128]{0,2,1:T(8,128)}, u32[]{:S(2)}, u32[]{:S(2)}) collective-permute-start(f32[128,8,128]{0,2,1:T(8,128)} %fusion.25), channel_id=1, source_target_pairs={{0,2},{2,4},{4,6},{6,8},{8,10},{10,12},{12,14},{14,16},{16,18},{18... | collective-permute-start | bytes 1572872 | tf_op jit(solution)/shard_map/ppermute | solution.py:17
  86.7 11.5 %collective-permute-start.24 = (f32[128,8]{0,1:T(8,128)S(1)}, f32[128,8]{0,1:T(8,128)S(1)}, u32[]{:S(2)}, u32[]{:S(2)}) collective-permute-start(f32[128,8]{0,1:T(8,128)S(1)} %get-tuple-element.17), channel_id=1, source_target_pairs={{6,0},{8,2},{10,4},{12,6},{14,8},{16,10},{18,12},{20,14},{22,16},{... | collective-permute-start | bytes 12296 | tf_op jit(solution)/shard_map/ppermute | solution.py:17
  93.6 14.3 %copy-start.31 = (bf16[128,8,128]{0,2,1:T(8,128)(2,1)}, bf16[128,8,128]{0,2,1:T(8,128)(2,1)S(1)}, u32[]{:S(2)}) copy-start(bf16[128,8,128]{0,2,1:T(8,128)(2,1)S(1)} %collective-permute-done.29) | copy-start | bytes 786436
  93.6 18.1 %collective-permute-start.13 = (f32[128,8,128]{0,2,1:T(8,128)}, f32[128,8,128]{0,2,1:T(8,128)}, u32[]{:S(2)}, u32[]{:S(2)}) collective-permute-start(f32[128,8,128]{0,2,1:T(8,128)} %fusion.27), channel_id=1, source_target_pairs={{0,4},{2,6},{4,8},{6,10},{8,12},{10,14},{12,16},{14,18},{16,20},{1... | collective-permute-start | bytes 1572872 | tf_op jit(solution)/shard_map/ppermute | solution.py:17
  95.6 26.3 %collective-permute-start.14 = (f32[128,8,128]{0,2,1:T(8,128)}, f32[128,8,128]{0,2,1:T(8,128)}, u32[]{:S(2)}, u32[]{:S(2)}) collective-permute-start(f32[128,8,128]{0,2,1:T(8,128)} %fusion.29), channel_id=1, source_target_pairs={{0,6},{2,8},{4,10},{6,12},{8,14},{10,16},{12,18},{14,20},{16,22},{... | collective-permute-start | bytes 1572872 | tf_op jit(solution)/shard_map/ppermute | solution.py:17
  96.9 13.4 %copy-start.16 = (bf16[128,8,128]{0,2,1:T(8,128)(2,1)}, bf16[128,8,128]{0,2,1:T(8,128)(2,1)S(1)}, u32[]{:S(2)}) copy-start(bf16[128,8,128]{0,2,1:T(8,128)(2,1)S(1)} %collective-permute-done.17) | copy-start | bytes 786436
  96.9 24.9 %collective-permute-start.15 = (f32[128,8,128]{0,2,1:T(8,128)}, f32[128,8,128]{0,2,1:T(8,128)}, u32[]{:S(2)}, u32[]{:S(2)}) collective-permute-start(f32[128,8,128]{0,2,1:T(8,128)} %fusion.31), channel_id=1, source_target_pairs={{0,8},{2,10},{4,12},{6,14},{8,16},{10,18},{12,20},{14,22},{16,24},... | collective-permute-start | bytes 1572872 | tf_op jit(solution)/shard_map/ppermute | solution.py:17
  98.2 6.3 %collective-permute-start.28 = (f32[128,8]{0,1:T(8,128)S(1)}, f32[128,8]{0,1:T(8,128)S(1)}, u32[]{:S(2)}, u32[]{:S(2)}) collective-permute-start(f32[128,8]{0,1:T(8,128)S(1)} %get-tuple-element.17), channel_id=1, source_target_pairs={{8,0},{10,2},{12,4},{14,6},{16,8},{18,10},{20,12},{22,14},{24,16},... | collective-permute-start | bytes 12296 | tf_op jit(solution)/shard_map/ppermute | solution.py:17
  104.5 5.7 %collective-permute-start.16 = (f32[128,8]{0,1:T(8,128)S(1)}, f32[128,8]{0,1:T(8,128)S(1)}, u32[]{:S(2)}, u32[]{:S(2)}) collective-permute-start(f32[128,8]{0,1:T(8,128)S(1)} %get-tuple-element.17), channel_id=1, source_target_pairs={{2,0},{4,2},{6,4},{8,6},{10,8},{12,10},{14,12},{16,14},{18,16},{20... | collective-permute-start | bytes 12296 | tf_op jit(solution)/shard_map/ppermute | solution.py:17
  111.5 68.8 %reduce-scatter.3.cloned.1.call-start = ((), (), s32[]{:S(2)}) async-start(), calls=%async_computation.2 | async-start | bytes 196608 | tf_op jit(solution)/shard_map/reduce_scatter | solution.py:145
  122.5 26.9 %copy-start.4 = (f32[128,8,256]{2,0,1:T(8,128)S(1)}, f32[128,8,256]{2,0,1:T(8,128)}, u32[]{:S(2)}) copy-start(f32[128,8,256]{2,0,1:T(8,128)} %copy-done.2) | copy-start | bytes 3145732
  122.5 26.9 %copy-start.19 = (bf16[128,1024]{0,1:T(8,128)(2,1)S(1)}, bf16[128,1024]{0,1:T(8,128)(2,1)}, u32[]{:S(2)}) copy-start(bf16[128,1024]{0,1:T(8,128)(2,1)} %copy.88) | copy-start | bytes 786436
  122.5 27.0 %copy-start.29 = (pred[128,256]{1,0:T(8,128)(4,1)S(1)}, pred[128,256]{1,0:T(8,128)(4,1)}, u32[]{:S(2)}) copy-start(pred[128,256]{1,0:T(8,128)(4,1)} %copy-done.27) | copy-start | bytes 98308
  125.7 27.7 %collective-permute-start.30 = (f32[128,8]{0,1:T(8,128)S(1)}, f32[128,8]{0,1:T(8,128)S(1)}, u32[]{:S(2)}, u32[]{:S(2)}) collective-permute-start(f32[128,8]{0,1:T(8,128)S(1)} %multiply_reduce_fusion), channel_id=1, source_target_pairs={{8,0},{10,2},{12,4},{14,6},{16,8},{18,10},{20,12},{22,14},{24,16},... | collective-permute-start | bytes 12296 | tf_op jit(solution)/shard_map/ppermute | solution.py:17
  130.0 22.0 %collective-permute-start.26 = (f32[128,8]{0,1:T(8,128)S(1)}, f32[128,8]{0,1:T(8,128)S(1)}, u32[]{:S(2)}, u32[]{:S(2)}) collective-permute-start(f32[128,8]{0,1:T(8,128)S(1)} %multiply_reduce_fusion), channel_id=1, source_target_pairs={{6,0},{8,2},{10,4},{12,6},{14,8},{16,10},{18,12},{20,14},{22,16},{... | collective-permute-start | bytes 12296 | tf_op jit(solution)/shard_map/ppermute | solution.py:17
  145.2 5.1 %collective-permute-start.22 = (f32[128,8]{0,1:T(8,128)S(1)}, f32[128,8]{0,1:T(8,128)S(1)}, u32[]{:S(2)}, u32[]{:S(2)}) collective-permute-start(f32[128,8]{0,1:T(8,128)S(1)} %multiply_reduce_fusion), channel_id=1, source_target_pairs={{4,0},{6,2},{8,4},{10,6},{12,8},{14,10},{16,12},{18,14},{20,16},{2... | collective-permute-start | bytes 12296 | tf_op jit(solution)/shard_map/ppermute | solution.py:17
  147.2 7.7 %collective-permute-start.18 = (f32[128,8]{0,1:T(8,128)S(1)}, f32[128,8]{0,1:T(8,128)S(1)}, u32[]{:S(2)}, u32[]{:S(2)}) collective-permute-start(f32[128,8]{0,1:T(8,128)S(1)} %multiply_reduce_fusion), channel_id=1, source_target_pairs={{2,0},{4,2},{6,4},{8,6},{10,8},{12,10},{14,12},{16,14},{18,16},{20... | collective-permute-start | bytes 12296 | tf_op jit(solution)/shard_map/ppermute | solution.py:17
  156.3 25.5 %collective-permute-start.19 = (f32[128,8,128]{0,2,1:T(8,128)S(1)}, f32[128,8,128]{0,2,1:T(8,128)S(1)}, u32[]{:S(2)}, u32[]{:S(2)}) collective-permute-start(f32[128,8,128]{0,2,1:T(8,128)S(1)} %fusion.92), channel_id=1, source_target_pairs={{0,2},{2,4},{4,6},{6,8},{8,10},{10,12},{12,14},{14,16},{16,18},{18... | collective-permute-start | bytes 1572872 | tf_op jit(solution)/shard_map/ppermute | solution.py:17
  159.7 22.1 %collective-permute-start.31 = (f32[128,8,128]{0,2,1:T(8,128)S(1)}, f32[128,8,128]{0,2,1:T(8,128)}, u32[]{:S(2)}, u32[]{:S(2)}) collective-permute-start(f32[128,8,128]{0,2,1:T(8,128)S(1)} %fusion.86), channel_id=1, source_target_pairs={{0,8},{2,10},{4,12},{6,14},{8,16},{10,18},{12,20},{14,22},{16,24},... | collective-permute-start | bytes 1572872 | tf_op jit(solution)/shard_map/ppermute | solution.py:17
  161.0 26.0 %collective-permute-start.27 = (f32[128,8,128]{0,2,1:T(8,128)S(1)}, f32[128,8,128]{0,2,1:T(8,128)}, u32[]{:S(2)}, u32[]{:S(2)}) collective-permute-start(f32[128,8,128]{0,2,1:T(8,128)S(1)} %fusion.88), channel_id=1, source_target_pairs={{0,6},{2,8},{4,10},{6,12},{8,14},{10,16},{12,18},{14,20},{16,22},{... | collective-permute-start | bytes 1572872 | tf_op jit(solution)/shard_map/ppermute | solution.py:17
  162.3 39.6 %collective-permute-start.23 = (f32[128,8,128]{0,2,1:T(8,128)S(1)}, f32[128,8,128]{0,2,1:T(8,128)}, u32[]{:S(2)}, u32[]{:S(2)}) collective-permute-start(f32[128,8,128]{0,2,1:T(8,128)S(1)} %fusion.90), channel_id=1, source_target_pairs={{0,4},{2,6},{4,8},{6,10},{8,12},{10,14},{12,16},{14,18},{16,20},{1... | collective-permute-start | bytes 1572872 | tf_op jit(solution)/shard_map/ppermute | solution.py:17
  166.3 35.6 %copy-start.6 = (bf16[128,8,256]{2,0,1:T(8,128)(2,1)S(1)}, bf16[128,8,256]{2,0,1:T(8,128)(2,1)}, u32[]{:S(2)}) copy-start(bf16[128,8,256]{2,0,1:T(8,128)(2,1)} %copy-done.5) | copy-start | bytes 1572868
  (32 other events, 91.6 us)
Sparse Core Ops, SparseCore 0:
  111.6 12.0 reduce-scatter.4
  167.4 12.8 reduce-scatter.2
where the time goes:
time: 213 us; the launch traced here: 211 us
  starting transfers between devices  102 us (48%)
  waiting for transfers between devices  45.5 us (21%)
  matrix products  25.9 us (12%)
  between operations  15.1 us (7%)
  local copies, waits for them, and re-layouts  9.04 us (4%)
  blocking collectives  7.17 us (3%)
  other arithmetic  6.74 us (3%)
    ppermute x32, starting transfers between devices, shifted(): lax.ppermute(value, axis, [(source, source + steps) for source in range(f...  101 us
    ppermute x32, waiting for transfers between devices, shifted(): lax.ppermute(value, axis, [(source, source + steps) for source in range(f...  33.9 us
    reduce_scatter x1, waiting for transfers between devices, on_device(): lax.psum_scatter(dk_acc, 'inner', scatter_dimension=0, tiled=True)  11.5 us
    dot_general x5, matrix products, partial_forward(): jnp.einsum('thk,kd->thd', weights, val_grp.astype(jnp.float32), precision...  10.1 us
    unnamed x95, local copies, waits for them, and re-layouts  8.11 us
  transfers between devices with their start and end apart: 34, of which 7 were waited for; matrix products, arithmetic and copies ran while one was open for 15% of the time, Pallas kernels for 0%

commit v1 on v0

v1 whole, which is shorter than its diff:
```python
import functools
import math

import jax
import jax.numpy as jnp
from jax import lax
from jax.experimental import pallas as pl
from jax.experimental.pallas import tpu as pltpu
from jax.sharding import PartitionSpec as P

REACH = 4
NEG = -1e30
AXES = ("outer", "inner")
LANES_CONTRACT = (((1,), (1,)), ((), ()))
ROWS_CONTRACT = (((0,), (0,)), ((), ()))


def permuted(value, target):
    count = lax.axis_size("outer") * lax.axis_size("inner")
    return lax.ppermute(value, AXES, [(at, target(at, count)) for at in range(count)])


def across_core(at, count):
    return at ^ 2


def across_x(at, count):
    return at ^ 1


def ahead(steps, at, count):
    return ((at + steps) % count) ^ ((at >> 1) & 1)


def behind(steps, at, count):
    return ((at ^ ((at >> 1) & 1)) - steps) % count


def own_slots(at):
    turned = at ^ ((at >> 1) & 1)
    slots = [at ^ 1]
    for steps in (8, 4):
        slots += [turned - steps, (turned ^ 2) - steps]
    return slots


def paired_slots(at):
    return [at, at ^ 2] + own_slots(at) + own_slots(at ^ 2)


def grouped_slots(n_inner, at):
    first = at - at % n_inner
    return [first - step * n_inner + j for step in range(REACH + 1) for j in range(n_inner)]


def attention_kernel(slots_of, window, heads, piece_blocks, out_blocks, docs, *refs):
    n_pieces, n_outs = len(piece_blocks), len(out_blocks)
    doc_ref, q_ref, do_ref = refs[:3]
    pieces = refs[3 : 3 + n_pieces]
    dq_ref = refs[3 + n_pieces]
    outs = refs[4 + n_pieces : 4 + n_pieces + n_outs]
    kw, vw, bias, t_buf, dp_buf, dk_acc, dv_acc = refs[4 + n_pieces + n_outs :]
    tokens, head_dim = q_ref.shape[0], kw.shape[1]
    n_inner = lax.axis_size("inner")
    me = lax.axis_index("outer") * n_inner + lax.axis_index("inner")
    slots = slots_of(me)
    scale = 1.0 / math.sqrt(head_dim)

    def rows_of(s):
        return pl.ds(pl.multiple_of(s * tokens, tokens), tokens)

    where = [(ref, i) for ref, n in zip(pieces, piece_blocks) for i in range(n)]
    for slot, (ref, i) in zip(slots, where):
        s = me - slot

        @pl.when((s >= 0) & (s <= window))
        def _():
            kw[rows_of(s), :] = ref[i * tokens : (i + 1) * tokens, :head_dim]
            vw[rows_of(s), :] = ref[i * tokens : (i + 1) * tokens, head_dim:]

    position = me * tokens + lax.broadcasted_iota(jnp.int32, (1, tokens), 1)
    start = jnp.zeros((1, tokens), jnp.int32)
    end = jnp.int32(0)
    for n in range(docs):
        end = end + doc_ref[n]
        start = jnp.where(position >= end, end, start)
    for s in range(window + 1):
        key_at = (me - s) * tokens + lax.broadcasted_iota(jnp.int32, (tokens, tokens), 0)
        seen = (key_at >= start) & (key_at <= position)
        bias[s * tokens : (s + 1) * tokens, :] = jnp.where(seen, 0.0, NEG)

    factor = scale * math.log2(math.e)
    blocks = window + 1

    def one_pair(pair, slot, first):
        def side(ref):
            cut = [
                ref[:, pl.ds(pl.multiple_of((2 * pair + i) * head_dim, head_dim), head_dim)]
                for i in range(2)
            ]
            return jnp.concatenate(cut, axis=0)

        qp, dop = side(q_ref), side(do_ref)
        width = 2 * tokens
        peak = jnp.full((8, width), NEG, jnp.float32)
        for b in range(blocks):
            span = slice(b * tokens, (b + 1) * tokens)
            scores = lax.dot_general(
                kw[span, :], qp, LANES_CONTRACT, preferred_element_type=jnp.float32
            )
            off = bias[span, :]
            t = scores * factor + jnp.concatenate([off, off], axis=1)
            t_buf[slot, span, :] = t
            peak = jnp.maximum(peak, jnp.max(t.reshape(tokens // 8, 8, width), axis=0))
        peak = jnp.max(peak, axis=0, keepdims=True)
        total = jnp.zeros((8, width), jnp.float32)
        moment = jnp.zeros((8, width), jnp.float32)
        for b in range(blocks):
            span = slice(b * tokens, (b + 1) * tokens)
            p = jnp.exp2(t_buf[slot, span, :] - peak)
            dp = lax.dot_general(
                vw[span, :], dop, LANES_CONTRACT, preferred_element_type=jnp.float32
            )
            t_buf[slot, span, :] = p
            dp_buf[slot, span, :] = dp
            total = total + jnp.sum(p.reshape(tokens // 8, 8, width), axis=0)
            moment = moment + jnp.sum((p * dp).reshape(tokens // 8, 8, width), axis=0)
        share = 1.0 / jnp.sum(total, axis=0, keepdims=True)
        delta = jnp.sum(moment, axis=0, keepdims=True) * share
        dq = jnp.zeros((width, head_dim), jnp.float32)
        for b in range(blocks):
            span = slice(b * tokens, (b + 1) * tokens)
            p = t_buf[slot, span, :] * share
            low = p.astype(jnp.bfloat16)
            ds = (p * (dp_buf[slot, span, :] - delta)).astype(jnp.bfloat16)
            dv = jnp.dot(low, dop, preferred_element_type=jnp.float32)
            dk = jnp.dot(ds, qp, preferred_element_type=jnp.float32)
            if first is True:
                dv_acc[span, :] = dv
                dk_acc[span, :] = dk
            else:
                dv_acc[span, :] += dv
                dk_acc[span, :] += dk
            dq = dq + lax.dot_general(
                ds, kw[span, :], ROWS_CONTRACT, preferred_element_type=jnp.float32
            )
        dq = (dq * scale).astype(jnp.bfloat16)
        for i in range(2):
            dq_ref[:, pl.ds(pl.multiple_of((2 * pair + i) * head_dim, head_dim), head_dim)] = dq[
                i * tokens : (i + 1) * tokens
            ]

    n_pairs = heads // 2
    if blocks <= 12:
        for pair in range(n_pairs):
            one_pair(pair, pair % 2, pair == 0)
    else:
        dk_acc[...] = jnp.zeros_like(dk_acc)
        dv_acc[...] = jnp.zeros_like(dv_acc)

        def step(pair, carry):
            one_pair(pair, 0, False)
            return carry

        lax.fori_loop(0, n_pairs, step, 0)

    places = [(ref, i) for ref, n in zip(outs, out_blocks) for i in range(n)]
    for slot, (ref, i) in zip(slots, places):
        s = me - slot
        mine = slice(i * tokens, (i + 1) * tokens)
        inside = (s >= 0) & (s <= window)

        @pl.when(inside)
        def _():
            ref[mine, :head_dim] = dk_acc[rows_of(s), :].astype(ref.dtype)
            ref[mine, head_dim:] = dv_acc[rows_of(s), :].astype(ref.dtype)

        @pl.when(jnp.logical_not(inside))
        def _():
            ref[mine, :] = jnp.zeros((tokens, 2 * head_dim), ref.dtype)


def attend(slots_of, window, queries, grad_out, doc_lengths, pieces, out_blocks, out_types):
    tokens, width = queries.shape
    head_dim = pieces[0].shape[1] // 2
    heads = width // head_dim
    keys = (window + 1) * tokens
    slots = 2 if window + 1 <= 12 else 1
    kernel = functools.partial(
        attention_kernel,
        slots_of,
        window,
        heads,
        [piece.shape[0] // tokens for piece in pieces],
        out_blocks,
        doc_lengths.shape[0],
    )
    whole = pl.BlockSpec(memory_space=pltpu.VMEM)
    return pl.pallas_call(
        kernel,
        out_shape=[jax.ShapeDtypeStruct((tokens, width), jnp.bfloat16)]
        + [
            jax.ShapeDtypeStruct((n * tokens, 2 * head_dim), kind)
            for n, kind in zip(out_blocks, out_types)
        ],
        in_specs=[pl.BlockSpec(memory_space=pltpu.SMEM)] + [whole] * (2 + len(pieces)),
        out_specs=[whole] * (1 + len(out_blocks)),
        scratch_shapes=[
            pltpu.VMEM((keys, head_dim), jnp.bfloat16),
            pltpu.VMEM((keys, head_dim), jnp.bfloat16),
            pltpu.VMEM((keys, tokens), jnp.float32),
            pltpu.VMEM((slots, keys, 2 * tokens), jnp.float32),
            pltpu.VMEM((slots, keys, 2 * tokens), jnp.float32),
            pltpu.VMEM((keys, head_dim), jnp.float32),
            pltpu.VMEM((keys, head_dim), jnp.float32),
        ],
        compiler_params=pltpu.CompilerParams(vmem_limit_bytes=56 * 2**20),
    )(doc_lengths, queries, grad_out, *pieces)


def finish(sums, head_dim):
    scale = 1.0 / math.sqrt(head_dim)
    grad_keys = (sums[:, :head_dim] * scale).astype(jnp.bfloat16)
    return grad_keys, sums[:, head_dim:].astype(jnp.bfloat16)


def paired(queries, keys, values, grad_out, doc_lengths):
    tokens, head_dim = keys.shape
    low, high = jnp.bfloat16, jnp.float32
    own = jnp.concatenate([keys, values], axis=1)
    partner = permuted(own, across_core)
    by_x = permuted(own, across_x)
    both = jnp.concatenate([own, partner], axis=0)
    by_8 = permuted(both, functools.partial(ahead, 8))
    by_4 = permuted(both, functools.partial(ahead, 4))
    fetched = permuted(jnp.concatenate([by_x, by_8, by_4], axis=0), across_core)
    grad_queries, mine, over, keep, give = attend(
        paired_slots,
        REACH * 2,
        queries,
        grad_out,
        doc_lengths,
        [own, partner, by_x, by_8, by_4, fetched],
        [1, 1, 5, 5],
        [high, low, high, low],
    )
    given = permuted(jnp.concatenate([over, give], axis=0), across_core)
    total = (keep + given[tokens:].astype(high)).astype(low)
    back_x = permuted(total[:tokens], across_x)
    back_8 = permuted(total[tokens : 3 * tokens], functools.partial(behind, 8))
    back_4 = permuted(total[3 * tokens :], functools.partial(behind, 4))
    far = back_8.astype(high) + back_4.astype(high)
    last = permuted(far[tokens:].astype(low), across_core)
    sums = (
        mine
        + given[:tokens].astype(high)
        + back_x.astype(high)
        + far[:tokens]
        + last.astype(high)
    )
    return (grad_queries,) + finish(sums, head_dim)


def grouped(queries, keys, values, grad_out, doc_lengths):
    tokens, head_dim = keys.shape
    n_inner, n_outer = lax.axis_size("inner"), lax.axis_size("outer")

    def turned(value, steps):
        return lax.ppermute(
            value, "outer", [(at, (at + steps) % n_outer) for at in range(n_outer)]
        )

    own = jnp.concatenate([keys, values], axis=1)
    group = lax.all_gather(own, "inner", axis=0, tiled=True)
    pieces = [group] + [turned(group, step) for step in range(1, REACH + 1)]
    results = attend(
        functools.partial(grouped_slots, n_inner),
        REACH * n_inner,
        queries,
        grad_out,
        doc_lengths,
        pieces,
        [n_inner] * (REACH + 1),
        [jnp.float32] * (REACH + 1),
    )
    sums = results[1]
    for step in range(1, REACH + 1):
        sums = sums + turned(results[1 + step], -step)
    sums = lax.psum_scatter(sums, "inner", scatter_dimension=0, tiled=True)
    return (results[0],) + finish(sums, head_dim)


def on_device(queries, keys, values, grad_out, doc_lengths):
    if lax.axis_size("inner") == 2 and lax.axis_size("outer") % 4 == 0:
        return paired(queries, keys, values, grad_out, doc_lengths)
    return grouped(queries, keys, values, grad_out, doc_lengths)


def solution(mesh):
    rows = P(("outer", "inner"), None)
    return jax.shard_map(
        on_device,
        mesh=mesh,
        in_specs=(rows, rows, rows, rows, P()),
        out_specs=(rows, rows, rows),
        check_vma=False,
    )
```

time: 213 us -> 40.2 us (0.19)
  the two profiles are of different devices: /device:TPU:27 before, /device:TPU:0 now
where the time goes in v1:
time: 40.2 us; the launch traced here: 39.4 us
  starting transfers between devices  13 us (32%)
  waiting for transfers between devices  12.9 us (32%)
  Pallas kernels  7.55 us (19%)
  local copies, waits for them, and re-layouts  3.42 us (9%)
  other arithmetic  1.86 us (5%)
  between operations  0.73 us (2%)
    ppermute x10, starting transfers between devices, permuted(): lax.ppermute(value, AXES, [(at, target(at, count)) for at in range(count)])  13 us
    ppermute x10, waiting for transfers between devices, permuted(): lax.ppermute(value, AXES, [(at, target(at, count)) for at in range(count)])  12.9 us
    pallas_call x1, Pallas kernels, attend(): pl.pallas_call(kernel, out_shape=[jax.ShapeDtypeStruct((tokens, width), j...  7.55 us
    unnamed x19, local copies, waits for them, and re-layouts  2.75 us
    concatenate x1, other arithmetic, paired(): given = permuted(jnp.concatenate([over, give], axis=0), across_core)  1.07 us
  transfers between devices with their start and end apart: 10, of which 10 were waited for; matrix products, arithmetic and copies ran while one was open for 0% of the time, Pallas kernels for 0%

profile of v1, /device:TPU:0, one launch (start us, length us, event | category | flops | bytes accessed | tf_op | source)
XLA Modules:
  0.0 39.4 jit_solution(6928036293703106943)
XLA Ops:
  0.6 0.0 copy-start.8
  0.6 0.8 %constant_dynamic-update-slice_fusion.1 = bf16[128,256]{1,0:T(8,128)(2,1)S(1)} fusion(bf16[128,128]{1,0:T(8,128)(2,1)} %param.6), kind=kLoop, calls=%fused_computation.12 | loop fusion | bytes 65536
  1.4 0.0 copy-done.8
  1.4 0.0 copy-start.3
  1.4 0.5 %collective-permute-start = (bf16[128,256]{1,0:T(8,128)(2,1)S(1)}, bf16[128,256]{1,0:T(8,128)(2,1)S(1)}, u32[]{:S(2)}, u32[]{:S(2)}) collective-permute-start(bf16[128,256]{1,0:T(8,128)(2,1)S(1)} %constant_dynamic-update-slice_fusion.refs_3_), channel_id=1, source_target_pairs={{0,2},{1,3},{2,0},{3,1},{4,6},{5,7},{6,4},{7,5},{8,10},{9,11},{10,... | collective-permute-start | bytes 196616 | tf_op jit(solution)/shard_map/ppermute | solution.py:20
  2.0 0.9 %collective-permute-done.refs_4_ = bf16[128,256]{1,0:T(8,128)(2,1)S(1)} collective-permute-done((bf16[128,256]{1,0:T(8,128)(2,1)S(1)}, bf16[128,256]{1,0:T(8,128)(2,1)S(1)}, u32[]{:S(2)}, u32[]{:S(2)}) %collective-permute-start) | collective-permute-done | bytes 65568 | tf_op jit(solution)/shard_map/ppermute | solution.py:20
  2.9 0.0 copy-start.6
  2.9 0.6 %copy-done.6 = bf16[128,256]{1,0:T(8,128)(2,1)} copy-done((bf16[128,256]{1,0:T(8,128)(2,1)}, bf16[128,256]{1,0:T(8,128)(2,1)S(1)}, u32[]{:S(2)}) %copy-start.6) | copy-done | bytes 65560
  3.5 2.9 %collective-permute-start.3 = (bf16[256,256]{1,0:T(8,128)(2,1)S(1)}, bf16[256,256]{1,0:T(8,128)(2,1)S(1)}, u32[]{:S(2)}, u32[]{:S(2)}) collective-permute-start(bf16[256,256]{1,0:T(8,128)(2,1)S(1)} %pad_maximum_fusion.2), channel_id=1, source_target_pairs={{0,4},{1,5},{2,7},{3,6},{4,8},{5,9},{6,11},{7,10},{8,12},{9,13},{1... | collective-permute-start | bytes 393224 | tf_op jit(solution)/shard_map/ppermute | solution.py:20
  6.4 1.6 %collective-permute-start.2 = (bf16[256,256]{1,0:T(8,128)(2,1)S(1)}, bf16[256,256]{1,0:T(8,128)(2,1)S(1)}, u32[]{:S(2)}, u32[]{:S(2)}) collective-permute-start(bf16[256,256]{1,0:T(8,128)(2,1)S(1)} %pad_maximum_fusion.2), channel_id=1, source_target_pairs={{0,8},{1,9},{2,11},{3,10},{4,12},{5,13},{6,15},{7,14},{8,16},{9,17... | collective-permute-start | bytes 393224 | tf_op jit(solution)/shard_map/ppermute | solution.py:20
  7.9 0.0 copy-done.3
  7.9 1.5 %collective-permute-start.1 = (bf16[128,256]{1,0:T(8,128)(2,1)S(1)}, bf16[128,256]{1,0:T(8,128)(2,1)S(1)}, u32[]{:S(2)}, u32[]{:S(2)}) collective-permute-start(bf16[128,256]{1,0:T(8,128)(2,1)S(1)} %constant_dynamic-update-slice_fusion.refs_3_), channel_id=1, source_target_pairs={{0,1},{1,0},{2,3},{3,2},{4,5},{5,4},{6,7},{7,6},{8,9},{9,8},{10,11... | collective-permute-start | bytes 196616 | tf_op jit(solution)/shard_map/ppermute | solution.py:20
  9.4 3.0 %collective-permute-done.1.refs_5_ = bf16[128,256]{1,0:T(8,128)(2,1)S(1)} collective-permute-done((bf16[128,256]{1,0:T(8,128)(2,1)S(1)}, bf16[128,256]{1,0:T(8,128)(2,1)S(1)}, u32[]{:S(2)}, u32[]{:S(2)}) %collective-permute-start.1) | collective-permute-done | bytes 65568 | tf_op jit(solution)/shard_map/ppermute | solution.py:20
  12.4 0.0 copy-start.5
  12.4 1.4 %collective-permute-done.3.refs_7_ = bf16[256,256]{1,0:T(8,128)(2,1)S(1)} collective-permute-done((bf16[256,256]{1,0:T(8,128)(2,1)S(1)}, bf16[256,256]{1,0:T(8,128)(2,1)S(1)}, u32[]{:S(2)}, u32[]{:S(2)}) %collective-permute-start.3) | collective-permute-done | bytes 131104 | tf_op jit(solution)/shard_map/ppermute | solution.py:20
  13.8 0.0 copy-start.1
  13.8 0.6 %collective-permute-done.2.refs_6_ = bf16[256,256]{1,0:T(8,128)(2,1)S(1)} collective-permute-done((bf16[256,256]{1,0:T(8,128)(2,1)S(1)}, bf16[256,256]{1,0:T(8,128)(2,1)S(1)}, u32[]{:S(2)}, u32[]{:S(2)}) %collective-permute-start.2) | collective-permute-done | bytes 131104 | tf_op jit(solution)/shard_map/ppermute | solution.py:20
  14.4 0.0 copy-start.2
  14.5 0.0 copy-done.5
  14.5 0.0 copy-done.1
  14.5 0.6 %copy-done.2 = bf16[256,256]{1,0:T(8,128)(2,1)} copy-done((bf16[256,256]{1,0:T(8,128)(2,1)}, bf16[256,256]{1,0:T(8,128)(2,1)S(1)}, u32[]{:S(2)}) %copy-start.2) | copy-done | bytes 131096
  15.1 0.5 %collective-permute-start.4 = (bf16[640,256]{1,0:T(8,128)(2,1)S(1)}, bf16[640,256]{1,0:T(8,128)(2,1)S(1)}, u32[]{:S(2)}, u32[]{:S(2)}) collective-permute-start(bf16[640,256]{1,0:T(8,128)(2,1)S(1)} %pad_maximum_fusion.1), channel_id=1, source_target_pairs={{0,2},{1,3},{2,0},{3,1},{4,6},{5,7},{6,4},{7,5},{8,10},{9,11},{10,... | collective-permute-start | bytes 983048 | tf_op jit(solution)/shard_map/ppermute | solution.py:20
  15.5 1.3 %collective-permute-done.4.refs_8_ = bf16[640,256]{1,0:T(8,128)(2,1)S(1)} collective-permute-done((bf16[640,256]{1,0:T(8,128)(2,1)S(1)}, bf16[640,256]{1,0:T(8,128)(2,1)S(1)}, u32[]{:S(2)}, u32[]{:S(2)}) %collective-permute-start.4) | collective-permute-done | bytes 327712 | tf_op jit(solution)/shard_map/ppermute | solution.py:20
  16.8 0.0 copy-start.4
  16.8 0.7 %copy-done.4 = bf16[640,256]{1,0:T(8,128)(2,1)} copy-done((bf16[640,256]{1,0:T(8,128)(2,1)}, bf16[640,256]{1,0:T(8,128)(2,1)S(1)}, u32[]{:S(2)}) %copy-start.4) | copy-done | bytes 327704
  17.5 7.6 %shard_map.76 = (bf16[128,1024]{1,0:T(8,128)(2,1)}, f32[128,256]{1,0:T(8,128)}, bf16[128,256]{1,0:T(8,128)(2,1)}, f32[640,256]{1,0:T(8,128)}, bf16[640,256]{1,0:T(8,128)(2,1)}) custom-call(s32[16]{0:T(128)} %refs_0_.1, bf16[128,1024]{1,0:T(8,128)(2,1)} %refs_1_.1, bf16[128,1024]{1,0:T(8,128)(2,1)} %refs_2_.1, bf16[128,256]{1,0:T(8,128)(2,1)} %copy-done.3, ...), custom_call_target="tpu_custom_call" | custom-call | tf_op jit(solution)/shard_map/pallas_call | solution.py:199
  25.1 0.0 copy-start
  25.1 1.1 %pad_maximum_fusion = bf16[768,256]{1,0:T(8,128)(2,1)S(1)} fusion(bf16[640,256]{1,0:T(8,128)(2,1)} %get-tuple-element.11, bf16[128,256]{1,0:T(8,128)(2,1)} %get-tuple-element.10), kind=kLoop, calls=%fused_computation.1 | loop fusion | flops 786432 | bytes 786432 | tf_op jit(solution)/shard_map/concatenate | solution.py:247
  26.2 0.4 %collective-permute-start.5 = (bf16[768,256]{1,0:T(8,128)(2,1)S(1)}, bf16[768,256]{1,0:T(8,128)(2,1)S(1)}, u32[]{:S(2)}, u32[]{:S(2)}) collective-permute-start(bf16[768,256]{1,0:T(8,128)(2,1)S(1)} %pad_maximum_fusion), channel_id=1, source_target_pairs={{0,2},{1,3},{2,0},{3,1},{4,6},{5,7},{6,4},{7,5},{8,10},{9,11},{10,... | collective-permute-start | bytes 1179656 | tf_op jit(solution)/shard_map/ppermute | solution.py:20
  26.6 1.3 %collective-permute-done.5 = bf16[768,256]{1,0:T(8,128)(2,1)S(1)} collective-permute-done((bf16[768,256]{1,0:T(8,128)(2,1)S(1)}, bf16[768,256]{1,0:T(8,128)(2,1)S(1)}, u32[]{:S(2)}, u32[]{:S(2)}) %collective-permute-start.5) | collective-permute-done | bytes 393248 | tf_op jit(solution)/shard_map/ppermute | solution.py:20
  28.0 0.0 copy-done
  28.0 0.1 add_convert_fusion
  28.1 1.9 %collective-permute-start.7 = (bf16[256,256]{1,0:T(8,128)(2,1)S(1)}, bf16[256,256]{1,0:T(8,128)(2,1)S(1)}, u32[]{:S(2)}, u32[]{:S(2)}) collective-permute-start(bf16[256,256]{1,0:T(8,128)(2,1)S(1)} %get-tuple-element.13), channel_id=1, source_target_pairs={{0,24},{1,25},{2,27},{3,26},{4,28},{5,29},{6,31},{7,30},{8,0},{9,1... | collective-permute-start | bytes 393224 | tf_op jit(solution)/shard_map/ppermute | solution.py:20
  29.9 2.5 %collective-permute-start.8 = (bf16[256,256]{1,0:T(8,128)(2,1)S(1)}, bf16[256,256]{1,0:T(8,128)(2,1)S(1)}, u32[]{:S(2)}, u32[]{:S(2)}) collective-permute-start(bf16[256,256]{1,0:T(8,128)(2,1)S(1)} %get-tuple-element.14), channel_id=1, source_target_pairs={{0,28},{1,29},{2,31},{3,30},{4,0},{5,1},{6,3},{7,2},{8,4},{9,5},{1... | collective-permute-start | bytes 393224 | tf_op jit(solution)/shard_map/ppermute | solution.py:20
  32.5 1.0 %collective-permute-start.6 = (bf16[128,256]{1,0:T(8,128)(2,1)S(1)}, bf16[128,256]{1,0:T(8,128)(2,1)S(1)}, u32[]{:S(2)}, u32[]{:S(2)}) collective-permute-start(bf16[128,256]{1,0:T(8,128)(2,1)S(1)} %slice.40), channel_id=1, source_target_pairs={{0,1},{1,0},{2,3},{3,2},{4,5},{5,4},{6,7},{7,6},{8,9},{9,8},{10,11... | collective-permute-start | bytes 196616 | tf_op jit(solution)/shard_map/ppermute | solution.py:20
  33.5 0.9 %collective-permute-done.7 = bf16[256,256]{1,0:T(8,128)(2,1)S(1)} collective-permute-done((bf16[256,256]{1,0:T(8,128)(2,1)S(1)}, bf16[256,256]{1,0:T(8,128)(2,1)S(1)}, u32[]{:S(2)}, u32[]{:S(2)}) %collective-permute-start.7) | collective-permute-done | bytes 131104 | tf_op jit(solution)/shard_map/ppermute | solution.py:20
  34.4 2.4 %collective-permute-done.8 = bf16[256,256]{1,0:T(8,128)(2,1)S(1)} collective-permute-done((bf16[256,256]{1,0:T(8,128)(2,1)S(1)}, bf16[256,256]{1,0:T(8,128)(2,1)S(1)}, u32[]{:S(2)}, u32[]{:S(2)}) %collective-permute-start.8) | collective-permute-done | bytes 131104 | tf_op jit(solution)/shard_map/ppermute | solution.py:20
  36.8 0.0 copy-start.7
  36.8 0.2 collective-permute-start.9
  37.0 0.8 %collective-permute-done.6 = bf16[128,256]{1,0:T(8,128)(2,1)S(1)} collective-permute-done((bf16[128,256]{1,0:T(8,128)(2,1)S(1)}, bf16[128,256]{1,0:T(8,128)(2,1)S(1)}, u32[]{:S(2)}, u32[]{:S(2)}) %collective-permute-start.6) | collective-permute-done | bytes 65568 | tf_op jit(solution)/shard_map/ppermute | solution.py:20
  37.8 0.3 collective-permute-done.9
  38.1 0.0 copy-done.7
  38.2 0.6 %slice.58 = bf16[128,128]{1,0:T(8,128)(2,1)} slice(f32[128,256]{1,0:T(8,128)S(1)} %fusion), slice={[0:128], [128:256]} | slice | bytes 65536 | tf_op jit(solution)/shard_map/slice | solution.py:224
  38.8 0.6 %fusion.1 = bf16[128,128]{1,0:T(8,128)(2,1)} fusion(f32[128,256]{1,0:T(8,128)S(1)} %fusion), kind=kLoop, calls=%fused_computation.10 | loop fusion | flops 32768 | bytes 98304 | tf_op jit(solution)/shard_map/convert_element_type | solution.py:223
  (8 shorter events, 0.1 us)
Async XLA Ops:
  0.6 0.8 %copy-start.8 = (bf16[128,128]{1,0:T(8,128)(2,1)S(1)}, bf16[128,128]{1,0:T(8,128)(2,1)}, u32[]{:S(2)}) copy-start(bf16[128,128]{1,0:T(8,128)(2,1)} %param.7) | copy-start | bytes 98308
  1.4 6.5 %copy-start.3 = (bf16[128,256]{1,0:T(8,128)(2,1)}, bf16[128,256]{1,0:T(8,128)(2,1)S(1)}, u32[]{:S(2)}) copy-start(bf16[128,256]{1,0:T(8,128)(2,1)S(1)} %constant_dynamic-update-slice_fusion.refs_3_) | copy-start | bytes 196612
  1.4 1.4 %collective-permute-start = (bf16[128,256]{1,0:T(8,128)(2,1)S(1)}, bf16[128,256]{1,0:T(8,128)(2,1)S(1)}, u32[]{:S(2)}, u32[]{:S(2)}) collective-permute-start(bf16[128,256]{1,0:T(8,128)(2,1)S(1)} %constant_dynamic-update-slice_fusion.refs_3_), channel_id=1, source_target_pairs={{0,2},{1,3},{2,0},{3,1},{4,6},{5,7},{6,4},{7,5},{8,10},{9,11},{10,... | collective-permute-start | bytes 196616 | tf_op jit(solution)/shard_map/ppermute | solution.py:20
  2.9 0.6 %copy-start.6 = (bf16[128,256]{1,0:T(8,128)(2,1)}, bf16[128,256]{1,0:T(8,128)(2,1)S(1)}, u32[]{:S(2)}) copy-start(bf16[128,256]{1,0:T(8,128)(2,1)S(1)} %collective-permute-done.refs_4_) | copy-start | bytes 196612
  3.5 10.3 %collective-permute-start.3 = (bf16[256,256]{1,0:T(8,128)(2,1)S(1)}, bf16[256,256]{1,0:T(8,128)(2,1)S(1)}, u32[]{:S(2)}, u32[]{:S(2)}) collective-permute-start(bf16[256,256]{1,0:T(8,128)(2,1)S(1)} %pad_maximum_fusion.2), channel_id=1, source_target_pairs={{0,4},{1,5},{2,7},{3,6},{4,8},{5,9},{6,11},{7,10},{8,12},{9,13},{1... | collective-permute-start | bytes 393224 | tf_op jit(solution)/shard_map/ppermute | solution.py:20
  6.4 8.1 %collective-permute-start.2 = (bf16[256,256]{1,0:T(8,128)(2,1)S(1)}, bf16[256,256]{1,0:T(8,128)(2,1)S(1)}, u32[]{:S(2)}, u32[]{:S(2)}) collective-permute-start(bf16[256,256]{1,0:T(8,128)(2,1)S(1)} %pad_maximum_fusion.2), channel_id=1, source_target_pairs={{0,8},{1,9},{2,11},{3,10},{4,12},{5,13},{6,15},{7,14},{8,16},{9,17... | collective-permute-start | bytes 393224 | tf_op jit(solution)/shard_map/ppermute | solution.py:20
  7.9 4.5 %collective-permute-start.1 = (bf16[128,256]{1,0:T(8,128)(2,1)S(1)}, bf16[128,256]{1,0:T(8,128)(2,1)S(1)}, u32[]{:S(2)}, u32[]{:S(2)}) collective-permute-start(bf16[128,256]{1,0:T(8,128)(2,1)S(1)} %constant_dynamic-update-slice_fusion.refs_3_), channel_id=1, source_target_pairs={{0,1},{1,0},{2,3},{3,2},{4,5},{5,4},{6,7},{7,6},{8,9},{9,8},{10,11... | collective-permute-start | bytes 196616 | tf_op jit(solution)/shard_map/ppermute | solution.py:20
  12.4 2.0 %copy-start.5 = (bf16[128,256]{1,0:T(8,128)(2,1)}, bf16[128,256]{1,0:T(8,128)(2,1)S(1)}, u32[]{:S(2)}) copy-start(bf16[128,256]{1,0:T(8,128)(2,1)S(1)} %collective-permute-done.1.refs_5_) | copy-start | bytes 196612
  13.8 0.7 %copy-start.1 = (bf16[256,256]{1,0:T(8,128)(2,1)}, bf16[256,256]{1,0:T(8,128)(2,1)S(1)}, u32[]{:S(2)}) copy-start(bf16[256,256]{1,0:T(8,128)(2,1)S(1)} %collective-permute-done.3.refs_7_) | copy-start | bytes 393220
  14.4 0.7 %copy-start.2 = (bf16[256,256]{1,0:T(8,128)(2,1)}, bf16[256,256]{1,0:T(8,128)(2,1)S(1)}, u32[]{:S(2)}) copy-start(bf16[256,256]{1,0:T(8,128)(2,1)S(1)} %collective-permute-done.2.refs_6_) | copy-start | bytes 393220
  15.1 1.7 %collective-permute-start.4 = (bf16[640,256]{1,0:T(8,128)(2,1)S(1)}, bf16[640,256]{1,0:T(8,128)(2,1)S(1)}, u32[]{:S(2)}, u32[]{:S(2)}) collective-permute-start(bf16[640,256]{1,0:T(8,128)(2,1)S(1)} %pad_maximum_fusion.1), channel_id=1, source_target_pairs={{0,2},{1,3},{2,0},{3,1},{4,6},{5,7},{6,4},{7,5},{8,10},{9,11},{10,... | collective-permute-start | bytes 983048 | tf_op jit(solution)/shard_map/ppermute | solution.py:20
  16.8 0.7 %copy-start.4 = (bf16[640,256]{1,0:T(8,128)(2,1)}, bf16[640,256]{1,0:T(8,128)(2,1)S(1)}, u32[]{:S(2)}) copy-start(bf16[640,256]{1,0:T(8,128)(2,1)S(1)} %collective-permute-done.4.refs_8_) | copy-start | bytes 983044
  25.1 2.9 %copy-start = (f32[640,256]{1,0:T(8,128)S(1)}, f32[640,256]{1,0:T(8,128)}, u32[]{:S(2)}) copy-start(f32[640,256]{1,0:T(8,128)} %get-tuple-element.12) | copy-start | bytes 1966084
  26.2 1.8 %collective-permute-start.5 = (bf16[768,256]{1,0:T(8,128)(2,1)S(1)}, bf16[768,256]{1,0:T(8,128)(2,1)S(1)}, u32[]{:S(2)}, u32[]{:S(2)}) collective-permute-start(bf16[768,256]{1,0:T(8,128)(2,1)S(1)} %pad_maximum_fusion), channel_id=1, source_target_pairs={{0,2},{1,3},{2,0},{3,1},{4,6},{5,7},{6,4},{7,5},{8,10},{9,11},{10,... | collective-permute-start | bytes 1179656 | tf_op jit(solution)/shard_map/ppermute | solution.py:20
  28.1 6.3 %collective-permute-start.7 = (bf16[256,256]{1,0:T(8,128)(2,1)S(1)}, bf16[256,256]{1,0:T(8,128)(2,1)S(1)}, u32[]{:S(2)}, u32[]{:S(2)}) collective-permute-start(bf16[256,256]{1,0:T(8,128)(2,1)S(1)} %get-tuple-element.13), channel_id=1, source_target_pairs={{0,24},{1,25},{2,27},{3,26},{4,28},{5,29},{6,31},{7,30},{8,0},{9,1... | collective-permute-start | bytes 393224 | tf_op jit(solution)/shard_map/ppermute | solution.py:20
  29.9 6.8 %collective-permute-start.8 = (bf16[256,256]{1,0:T(8,128)(2,1)S(1)}, bf16[256,256]{1,0:T(8,128)(2,1)S(1)}, u32[]{:S(2)}, u32[]{:S(2)}) collective-permute-start(bf16[256,256]{1,0:T(8,128)(2,1)S(1)} %get-tuple-element.14), channel_id=1, source_target_pairs={{0,28},{1,29},{2,31},{3,30},{4,0},{5,1},{6,3},{7,2},{8,4},{9,5},{1... | collective-permute-start | bytes 393224 | tf_op jit(solution)/shard_map/ppermute | solution.py:20
  32.5 5.4 %collective-permute-start.6 = (bf16[128,256]{1,0:T(8,128)(2,1)S(1)}, bf16[128,256]{1,0:T(8,128)(2,1)S(1)}, u32[]{:S(2)}, u32[]{:S(2)}) collective-permute-start(bf16[128,256]{1,0:T(8,128)(2,1)S(1)} %slice.40), channel_id=1, source_target_pairs={{0,1},{1,0},{2,3},{3,2},{4,5},{5,4},{6,7},{7,6},{8,9},{9,8},{10,11... | collective-permute-start | bytes 196616 | tf_op jit(solution)/shard_map/ppermute | solution.py:20
  36.8 1.4 %copy-start.7 = (f32[128,256]{1,0:T(8,128)S(1)}, f32[128,256]{1,0:T(8,128)}, u32[]{:S(2)}) copy-start(f32[128,256]{1,0:T(8,128)} %get-tuple-element.9) | copy-start | bytes 393220
  36.8 1.3 %collective-permute-start.9 = (bf16[128,256]{1,0:T(8,128)(2,1)S(1)}, bf16[128,256]{1,0:T(8,128)(2,1)S(1)}, u32[]{:S(2)}, u32[]{:S(2)}) collective-permute-start(bf16[128,256]{1,0:T(8,128)(2,1)S(1)} %slice.57), channel_id=1, source_target_pairs={{0,2},{1,3},{2,0},{3,1},{4,6},{5,7},{6,4},{7,5},{8,10},{9,11},{10,... | collective-permute-start | bytes 196616 | tf_op jit(solution)/shard_map/ppermute | solution.py:20

commit v2 on v1

--- a/solution.py
+++ b/solution.py
@@ -48,12 +48,16 @@
     return [at, at ^ 2] + own_slots(at) + own_slots(at ^ 2)
 
 
+def paired_given(at):
+    return [at] + own_slots(at) + [at ^ 2] + own_slots(at ^ 2)
+
+
 def grouped_slots(n_inner, at):
     first = at - at % n_inner
     return [first - step * n_inner + j for step in range(REACH + 1) for j in range(n_inner)]
 
 
-def attention_kernel(slots_of, window, heads, piece_blocks, out_blocks, docs, *refs):
+def attention_kernel(slots_of, given_of, window, heads, piece_blocks, out_blocks, docs, *refs):
     n_pieces, n_outs = len(piece_blocks), len(out_blocks)
     doc_ref, q_ref, do_ref = refs[:3]
     pieces = refs[3 : 3 + n_pieces]
@@ -75,8 +79,8 @@
 
         @pl.when((s >= 0) & (s <= window))
         def _():
-            kw[rows_of(s), :] = ref[i * tokens : (i + 1) * tokens, :head_dim]
-            vw[rows_of(s), :] = ref[i * tokens : (i + 1) * tokens, head_dim:]
+            kw[rows_of(s), :] = ref[2 * i * tokens : (2 * i + 1) * tokens, :]
+            vw[rows_of(s), :] = ref[(2 * i + 1) * tokens : (2 * i + 2) * tokens, :]
 
     position = me * tokens + lax.broadcasted_iota(jnp.int32, (1, tokens), 1)
     start = jnp.zeros((1, tokens), jnp.int32)
@@ -165,33 +169,35 @@
         lax.fori_loop(0, n_pairs, step, 0)
 
     places = [(ref, i) for ref, n in zip(outs, out_blocks) for i in range(n)]
-    for slot, (ref, i) in zip(slots, places):
+    for slot, (ref, i) in zip(given_of(me), places):
         s = me - slot
-        mine = slice(i * tokens, (i + 1) * tokens)
+        first, second = (slice((2 * i + j) * tokens, (2 * i + j + 1) * tokens) for j in range(2))
         inside = (s >= 0) & (s <= window)
 
         @pl.when(inside)
         def _():
-            ref[mine, :head_dim] = dk_acc[rows_of(s), :].astype(ref.dtype)
-            ref[mine, head_dim:] = dv_acc[rows_of(s), :].astype(ref.dtype)
+            ref[first, :] = dk_acc[rows_of(s), :].astype(ref.dtype)
+            ref[second, :] = dv_acc[rows_of(s), :].astype(ref.dtype)
 
         @pl.when(jnp.logical_not(inside))
         def _():
-            ref[mine, :] = jnp.zeros((tokens, 2 * head_dim), ref.dtype)
-
-
-def attend(slots_of, window, queries, grad_out, doc_lengths, pieces, out_blocks, out_types):
+            ref[first, :] = jnp.zeros((tokens, head_dim), ref.dtype)
+            ref[second, :] = jnp.zeros((tokens, head_dim), ref.dtype)
+
+
+def attend(slots_of, given_of, window, queries, grad_out, doc_lengths, pieces, out_blocks, out_types):
     tokens, width = queries.shape
-    head_dim = pieces[0].shape[1] // 2
+    head_dim = pieces[0].shape[1]
     heads = width // head_dim
     keys = (window + 1) * tokens
     slots = 2 if window + 1 <= 12 else 1
     kernel = functools.partial(
         attention_kernel,
         slots_of,
+        given_of,
         window,
         heads,
-        [piece.shape[0] // tokens for piece in pieces],
+        [piece.shape[0] // (2 * tokens) for piece in pieces],
         out_blocks,
         doc_lengths.shape[0],
     )
@@ -200,7 +206,7 @@
         kernel,
         out_shape=[jax.ShapeDtypeStruct((tokens, width), jnp.bfloat16)]
         + [
-            jax.ShapeDtypeStruct((n * tokens, 2 * head_dim), kind)
+            jax.ShapeDtypeStruct((2 * n * tokens, head_dim), kind)
             for n, kind in zip(out_blocks, out_types)
         ],
         in_specs=[pl.BlockSpec(memory_space=pltpu.SMEM)] + [whole] * (2 + len(pieces)),
@@ -214,48 +220,51 @@
             pltpu.VMEM((keys, head_dim), jnp.float32),
             pltpu.VMEM((keys, head_dim), jnp.float32),
         ],
-        compiler_params=pltpu.CompilerParams(vmem_limit_bytes=56 * 2**20),
+        compiler_params=pltpu.CompilerParams(vmem_limit_bytes=(16 if window <= 12 else 56) * 2**20),
     )(doc_lengths, queries, grad_out, *pieces)
 
 
 def finish(sums, head_dim):
     scale = 1.0 / math.sqrt(head_dim)
-    grad_keys = (sums[:, :head_dim] * scale).astype(jnp.bfloat16)
-    return grad_keys, sums[:, head_dim:].astype(jnp.bfloat16)
+    half = sums.shape[0] // 2
+    grad_keys = (sums[:half] * scale).astype(jnp.bfloat16)
+    return grad_keys, sums[half:].astype(jnp.bfloat16)
 
 
 def paired(queries, keys, values, grad_out, doc_lengths):
     tokens, head_dim = keys.shape
     low, high = jnp.bfloat16, jnp.float32
-    own = jnp.concatenate([keys, values], axis=1)
+    block = 2 * tokens
+    own = jnp.concatenate([keys, values], axis=0)
     partner = permuted(own, across_core)
     by_x = permuted(own, across_x)
     both = jnp.concatenate([own, partner], axis=0)
+    by_4 = permuted(both, functools.partial(ahead, 4))
     by_8 = permuted(both, functools.partial(ahead, 8))
-    by_4 = permuted(both, functools.partial(ahead, 4))
     fetched = permuted(jnp.concatenate([by_x, by_8, by_4], axis=0), across_core)
-    grad_queries, mine, over, keep, give = attend(
+    grad_queries, mine, keep, give = attend(
         paired_slots,
+        paired_given,
         REACH * 2,
         queries,
         grad_out,
         doc_lengths,
         [own, partner, by_x, by_8, by_4, fetched],
-        [1, 1, 5, 5],
-        [high, low, high, low],
-    )
-    given = permuted(jnp.concatenate([over, give], axis=0), across_core)
-    total = (keep + given[tokens:].astype(high)).astype(low)
-    back_x = permuted(total[:tokens], across_x)
-    back_8 = permuted(total[tokens : 3 * tokens], functools.partial(behind, 8))
-    back_4 = permuted(total[3 * tokens :], functools.partial(behind, 4))
+        [1, 5, 6],
+        [high, high, low],
+    )
+    given = permuted(give, across_core)
+    total = (keep + given[block:].astype(high)).astype(low)
+    back_4 = permuted(total[3 * block :], functools.partial(behind, 4))
+    back_8 = permuted(total[block : 3 * block], functools.partial(behind, 8))
+    back_x = permuted(total[:block], across_x)
     far = back_8.astype(high) + back_4.astype(high)
-    last = permuted(far[tokens:].astype(low), across_core)
+    last = permuted(far[block:].astype(low), across_core)
     sums = (
         mine
-        + given[:tokens].astype(high)
+        + given[:block].astype(high)
         + back_x.astype(high)
-        + far[:tokens]
+        + far[:block]
         + last.astype(high)
     )
     return (grad_queries,) + finish(sums, head_dim)
@@ -270,10 +279,11 @@
             value, "outer", [(at, (at + steps) % n_outer) for at in range(n_outer)]
         )
 
-    own = jnp.concatenate([keys, values], axis=1)
+    own = jnp.concatenate([keys, values], axis=0)
     group = lax.all_gather(own, "inner", axis=0, tiled=True)
     pieces = [group] + [turned(group, step) for step in range(1, REACH + 1)]
     results = attend(
+        functools.partial(grouped_slots, n_inner),
         functools.partial(grouped_slots, n_inner),
         REACH * n_inner,
         queries,

time: 40.2 us -> 36 us (0.90)
  local copies, waits for them, and re-layouts: 3.42 us -> 1.48 us
  Pallas kernels: 7.55 us -> 6.35 us
  other arithmetic: 1.86 us -> 0.8 us
    unnamed x19 -> x10, local copies, waits for them, and re-layouts: 2.75 us -> 0.81 us
    pallas_call x1, Pallas kernels: 7.55 us -> 6.35 us  [attend(): pl.pallas_call(kernel, out_shape=[jax.ShapeDtypeStruct((tokens, width), j...]
    concatenate x2 -> x0, other arithmetic: 1.08 us -> none  [the longest x1 1.07 us: paired(): given = permuted(jnp.concatenate([over, give], axis=0), across_core)]
where the time goes in v2:
time: 36 us; the launch traced here: 35.4 us
  waiting for transfers between devices  13.1 us (36%)
  starting transfers between devices  12.9 us (36%)
  Pallas kernels  6.35 us (18%)
  local copies, waits for them, and re-layouts  1.48 us (4%)
  other arithmetic  0.8 us (2%)
  between operations  0.73 us (2%)
    ppermute x10, waiting for transfers between devices, permuted(): lax.ppermute(value, AXES, [(at, target(at, count)) for at in range(count)])  13.1 us
    ppermute x10, starting transfers between devices, permuted(): lax.ppermute(value, AXES, [(at, target(at, count)) for at in range(count)])  12.9 us
    pallas_call x1, Pallas kernels, attend(): pl.pallas_call(kernel, out_shape=[jax.ShapeDtypeStruct((tokens, width), j...  6.35 us
    unnamed x10, local copies, waits for them, and re-layouts  0.81 us
  transfers between devices with their start and end apart: 10, of which 10 were waited for; matrix products, arithmetic and copies ran while one was open for 0% of the time, Pallas kernels for 0%

profile of v2, /device:TPU:0, one launch (start us, length us, event | category | flops | bytes accessed | tf_op | source)
XLA Modules:
  0.0 35.4 jit_solution(3857151954623919276)
XLA Ops:
  0.6 0.0 copy-start.3
  0.6 0.8 %constant_dynamic-update-slice_fusion.4 = (bf16[512,128]{1,0:T(8,128)(2,1)S(1)}, bf16[256,128]{1,0:T(8,128)(2,1)S(1)}) fusion(bf16[128,128]{1,0:T(8,128)(2,1)} %param.6), kind=kLoop, calls=%fused_computation.13 | loop fusion | bytes 98304
  1.4 0.0 copy-done.3
  1.4 0.5 %collective-permute-start = (bf16[256,128]{1,0:T(8,128)(2,1)S(1)}, bf16[256,128]{1,0:T(8,128)(2,1)S(1)}, u32[]{:S(2)}, u32[]{:S(2)}) collective-permute-start(bf16[256,128]{1,0:T(8,128)(2,1)S(1)} %get-tuple-element.14.refs_3_), channel_id=1, source_target_pairs={{0,2},{1,3},{2,0},{3,1},{4,6},{5,7},{6,4},{7,5},{8,10},{9,11},{10,... | collective-permute-start | bytes 196616 | tf_op jit(solution)/shard_map/ppermute | solution.py:20
  2.0 0.9 %collective-permute-done.refs_4_ = bf16[256,128]{1,0:T(8,128)(2,1)S(1)} collective-permute-done((bf16[256,128]{1,0:T(8,128)(2,1)S(1)}, bf16[256,128]{1,0:T(8,128)(2,1)S(1)}, u32[]{:S(2)}, u32[]{:S(2)}) %collective-permute-start) | collective-permute-done | bytes 65568 | tf_op jit(solution)/shard_map/ppermute | solution.py:20
  2.9 0.0 copy-start
  2.9 0.0 copy-start.1
  2.9 0.0 copy-start.2
  2.9 2.9 %collective-permute-start.3 = (bf16[512,128]{1,0:T(8,128)(2,1)S(1)}, bf16[512,128]{1,0:T(8,128)(2,1)S(1)}, u32[]{:S(2)}, u32[]{:S(2)}) collective-permute-start(bf16[512,128]{1,0:T(8,128)(2,1)S(1)} %constant_dynamic-update-slice_fusion.2), channel_id=1, source_target_pairs={{0,4},{1,5},{2,7},{3,6},{4,8},{5,9},{6,11},{7,10},{8,12},{9,13},{1... | collective-permute-start | bytes 393224 | tf_op jit(solution)/shard_map/ppermute | solution.py:20
  5.8 1.6 %collective-permute-start.2 = (bf16[512,128]{1,0:T(8,128)(2,1)S(1)}, bf16[512,128]{1,0:T(8,128)(2,1)S(1)}, u32[]{:S(2)}, u32[]{:S(2)}) collective-permute-start(bf16[512,128]{1,0:T(8,128)(2,1)S(1)} %constant_dynamic-update-slice_fusion.2), channel_id=1, source_target_pairs={{0,8},{1,9},{2,11},{3,10},{4,12},{5,13},{6,15},{7,14},{8,16},{9,17... | collective-permute-start | bytes 393224 | tf_op jit(solution)/shard_map/ppermute | solution.py:20
  7.4 1.5 %collective-permute-start.1 = (bf16[256,128]{1,0:T(8,128)(2,1)S(1)}, bf16[256,128]{1,0:T(8,128)(2,1)S(1)}, u32[]{:S(2)}, u32[]{:S(2)}) collective-permute-start(bf16[256,128]{1,0:T(8,128)(2,1)S(1)} %get-tuple-element.14.refs_3_), channel_id=1, source_target_pairs={{0,1},{1,0},{2,3},{3,2},{4,5},{5,4},{6,7},{7,6},{8,9},{9,8},{10,11... | collective-permute-start | bytes 196616 | tf_op jit(solution)/shard_map/ppermute | solution.py:20
  8.9 3.0 %collective-permute-done.1.refs_5_ = bf16[256,128]{1,0:T(8,128)(2,1)S(1)} collective-permute-done((bf16[256,128]{1,0:T(8,128)(2,1)S(1)}, bf16[256,128]{1,0:T(8,128)(2,1)S(1)}, u32[]{:S(2)}, u32[]{:S(2)}) %collective-permute-start.1) | collective-permute-done | bytes 65568 | tf_op jit(solution)/shard_map/ppermute | solution.py:20
  11.9 1.4 %collective-permute-done.3.refs_7_ = bf16[512,128]{1,0:T(8,128)(2,1)S(1)} collective-permute-done((bf16[512,128]{1,0:T(8,128)(2,1)S(1)}, bf16[512,128]{1,0:T(8,128)(2,1)S(1)}, u32[]{:S(2)}, u32[]{:S(2)}) %collective-permute-start.3) | collective-permute-done | bytes 131104 | tf_op jit(solution)/shard_map/ppermute | solution.py:20
  13.3 0.6 %collective-permute-done.2.refs_6_ = bf16[512,128]{1,0:T(8,128)(2,1)S(1)} collective-permute-done((bf16[512,128]{1,0:T(8,128)(2,1)S(1)}, bf16[512,128]{1,0:T(8,128)(2,1)S(1)}, u32[]{:S(2)}, u32[]{:S(2)}) %collective-permute-start.2) | collective-permute-done | bytes 131104 | tf_op jit(solution)/shard_map/ppermute | solution.py:20
  13.9 0.5 %collective-permute-start.4 = (bf16[1280,128]{1,0:T(8,128)(2,1)S(1)}, bf16[1280,128]{1,0:T(8,128)(2,1)S(1)}, u32[]{:S(2)}, u32[]{:S(2)}) collective-permute-start(bf16[1280,128]{1,0:T(8,128)(2,1)S(1)} %pad_maximum_fusion), channel_id=1, source_target_pairs={{0,2},{1,3},{2,0},{3,1},{4,6},{5,7},{6,4},{7,5},{8,10},{9,11},{10,... | collective-permute-start | bytes 983048 | tf_op jit(solution)/shard_map/ppermute | solution.py:20
  14.5 1.3 %collective-permute-done.4.refs_8_ = bf16[1280,128]{1,0:T(8,128)(2,1)S(1)} collective-permute-done((bf16[1280,128]{1,0:T(8,128)(2,1)S(1)}, bf16[1280,128]{1,0:T(8,128)(2,1)S(1)}, u32[]{:S(2)}, u32[]{:S(2)}) %collective-permute-start.4) | collective-permute-done | bytes 327712 | tf_op jit(solution)/shard_map/ppermute | solution.py:20
  15.7 0.0 copy-done
  15.7 0.0 copy-done.1
  15.7 0.0 copy-done.2
  15.7 6.3 %shard_map.76 = (bf16[128,1024]{1,0:T(8,128)(2,1)}, f32[256,128]{1,0:T(8,128)S(1)}, f32[1280,128]{1,0:T(8,128)S(1)}, bf16[1536,128]{1,0:T(8,128)(2,1)S(1)}) custom-call(s32[16]{0:T(128)S(1)} %copy-done.2, bf16[128,1024]{1,0:T(8,128)(2,1)S(1)} %copy-done, bf16[128,1024]{1,0:T(8,128)(2,1)S(1)} %copy-done.1, bf16[256,128]{1,0:T(8,128)(2,1)S(1)} %get-tuple-element.14.refs_3_, ...), custom_call_target="tpu_custom_call" | custom-call | tf_op jit(solution)/shard_map/pallas_call | solution.py:205
  22.1 0.4 %collective-permute-start.5 = (bf16[1536,128]{1,0:T(8,128)(2,1)S(1)}, bf16[1536,128]{1,0:T(8,128)(2,1)S(1)}, u32[]{:S(2)}, u32[]{:S(2)}) collective-permute-start(bf16[1536,128]{1,0:T(8,128)(2,1)S(1)} %get-tuple-element.9), channel_id=1, source_target_pairs={{0,2},{1,3},{2,0},{3,1},{4,6},{5,7},{6,4},{7,5},{8,10},{9,11},{10,... | collective-permute-start | bytes 1179656 | tf_op jit(solution)/shard_map/ppermute | solution.py:20
  22.5 1.3 %collective-permute-done.5 = bf16[1536,128]{1,0:T(8,128)(2,1)S(1)} collective-permute-done((bf16[1536,128]{1,0:T(8,128)(2,1)S(1)}, bf16[1536,128]{1,0:T(8,128)(2,1)S(1)}, u32[]{:S(2)}, u32[]{:S(2)}) %collective-permute-start.5) | collective-permute-done | bytes 393248 | tf_op jit(solution)/shard_map/ppermute | solution.py:20
  23.8 0.1 add_convert_fusion
  23.9 1.9 %collective-permute-start.7 = (bf16[512,128]{1,0:T(8,128)(2,1)S(1)}, bf16[512,128]{1,0:T(8,128)(2,1)S(1)}, u32[]{:S(2)}, u32[]{:S(2)}) collective-permute-start(bf16[512,128]{1,0:T(8,128)(2,1)S(1)} %get-tuple-element.11), channel_id=1, source_target_pairs={{0,24},{1,25},{2,27},{3,26},{4,28},{5,29},{6,31},{7,30},{8,0},{9,1... | collective-permute-start | bytes 393224 | tf_op jit(solution)/shard_map/ppermute | solution.py:20
  25.8 2.5 %collective-permute-start.8 = (bf16[512,128]{1,0:T(8,128)(2,1)S(1)}, bf16[512,128]{1,0:T(8,128)(2,1)S(1)}, u32[]{:S(2)}, u32[]{:S(2)}) collective-permute-start(bf16[512,128]{1,0:T(8,128)(2,1)S(1)} %get-tuple-element.12), channel_id=1, source_target_pairs={{0,28},{1,29},{2,31},{3,30},{4,0},{5,1},{6,3},{7,2},{8,4},{9,5},{1... | collective-permute-start | bytes 393224 | tf_op jit(solution)/shard_map/ppermute | solution.py:20
  28.3 1.0 %collective-permute-start.6 = (bf16[256,128]{1,0:T(8,128)(2,1)S(1)}, bf16[256,128]{1,0:T(8,128)(2,1)S(1)}, u32[]{:S(2)}, u32[]{:S(2)}) collective-permute-start(bf16[256,128]{1,0:T(8,128)(2,1)S(1)} %slice.40), channel_id=1, source_target_pairs={{0,1},{1,0},{2,3},{3,2},{4,5},{5,4},{6,7},{7,6},{8,9},{9,8},{10,11... | collective-permute-start | bytes 196616 | tf_op jit(solution)/shard_map/ppermute | solution.py:20
  29.3 0.9 %collective-permute-done.7 = bf16[512,128]{1,0:T(8,128)(2,1)S(1)} collective-permute-done((bf16[512,128]{1,0:T(8,128)(2,1)S(1)}, bf16[512,128]{1,0:T(8,128)(2,1)S(1)}, u32[]{:S(2)}, u32[]{:S(2)}) %collective-permute-start.7) | collective-permute-done | bytes 131104 | tf_op jit(solution)/shard_map/ppermute | solution.py:20
  30.3 2.4 %collective-permute-done.8 = bf16[512,128]{1,0:T(8,128)(2,1)S(1)} collective-permute-done((bf16[512,128]{1,0:T(8,128)(2,1)S(1)}, bf16[512,128]{1,0:T(8,128)(2,1)S(1)}, u32[]{:S(2)}, u32[]{:S(2)}) %collective-permute-start.8) | collective-permute-done | bytes 131104 | tf_op jit(solution)/shard_map/ppermute | solution.py:20
  32.7 0.1 collective-permute-start.9
  32.8 0.9 %collective-permute-done.6 = bf16[256,128]{1,0:T(8,128)(2,1)S(1)} collective-permute-done((bf16[256,128]{1,0:T(8,128)(2,1)S(1)}, bf16[256,128]{1,0:T(8,128)(2,1)S(1)}, u32[]{:S(2)}, u32[]{:S(2)}) %collective-permute-start.6) | collective-permute-done | bytes 65568 | tf_op jit(solution)/shard_map/ppermute | solution.py:20
  33.7 0.4 %collective-permute-done.9 = bf16[256,128]{1,0:T(8,128)(2,1)S(1)} collective-permute-done((bf16[256,128]{1,0:T(8,128)(2,1)S(1)}, bf16[256,128]{1,0:T(8,128)(2,1)S(1)}, u32[]{:S(2)}, u32[]{:S(2)}) %collective-permute-start.9) | collective-permute-done | bytes 65568 | tf_op jit(solution)/shard_map/ppermute | solution.py:20
  34.1 0.6 %slice.58 = bf16[128,128]{1,0:T(8,128)(2,1)} slice(f32[256,128]{1,0:T(8,128)S(1)} %fusion), slice={[128:256], [0:128]} | slice | bytes 65536 | tf_op jit(solution)/shard_map/slice | solution.py:231
  34.7 0.6 %fusion.1 = bf16[128,128]{1,0:T(8,128)(2,1)} fusion(f32[256,128]{1,0:T(8,128)S(1)} %fusion), kind=kLoop, calls=%fused_computation.8 | loop fusion | flops 32768 | bytes 98304 | tf_op jit(solution)/shard_map/convert_element_type | solution.py:230
  (8 shorter events, 0.2 us)
Async XLA Ops:
  0.6 0.8 %copy-start.3 = (bf16[128,128]{1,0:T(8,128)(2,1)S(1)}, bf16[128,128]{1,0:T(8,128)(2,1)}, u32[]{:S(2)}) copy-start(bf16[128,128]{1,0:T(8,128)(2,1)} %param.7) | copy-start | bytes 98308
  1.4 1.4 %collective-permute-start = (bf16[256,128]{1,0:T(8,128)(2,1)S(1)}, bf16[256,128]{1,0:T(8,128)(2,1)S(1)}, u32[]{:S(2)}, u32[]{:S(2)}) collective-permute-start(bf16[256,128]{1,0:T(8,128)(2,1)S(1)} %get-tuple-element.14.refs_3_), channel_id=1, source_target_pairs={{0,2},{1,3},{2,0},{3,1},{4,6},{5,7},{6,4},{7,5},{8,10},{9,11},{10,... | collective-permute-start | bytes 196616 | tf_op jit(solution)/shard_map/ppermute | solution.py:20
  2.9 12.8 %copy-start = (bf16[128,1024]{1,0:T(8,128)(2,1)S(1)}, bf16[128,1024]{1,0:T(8,128)(2,1)}, u32[]{:S(2)}) copy-start(bf16[128,1024]{1,0:T(8,128)(2,1)} %refs_1_.1) | copy-start | bytes 786436
  2.9 12.8 %copy-start.1 = (bf16[128,1024]{1,0:T(8,128)(2,1)S(1)}, bf16[128,1024]{1,0:T(8,128)(2,1)}, u32[]{:S(2)}) copy-start(bf16[128,1024]{1,0:T(8,128)(2,1)} %refs_2_.1) | copy-start | bytes 786436
  2.9 12.8 %copy-start.2 = (s32[16]{0:T(128)S(1)}, s32[16]{0:T(128)}, u32[]{:S(2)}) copy-start(s32[16]{0:T(128)} %refs_0_.1) | copy-start | bytes 196
  2.9 10.4 %collective-permute-start.3 = (bf16[512,128]{1,0:T(8,128)(2,1)S(1)}, bf16[512,128]{1,0:T(8,128)(2,1)S(1)}, u32[]{:S(2)}, u32[]{:S(2)}) collective-permute-start(bf16[512,128]{1,0:T(8,128)(2,1)S(1)} %constant_dynamic-update-slice_fusion.2), channel_id=1, source_target_pairs={{0,4},{1,5},{2,7},{3,6},{4,8},{5,9},{6,11},{7,10},{8,12},{9,13},{1... | collective-permute-start | bytes 393224 | tf_op jit(solution)/shard_map/ppermute | solution.py:20
  5.8 8.1 %collective-permute-start.2 = (bf16[512,128]{1,0:T(8,128)(2,1)S(1)}, bf16[512,128]{1,0:T(8,128)(2,1)S(1)}, u32[]{:S(2)}, u32[]{:S(2)}) collective-permute-start(bf16[512,128]{1,0:T(8,128)(2,1)S(1)} %constant_dynamic-update-slice_fusion.2), channel_id=1, source_target_pairs={{0,8},{1,9},{2,11},{3,10},{4,12},{5,13},{6,15},{7,14},{8,16},{9,17... | collective-permute-start | bytes 393224 | tf_op jit(solution)/shard_map/ppermute | solution.py:20
  7.4 4.5 %collective-permute-start.1 = (bf16[256,128]{1,0:T(8,128)(2,1)S(1)}, bf16[256,128]{1,0:T(8,128)(2,1)S(1)}, u32[]{:S(2)}, u32[]{:S(2)}) collective-permute-start(bf16[256,128]{1,0:T(8,128)(2,1)S(1)} %get-tuple-element.14.refs_3_), channel_id=1, source_target_pairs={{0,1},{1,0},{2,3},{3,2},{4,5},{5,4},{6,7},{7,6},{8,9},{9,8},{10,11... | collective-permute-start | bytes 196616 | tf_op jit(solution)/shard_map/ppermute | solution.py:20
  13.9 1.8 %collective-permute-start.4 = (bf16[1280,128]{1,0:T(8,128)(2,1)S(1)}, bf16[1280,128]{1,0:T(8,128)(2,1)S(1)}, u32[]{:S(2)}, u32[]{:S(2)}) collective-permute-start(bf16[1280,128]{1,0:T(8,128)(2,1)S(1)} %pad_maximum_fusion), channel_id=1, source_target_pairs={{0,2},{1,3},{2,0},{3,1},{4,6},{5,7},{6,4},{7,5},{8,10},{9,11},{10,... | collective-permute-start | bytes 983048 | tf_op jit(solution)/shard_map/ppermute | solution.py:20
  22.1 1.7 %collective-permute-start.5 = (bf16[1536,128]{1,0:T(8,128)(2,1)S(1)}, bf16[1536,128]{1,0:T(8,128)(2,1)S(1)}, u32[]{:S(2)}, u32[]{:S(2)}) collective-permute-start(bf16[1536,128]{1,0:T(8,128)(2,1)S(1)} %get-tuple-element.9), channel_id=1, source_target_pairs={{0,2},{1,3},{2,0},{3,1},{4,6},{5,7},{6,4},{7,5},{8,10},{9,11},{10,... | collective-permute-start | bytes 1179656 | tf_op jit(solution)/shard_map/ppermute | solution.py:20
  23.9 6.3 %collective-permute-start.7 = (bf16[512,128]{1,0:T(8,128)(2,1)S(1)}, bf16[512,128]{1,0:T(8,128)(2,1)S(1)}, u32[]{:S(2)}, u32[]{:S(2)}) collective-permute-start(bf16[512,128]{1,0:T(8,128)(2,1)S(1)} %get-tuple-element.11), channel_id=1, source_target_pairs={{0,24},{1,25},{2,27},{3,26},{4,28},{5,29},{6,31},{7,30},{8,0},{9,1... | collective-permute-start | bytes 393224 | tf_op jit(solution)/shard_map/ppermute | solution.py:20
  25.8 6.9 %collective-permute-start.8 = (bf16[512,128]{1,0:T(8,128)(2,1)S(1)}, bf16[512,128]{1,0:T(8,128)(2,1)S(1)}, u32[]{:S(2)}, u32[]{:S(2)}) collective-permute-start(bf16[512,128]{1,0:T(8,128)(2,1)S(1)} %get-tuple-element.12), channel_id=1, source_target_pairs={{0,28},{1,29},{2,31},{3,30},{4,0},{5,1},{6,3},{7,2},{8,4},{9,5},{1... | collective-permute-start | bytes 393224 | tf_op jit(solution)/shard_map/ppermute | solution.py:20
  28.3 5.4 %collective-permute-start.6 = (bf16[256,128]{1,0:T(8,128)(2,1)S(1)}, bf16[256,128]{1,0:T(8,128)(2,1)S(1)}, u32[]{:S(2)}, u32[]{:S(2)}) collective-permute-start(bf16[256,128]{1,0:T(8,128)(2,1)S(1)} %slice.40), channel_id=1, source_target_pairs={{0,1},{1,0},{2,3},{3,2},{4,5},{5,4},{6,7},{7,6},{8,9},{9,8},{10,11... | collective-permute-start | bytes 196616 | tf_op jit(solution)/shard_map/ppermute | solution.py:20
  32.7 1.3 %collective-permute-start.9 = (bf16[256,128]{1,0:T(8,128)(2,1)S(1)}, bf16[256,128]{1,0:T(8,128)(2,1)S(1)}, u32[]{:S(2)}, u32[]{:S(2)}) collective-permute-start(bf16[256,128]{1,0:T(8,128)(2,1)S(1)} %slice.57), channel_id=1, source_target_pairs={{0,2},{1,3},{2,0},{3,1},{4,6},{5,7},{6,4},{7,5},{8,10},{9,11},{10,... | collective-permute-start | bytes 196616 | tf_op jit(solution)/shard_map/ppermute | solution.py:20

commit v3 on v2

--- a/solution.py
+++ b/solution.py
@@ -42,14 +42,6 @@
     for steps in (8, 4):
         slots += [turned - steps, (turned ^ 2) - steps]
     return slots
-
-
-def paired_slots(at):
-    return [at, at ^ 2] + own_slots(at) + own_slots(at ^ 2)
-
-
-def paired_given(at):
-    return [at] + own_slots(at) + [at ^ 2] + own_slots(at ^ 2)
 
 
 def grouped_slots(n_inner, at):
@@ -231,43 +223,341 @@
     return grad_keys, sums[half:].astype(jnp.bfloat16)
 
 
+def head_rows(ref, rows):
+    tokens = ref.shape[0]
+    head_dim = rows.shape[1]
+    for h in range(rows.shape[0] // tokens):
+        rows[h * tokens : (h + 1) * tokens, :] = ref[:, h * head_dim : (h + 1) * head_dim]
+
+
+def own_position():
+    return lax.axis_index("outer") * lax.axis_size("inner") + lax.axis_index("inner")
+
+
+def document_starts(doc_ref, docs, position):
+    start = jnp.zeros(position.shape, jnp.int32)
+    end = jnp.int32(0)
+    for n in range(docs):
+        end = end + doc_ref[n]
+        start = jnp.where(position >= end, end, start)
+    return start
+
+
+def score_blocks(ids, blocks, start, me, q_rows, do_rows, bias, p_ref, dp_ref):
+    rows, head_dim = q_rows.shape
+    tokens = bias.shape[1]
+    factor = math.log2(math.e) / math.sqrt(head_dim)
+    position = me * tokens + lax.broadcasted_iota(jnp.int32, (1, tokens), 1)
+    spans = [slice(b * tokens, (b + 1) * tokens) for b in range(len(blocks))]
+    for span, at in zip(spans, ids):
+        key_at = at * tokens + lax.broadcasted_iota(jnp.int32, (tokens, tokens), 0)
+        seen = (key_at >= start) & (key_at <= position)
+        bias[span, :] = jnp.where(seen, 0.0, NEG)
+    width = 2 * tokens
+    stats = []
+    for pair in range(rows // width):
+        cols = slice(pair * width, (pair + 1) * width)
+        qp, dop = q_rows[cols, :], do_rows[cols, :]
+        peak = jnp.full((8, width), NEG, jnp.float32)
+        for span, (keys, values) in zip(spans, blocks):
+            scores = lax.dot_general(
+                keys(), qp, LANES_CONTRACT, preferred_element_type=jnp.float32
+            )
+            off = bias[span, :]
+            t = scores * factor + jnp.concatenate([off, off], axis=1)
+            p_ref[span, cols] = t
+            peak = jnp.maximum(peak, jnp.max(t.reshape(tokens // 8, 8, width), axis=0))
+        peak = jnp.max(peak, axis=0, keepdims=True)
+        total = jnp.zeros((8, width), jnp.float32)
+        moment = jnp.zeros((8, width), jnp.float32)
+        for span, (keys, values) in zip(spans, blocks):
+            p = jnp.exp2(p_ref[span, cols] - peak)
+            dp = lax.dot_general(
+                values(), dop, LANES_CONTRACT, preferred_element_type=jnp.float32
+            )
+            p_ref[span, cols] = p
+            dp_ref[span, cols] = dp
+            total = total + jnp.sum(p.reshape(tokens // 8, 8, width), axis=0)
+            moment = moment + jnp.sum((p * dp).reshape(tokens // 8, 8, width), axis=0)
+        stats.append(
+            (
+                peak,
+                jnp.sum(total, axis=0, keepdims=True),
+                jnp.sum(moment, axis=0, keepdims=True),
+            )
+        )
+    return [jnp.concatenate(parts, axis=1) for parts in zip(*stats)]
+
+
+def grad_block(p_ref, dp_ref, span, share, delta, q_rows, do_rows, ds_ref, ds_span):
+    p = p_ref[span, :] * share
+    low = p.astype(jnp.bfloat16)
+    ds = (p * (dp_ref[span, :] - delta)).astype(jnp.bfloat16)
+    ds_ref[ds_span, :] = ds
+    dk = jnp.dot(ds, q_rows[...], preferred_element_type=jnp.float32)
+    dv = jnp.dot(low, do_rows[...], preferred_element_type=jnp.float32)
+    return dk, dv
+
+
+def block_of(ref, i, tokens):
+    return (
+        lambda: ref[2 * i * tokens : (2 * i + 1) * tokens, :],
+        lambda: ref[(2 * i + 1) * tokens : (2 * i + 2) * tokens, :],
+    )
+
+
+def put_block(ref, i, dk, dv):
+    tokens = dk.shape[0]
+    ref[2 * i * tokens : (2 * i + 1) * tokens, :] = dk.astype(ref.dtype)
+    ref[(2 * i + 1) * tokens : (2 * i + 2) * tokens, :] = dv.astype(ref.dtype)
+
+
+def pack_kernel(keys, values, own, sems):
+    tokens = keys.shape[0]
+    copies = [
+        pltpu.make_async_copy(ref, own.at[pl.ds(i * tokens, tokens), :], sems.at[i])
+        for i, ref in enumerate((keys, values))
+    ]
+    for copy in copies:
+        copy.start()
+    for copy in copies:
+        copy.wait()
+
+
+def near_kernel(
+    docs, doc_hbm, q_hbm, do_hbm, own, partner,
+    p_out, dp_out, stats, q_rows, do_rows, starts,
+    bias, doc_ref, sems,
+):
+    me = own_position()
+    tokens = q_hbm.shape[0]
+    rows, head_dim = q_rows.shape
+    heads = rows // tokens
+    copies = [pltpu.make_async_copy(doc_hbm, doc_ref, sems.at[2 * heads])]
+    for i, (source, stacked) in enumerate(((q_hbm, q_rows), (do_hbm, do_rows))):
+        for h in range(heads):
+            copies.append(
+                pltpu.make_async_copy(
+                    source.at[:, pl.ds(h * head_dim, head_dim)],
+                    stacked.at[pl.ds(h * tokens, tokens), :],
+                    sems.at[i * heads + h],
+                )
+            )
+    for copy in copies:
+        copy.start()
+    for copy in copies:
+        copy.wait()
+    position = me * tokens + lax.broadcasted_iota(jnp.int32, (1, tokens), 1)
+    start = document_starts(doc_ref, docs, position)
+    starts[0:1, :] = start
+    peak, total, moment = score_blocks(
+        [me, me ^ 2],
+        [block_of(own, 0, tokens), block_of(partner, 0, tokens)],
+        start, me, q_rows, do_rows, bias, p_out, dp_out,
+    )
+    stats[0:1, :], stats[1:2, :], stats[2:3, :] = peak, total, moment
+
+
+def direct_kernel(q_rows, do_rows, starts, by_x, by_8, by_4, p_out, dp_out, stats, bias):
+    me = own_position()
+    tokens = starts.shape[1]
+    peak, total, moment = score_blocks(
+        own_slots(me),
+        [block_of(by_x, 0, tokens)] + [block_of(ref, i, tokens) for ref in (by_8, by_4) for i in range(2)],
+        starts[0:1, :], me, q_rows, do_rows, bias, p_out, dp_out,
+    )
+    stats[0:1, :], stats[1:2, :], stats[2:3, :] = peak, total, moment
+
+
+def fetched_ids(me):
+    slots = own_slots(me ^ 2)
+    return [jnp.where((me >> 1) & 1 == 0, slots[1], slots[0])] + slots[2:]
+
+
+def fetched_kernel(
+    q_rows, do_rows, starts, fetched, p_near, dp_near, stats_near, stats_direct,
+    give, ds_out, shares, bias, p_buf, dp_buf,
+):
+    me = own_position()
+    tokens = starts.shape[1]
+    ids = fetched_ids(me)
+    peak, total, moment = score_blocks(
+        ids,
+        [block_of(fetched, i, tokens) for i in range(4)],
+        starts[0:1, :], me, q_rows, do_rows, bias, p_buf, dp_buf,
+    )
+    parts = [(ref[0:1, :], ref[1:2, :], ref[2:3, :]) for ref in (stats_near, stats_direct)]
+    parts.append((peak, total, moment))
+    top = jnp.maximum(jnp.maximum(parts[0][0], parts[1][0]), peak)
+    factors = [jnp.exp2(part[0] - top) for part in parts]
+    one = 1.0 / sum(f * part[1] for f, part in zip(factors, parts))
+    delta = sum(f * part[2] for f, part in zip(factors, parts)) * one
+    shared = [f * one for f in factors]
+    shares[0:1, :], shares[1:2, :], shares[2:3, :] = shared[0], shared[1], delta
+    for i in range(4):
+        span = slice(i * tokens, (i + 1) * tokens)
+        put_block(give, 1 + i, *grad_block(p_buf, dp_buf, span, shared[2], delta, q_rows, do_rows, ds_out, span))
+    put_block(
+        give, 0,
+        *grad_block(
+            p_near, dp_near, slice(tokens, 2 * tokens), shared[0], delta, q_rows, do_rows,
+            ds_out, slice(4 * tokens, 5 * tokens),
+        ),
+    )
+
+
+def keep_kernel(q_rows, do_rows, p_ref, dp_ref, shares, keep, ds_out):
+    tokens = p_ref.shape[0] // 5
+    share, delta = shares[1:2, :], shares[2:3, :]
+    for i in range(5):
+        span = slice(i * tokens, (i + 1) * tokens)
+        put_block(keep, i, *grad_block(p_ref, dp_ref, span, share, delta, q_rows, do_rows, ds_out, span))
+
+
+def query_kernel(
+    q_rows, do_rows, p_ref, dp_ref, shares, ds_fetched, ds_direct, fetched, partner, by_x, by_8, by_4, own,
+    dq_ref, mine, ds_own,
+):
+    tokens = dq_ref.shape[0]
+    head_dim = own.shape[1]
+    scale = 1.0 / math.sqrt(head_dim)
+    span = slice(0, tokens)
+    put_block(
+        mine, 0, *grad_block(p_ref, dp_ref, span, shares[0:1, :], shares[2:3, :], q_rows, do_rows, ds_own, span)
+    )
+    where = [(ds_fetched, i, block_of(fetched, i, tokens)) for i in range(4)]
+    where.append((ds_fetched, 4, block_of(partner, 0, tokens)))
+    direct = [(by_x, 0)] + [(ref, i) for ref in (by_8, by_4) for i in range(2)]
+    where += [(ds_direct, n, block_of(ref, i, tokens)) for n, (ref, i) in enumerate(direct)]
+    where.append((ds_own, 0, block_of(own, 0, tokens)))
+    width = 2 * tokens
+    for pair in range(q_rows.shape[0] // width):
+        cols = slice(pair * width, (pair + 1) * width)
+        dq = jnp.zeros((width, head_dim), jnp.float32)
+        for ref, n, (keys, values) in where:
+            dq = dq + lax.dot_general(
+                ref[n * tokens : (n + 1) * tokens, cols], keys(), ROWS_CONTRACT,
+                preferred_element_type=jnp.float32,
+            )
+        dq = (dq * scale).astype(jnp.bfloat16)
+        for i in range(2):
+            h = 2 * pair + i
+            dq_ref[:, h * head_dim : (h + 1) * head_dim] = dq[i * tokens : (i + 1) * tokens]
+
+
+def result_kernel(mine, given, back_x, far, last, dk_ref, dv_ref):
+    tokens, head_dim = dk_ref.shape
+    high = jnp.float32
+    for half, (ref, scale) in enumerate(((dk_ref, 1.0 / math.sqrt(head_dim)), (dv_ref, 1.0))):
+        span = slice(half * tokens, (half + 1) * tokens)
+        sums = mine[span, :] + given[span, :].astype(high) + back_x[span, :].astype(high)
+        sums = sums + far[span, :] + last[span, :].astype(high)
+        ref[...] = (sums * scale).astype(ref.dtype)
+
+
+def local_call(kernel, outs, scratch, args, blocks, far=0):
+    whole = pl.BlockSpec(memory_space=pltpu.VMEM)
+    specs = [pl.BlockSpec(memory_space=pltpu.HBM)] * far + [whole] * (len(args) - far)
+    return pl.pallas_call(
+        kernel,
+        out_shape=[jax.ShapeDtypeStruct(shape, kind) for shape, kind in outs],
+        in_specs=specs,
+        out_specs=[whole] * len(outs),
+        scratch_shapes=[
+            pltpu.VMEM(*entry) if isinstance(entry, tuple) else entry for entry in scratch
+        ],
+        compiler_params=pltpu.CompilerParams(vmem_limit_bytes=16 * 2**20),
+        cost_estimate=pl.CostEstimate(
+            flops=blocks * 2 * 128 * 128 * 1024, bytes_accessed=blocks * 2**19, transcendentals=0
+        ),
+    )(*[pltpu.with_memory_space_constraint(arg, pltpu.HBM) for arg in args[:far]], *args[far:])
+
+
 def paired(queries, keys, values, grad_out, doc_lengths):
     tokens, head_dim = keys.shape
     low, high = jnp.bfloat16, jnp.float32
     block = 2 * tokens
-    own = jnp.concatenate([keys, values], axis=0)
+    rows = queries.shape[1] // head_dim * tokens
+    docs = doc_lengths.shape[0]
+    second = (own_position() >> 1) & 1
+
+    def part(n):
+        return [((n * tokens, rows), high)] * 2 + [((8, rows), high)], [((n * tokens, tokens), high)]
+
+    (own,) = local_call(
+        pack_kernel, [((block, head_dim), low)], [pltpu.SemaphoreType.DMA((2,))], [keys, values], 0, far=2
+    )
     partner = permuted(own, across_core)
     by_x = permuted(own, across_x)
     both = jnp.concatenate([own, partner], axis=0)
     by_4 = permuted(both, functools.partial(ahead, 4))
     by_8 = permuted(both, functools.partial(ahead, 8))
-    fetched = permuted(jnp.concatenate([by_x, by_8, by_4], axis=0), across_core)
-    grad_queries, mine, keep, give = attend(
-        paired_slots,
-        paired_given,
-        REACH * 2,
-        queries,
-        grad_out,
-        doc_lengths,
-        [own, partner, by_x, by_8, by_4, fetched],
-        [1, 5, 6],
-        [high, high, low],
+    outs, scratch = part(2)
+    p_near, dp_near, stats_near, q_rows, do_rows, starts = local_call(
+        functools.partial(near_kernel, docs),
+        outs + [((rows, head_dim), low)] * 2 + [((8, tokens), jnp.int32)],
+        scratch
+        + [
+            pltpu.SMEM(doc_lengths.shape, jnp.int32),
+            pltpu.SemaphoreType.DMA((2 * (rows // tokens) + 1,)),
+        ],
+        [doc_lengths, queries, grad_out, own, partner],
+        4,
+        far=3,
+    )
+    by_x, by_8, by_4, stats_near = lax.optimization_barrier((by_x, by_8, by_4, stats_near))
+    offered = jnp.where(second == 0, by_x, by_8[:block])
+    fetched = permuted(jnp.concatenate([offered, by_8[block:], by_4], axis=0), across_core)
+    p_direct, dp_direct, stats_direct = local_call(
+        direct_kernel, *part(5), [q_rows, do_rows, starts, by_x, by_8, by_4], 10
+    )
+    give, ds_fetched, shares = local_call(
+        fetched_kernel,
+        [((5 * block, head_dim), low), ((5 * tokens, rows), low), ((8, rows), high)],
+        part(4)[1] + [((4 * tokens, rows), high)] * 2,
+        [q_rows, do_rows, starts, fetched, p_near, dp_near, stats_near, stats_direct],
+        18,
     )
     given = permuted(give, across_core)
-    total = (keep + given[block:].astype(high)).astype(low)
-    back_4 = permuted(total[3 * block :], functools.partial(behind, 4))
-    back_8 = permuted(total[block : 3 * block], functools.partial(behind, 8))
-    back_x = permuted(total[:block], across_x)
+    keep, ds_direct = local_call(
+        keep_kernel,
+        [((5 * block, head_dim), high), ((5 * tokens, rows), low)],
+        [],
+        [q_rows, do_rows, p_direct, dp_direct, shares],
+        10,
+    )
+    back = given.astype(high)
+    swapped = back[block : 2 * block]
+    total_x = (keep[:block] + jnp.where(second == 0, swapped, 0.0)).astype(low)
+    total_8 = jnp.concatenate(
+        [
+            keep[block : 2 * block] + jnp.where(second == 0, 0.0, swapped),
+            keep[2 * block : 3 * block] + back[2 * block : 3 * block],
+        ],
+        axis=0,
+    ).astype(low)
+    total_4 = (keep[3 * block :] + back[3 * block :]).astype(low)
+    back_4 = permuted(total_4, functools.partial(behind, 4))
+    back_8 = permuted(total_8, functools.partial(behind, 8))
+    back_x = permuted(total_x, across_x)
+    grad_queries, mine = local_call(
+        query_kernel,
+        [(queries.shape, low), ((block, head_dim), high)],
+        [((tokens, rows), low)],
+        [q_rows, do_rows, p_near, dp_near, shares, ds_fetched, ds_direct, fetched, partner, by_x, by_8, by_4, own],
+        13,
+    )
+    back_8, back_4, back_x, mine = lax.optimization_barrier((back_8, back_4, back_x, mine))
     far = back_8.astype(high) + back_4.astype(high)
     last = permuted(far[block:].astype(low), across_core)
-    sums = (
-        mine
-        + given[:block].astype(high)
-        + back_x.astype(high)
-        + far[:block]
-        + last.astype(high)
-    )
-    return (grad_queries,) + finish(sums, head_dim)
+    grad_keys, grad_values = local_call(
+        result_kernel,
+        [((tokens, head_dim), low)] * 2,
+        [],
+        [mine, given[:block], back_x, far, last],
+        0,
+    )
+    return grad_queries, grad_keys, grad_values
 
 
 def grouped(queries, keys, values, grad_out, doc_lengths):

time: 36 us -> 32.1 us (0.89); the launches traced: 35.4 us -> 31.8 us
  waiting for transfers between devices: 13.1 us -> 8.62 us
  Pallas kernels: 6.35 us -> 9.45 us
  local copies, waits for them, and re-layouts: 1.48 us -> 0.02 us
  other arithmetic: 0.8 us -> 0.21 us
    ppermute x10, waiting for transfers between devices: 13.1 us -> 8.62 us  [permuted(): lax.ppermute(value, AXES, [(at, target(at, count)) for at in range(count)])]
    pallas_call x1 -> x7, Pallas kernels: 6.35 us -> 9.45 us  [local_call(): pl.pallas_call(kernel, out_shape=[jax.ShapeDtypeStruct(shape, kind) for s...]
    unnamed x10 -> x0, local copies, waits for them, and re-layouts: 0.81 us -> none
    slice x3 -> x1, local copies, waits for them, and re-layouts: 0.64 us -> 0.01 us  [paired(): given[:block]]
    convert_element_type x2 -> x3, other arithmetic: 0.71 us -> 0.13 us  [the longest x1 0.05 us: paired(): total_x = (keep[:block] + jnp.where(second == 0, swapped, 0.0)).astype(low)]
  transfers between devices with their start and end apart: 10 -> 10, of which waited for: 10 -> 7; matrix products, arithmetic and copies ran while one was open for 0% -> 0% of each run, Pallas kernels for 0% -> 18%
where the time goes in v3:
time: 32.1 us; the launch traced here: 31.8 us
  starting transfers between devices  12.8 us (40%)
  Pallas kernels  9.45 us (29%)
  waiting for transfers between devices  8.62 us (27%)
  between operations  0.74 us (2%)
    ppermute x10, starting transfers between devices, permuted(): lax.ppermute(value, AXES, [(at, target(at, count)) for at in range(count)])  12.8 us
    pallas_call x7, Pallas kernels, local_call(): pl.pallas_call(kernel, out_shape=[jax.ShapeDtypeStruct(shape, kind) for s...  9.45 us
    ppermute x10, waiting for transfers between devices, permuted(): lax.ppermute(value, AXES, [(at, target(at, count)) for at in range(count)])  8.62 us
  transfers between devices with their start and end apart: 10, of which 7 were waited for; matrix products, arithmetic and copies ran while one was open for 0% of the time, Pallas kernels for 18%

profile of v3, /device:TPU:0, one launch (start us, length us, event | category | flops | bytes accessed | tf_op | source)
XLA Modules:
  0.0 31.8 jit_solution(7050924480443881053)
XLA Ops:
  0.6 0.8 %shard_map.76.own = bf16[256,128]{1,0:T(8,128)(2,1)S(1)} custom-call(bf16[128,128]{1,0:T(8,128)(2,1)} %keys.1, bf16[128,128]{1,0:T(8,128)(2,1)} %values.1), custom_call_target="tpu_custom_call" | custom-call | tf_op jit(solution)/shard_map/pallas_call | solution.py:461
  1.4 0.5 %collective-permute-start = (bf16[256,128]{1,0:T(8,128)(2,1)S(1)}, bf16[256,128]{1,0:T(8,128)(2,1)S(1)}, u32[]{:S(2)}, u32[]{:S(2)}) collective-permute-start(bf16[256,128]{1,0:T(8,128)(2,1)S(1)} %shard_map.76.own), channel_id=1, source_target_pairs={{0,2},{1,3},{2,0},{3,1},{4,6},{5,7},{6,4},{7,5},{8,10},{9,11},{10,... | collective-permute-start | bytes 196616 | tf_op jit(solution)/shard_map/ppermute | solution.py:20
  1.9 0.9 %collective-permute-done.partner = bf16[256,128]{1,0:T(8,128)(2,1)S(1)} collective-permute-done((bf16[256,128]{1,0:T(8,128)(2,1)S(1)}, bf16[256,128]{1,0:T(8,128)(2,1)S(1)}, u32[]{:S(2)}, u32[]{:S(2)}) %collective-permute-start) | collective-permute-done | bytes 65568 | tf_op jit(solution)/shard_map/ppermute | solution.py:20
  2.9 2.9 %collective-permute-start.3 = (bf16[512,128]{1,0:T(8,128)(2,1)S(1)}, bf16[512,128]{1,0:T(8,128)(2,1)S(1)}, u32[]{:S(2)}, u32[]{:S(2)}) collective-permute-start(bf16[512,128]{1,0:T(8,128)(2,1)S(1)} %pad_maximum_fusion.1), channel_id=1, source_target_pairs={{0,4},{1,5},{2,7},{3,6},{4,8},{5,9},{6,11},{7,10},{8,12},{9,13},{1... | collective-permute-start | bytes 393224 | tf_op jit(solution)/shard_map/ppermute | solution.py:20
  5.8 1.6 %collective-permute-start.2 = (bf16[512,128]{1,0:T(8,128)(2,1)S(1)}, bf16[512,128]{1,0:T(8,128)(2,1)S(1)}, u32[]{:S(2)}, u32[]{:S(2)}) collective-permute-start(bf16[512,128]{1,0:T(8,128)(2,1)S(1)} %pad_maximum_fusion.1), channel_id=1, source_target_pairs={{0,8},{1,9},{2,11},{3,10},{4,12},{5,13},{6,15},{7,14},{8,16},{9,17... | collective-permute-start | bytes 393224 | tf_op jit(solution)/shard_map/ppermute | solution.py:20
  7.4 1.5 %collective-permute-start.1 = (bf16[256,128]{1,0:T(8,128)(2,1)S(1)}, bf16[256,128]{1,0:T(8,128)(2,1)S(1)}, u32[]{:S(2)}, u32[]{:S(2)}) collective-permute-start(bf16[256,128]{1,0:T(8,128)(2,1)S(1)} %shard_map.76.own), channel_id=1, source_target_pairs={{0,1},{1,0},{2,3},{3,2},{4,5},{5,4},{6,7},{7,6},{8,9},{9,8},{10,11... | collective-permute-start | bytes 196616 | tf_op jit(solution)/shard_map/ppermute | solution.py:20
  8.9 1.8 %shard_map.77 = (f32[256,1024]{1,0:T(8,128)S(1)}, f32[256,1024]{1,0:T(8,128)S(1)}, f32[8,1024]{1,0:T(8,128)S(1)}, bf16[1024,128]{1,0:T(8,128)(2,1)S(1)}, bf16[10...) custom-call(s32[16]{0:T(128)} %doc_hbm.1, bf16[128,1024]{1,0:T(8,128)(2,1)} %q_hbm.1, bf16[128,1024]{1,0:T(8,128)(2,1)} %do_hbm.1, ...), custom_call_target="tpu_custom_call" | custom-call | flops 134217728 | bytes 2097152 | tf_op jit(solution)/shard_map/pallas_call | solution.py:461
  10.6 1.2 %collective-permute-done.1.by_x = bf16[256,128]{1,0:T(8,128)(2,1)S(1)} collective-permute-done((bf16[256,128]{1,0:T(8,128)(2,1)S(1)}, bf16[256,128]{1,0:T(8,128)(2,1)S(1)}, u32[]{:S(2)}, u32[]{:S(2)}) %collective-permute-start.1) | collective-permute-done | bytes 65568 | tf_op jit(solution)/shard_map/ppermute | solution.py:20
  11.9 1.4 %collective-permute-done.3.by_4 = bf16[512,128]{1,0:T(8,128)(2,1)S(1)} collective-permute-done((bf16[512,128]{1,0:T(8,128)(2,1)S(1)}, bf16[512,128]{1,0:T(8,128)(2,1)S(1)}, u32[]{:S(2)}, u32[]{:S(2)}) %collective-permute-start.3) | collective-permute-done | bytes 131104 | tf_op jit(solution)/shard_map/ppermute | solution.py:20
  13.2 0.6 %collective-permute-done.2.by_8 = bf16[512,128]{1,0:T(8,128)(2,1)S(1)} collective-permute-done((bf16[512,128]{1,0:T(8,128)(2,1)S(1)}, bf16[512,128]{1,0:T(8,128)(2,1)S(1)}, u32[]{:S(2)}, u32[]{:S(2)}) %collective-permute-start.2) | collective-permute-done | bytes 131104 | tf_op jit(solution)/shard_map/ppermute | solution.py:20
  13.9 0.5 %collective-permute-start.4 = (bf16[1024,128]{1,0:T(8,128)(2,1)S(1)}, bf16[1024,128]{1,0:T(8,128)(2,1)S(1)}, u32[]{:S(2)}, u32[]{:S(2)}) collective-permute-start(bf16[1024,128]{1,0:T(8,128)(2,1)S(1)} %pad_maximum_fusion), channel_id=1, source_target_pairs={{0,2},{1,3},{2,0},{3,1},{4,6},{5,7},{6,4},{7,5},{8,10},{9,11},{10,... | collective-permute-start | bytes 786440 | tf_op jit(solution)/shard_map/ppermute | solution.py:20
  14.4 1.3 %shard_map.78 = (f32[640,1024]{1,0:T(8,128)S(1)}, f32[640,1024]{1,0:T(8,128)S(1)}, f32[8,1024]{1,0:T(8,128)S(1)}) custom-call(bf16[1024,128]{1,0:T(8,128)(2,1)S(1)} %get-tuple-element.29.q_rows, bf16[1024,128]{1,0:T(8,128)(2,1)S(1)} %get-tuple-element.30.do_rows, s32[8,128]{1,0:T(8,128)S(1)} %get-tuple-element.33.starts, ...), custom_call_target="tpu_custom_call" | custom-call | flops 335544320 | bytes 5242880 | tf_op jit(solution)/shard_map/pallas_call | solution.py:461
  15.7 0.0 collective-permute-done.4.fetched
  15.7 2.2 %shard_map.79 = (bf16[1280,128]{1,0:T(8,128)(2,1)S(1)}, bf16[640,1024]{1,0:T(8,128)(2,1)S(1)}, f32[8,1024]{1,0:T(8,128)S(1)}) custom-call(bf16[1024,128]{1,0:T(8,128)(2,1)S(1)} %get-tuple-element.29.q_rows, bf16[1024,128]{1,0:T(8,128)(2,1)S(1)} %get-tuple-element.30.do_rows, s32[8,128]{1,0:T(8,128)S(1)} %get-tuple-element.33.starts, ...), custom_call_target="tpu_custom_call" | custom-call | flops 603979776 | bytes 9437184 | tf_op jit(solution)/shard_map/pallas_call | solution.py:461
  17.9 0.3 collective-permute-start.5
  18.2 1.0 %shard_map.80 = (f32[1280,128]{1,0:T(8,128)S(1)}, bf16[640,1024]{1,0:T(8,128)(2,1)S(1)}) custom-call(bf16[1024,128]{1,0:T(8,128)(2,1)S(1)} %get-tuple-element.29.q_rows, bf16[1024,128]{1,0:T(8,128)(2,1)S(1)} %get-tuple-element.30.do_rows, f32[640,1024]{1,0:T(8,128)S(1)} %get-tuple-element.42.p_ref, f32[640,1024]{1,0:T(8,128)S(1)} %get-tuple-element.43.dp_ref, ...), custom_call_target="tpu_custom_call" | custom-call | flops 335544320 | bytes 5242880 | tf_op jit(solution)/shard_map/pallas_call | solution.py:461
  19.2 0.4 %collective-permute-done.5 = bf16[1280,128]{1,0:T(8,128)(2,1)S(1)} collective-permute-done((bf16[1280,128]{1,0:T(8,128)(2,1)S(1)}, bf16[1280,128]{1,0:T(8,128)(2,1)S(1)}, u32[]{:S(2)}, u32[]{:S(2)}) %collective-permute-start.5) | collective-permute-done | bytes 327712 | tf_op jit(solution)/shard_map/ppermute | solution.py:20
  19.8 1.9 %collective-permute-start.6 = (bf16[512,128]{1,0:T(8,128)(2,1)S(1)}, bf16[512,128]{1,0:T(8,128)(2,1)S(1)}, u32[]{:S(2)}, u32[]{:S(2)}) collective-permute-start(bf16[512,128]{1,0:T(8,128)(2,1)S(1)} %pad_maximum_fusion.2), channel_id=1, source_target_pairs={{0,24},{1,25},{2,27},{3,26},{4,28},{5,29},{6,31},{7,30},{8,0},{9,1... | collective-permute-start | bytes 393224 | tf_op jit(solution)/shard_map/ppermute | solution.py:20
  21.6 2.4 %collective-permute-start.7 = (bf16[512,128]{1,0:T(8,128)(2,1)S(1)}, bf16[512,128]{1,0:T(8,128)(2,1)S(1)}, u32[]{:S(2)}, u32[]{:S(2)}) collective-permute-start(bf16[512,128]{1,0:T(8,128)(2,1)S(1)} %fusion), channel_id=1, source_target_pairs={{0,28},{1,29},{2,31},{3,30},{4,0},{5,1},{6,3},{7,2},{8,4},{9,5},{1... | collective-permute-start | bytes 393224 | tf_op jit(solution)/shard_map/ppermute | solution.py:20
  24.0 1.2 %collective-permute-start.8 = (bf16[256,128]{1,0:T(8,128)(2,1)S(1)}, bf16[256,128]{1,0:T(8,128)(2,1)S(1)}, u32[]{:S(2)}, u32[]{:S(2)}) collective-permute-start(bf16[256,128]{1,0:T(8,128)(2,1)S(1)} %get-tuple-element.55), channel_id=1, source_target_pairs={{0,1},{1,0},{2,3},{3,2},{4,5},{5,4},{6,7},{7,6},{8,9},{9,8},{10,11... | collective-permute-start | bytes 196616 | tf_op jit(solution)/shard_map/ppermute | solution.py:20
  25.2 1.8 %shard_map.81 = (bf16[128,1024]{1,0:T(8,128)(2,1)}, f32[256,128]{1,0:T(8,128)S(1)}) custom-call(bf16[1024,128]{1,0:T(8,128)(2,1)S(1)} %get-tuple-element.29.q_rows, bf16[1024,128]{1,0:T(8,128)(2,1)S(1)} %get-tuple-element.30.do_rows, f32[256,1024]{1,0:T(8,128)S(1)} %get-tuple-element.31.p_near.p_ref, f32[256,1024]{1,0:T(8,128)S(1)} %get-tuple-element.32.dp_near.dp_ref, ...), custom_call_target="tpu_custom_call" | custom-call | flops 436207616 | bytes 6815744 | tf_op jit(solution)/shard_map/pallas_call | solution.py:461
  27.0 2.8 %collective-permute-done.8.back_x = bf16[256,128]{1,0:T(8,128)(2,1)S(1)} collective-permute-done((bf16[256,128]{1,0:T(8,128)(2,1)S(1)}, bf16[256,128]{1,0:T(8,128)(2,1)S(1)}, u32[]{:S(2)}, u32[]{:S(2)}) %collective-permute-start.8) | collective-permute-done | bytes 65568 | tf_op jit(solution)/shard_map/ppermute | solution.py:20
  29.8 0.0 collective-permute-done.6
  29.8 0.0 collective-permute-done.7
  29.9 0.1 collective-permute-start.9
  30.0 1.2 %collective-permute-done.9.last = bf16[256,128]{1,0:T(8,128)(2,1)S(1)} collective-permute-done((bf16[256,128]{1,0:T(8,128)(2,1)S(1)}, bf16[256,128]{1,0:T(8,128)(2,1)S(1)}, u32[]{:S(2)}, u32[]{:S(2)}) %collective-permute-start.9) | collective-permute-done | bytes 65568 | tf_op jit(solution)/shard_map/ppermute | solution.py:20
  31.2 0.7 %shard_map.82 = (bf16[128,128]{1,0:T(8,128)(2,1)}, bf16[128,128]{1,0:T(8,128)(2,1)}) custom-call(f32[256,128]{1,0:T(8,128)S(1)} %get-tuple-element.49.mine, bf16[256,128]{1,0:T(8,128)(2,1)S(1)} %slice.48.given, bf16[256,128]{1,0:T(8,128)(2,1)S(1)} %collective-permute-done.8.back_x, f32[512,128]{1,0:T(8,128)S(1)} %convert_add_fusion.far, ...), custom_call_target="tpu_custom_call" | custom-call | tf_op jit(solution)/shard_map/pallas_call | solution.py:461
  (10 shorter events, 0.2 us)
Async XLA Ops:
  1.4 1.4 %collective-permute-start = (bf16[256,128]{1,0:T(8,128)(2,1)S(1)}, bf16[256,128]{1,0:T(8,128)(2,1)S(1)}, u32[]{:S(2)}, u32[]{:S(2)}) collective-permute-start(bf16[256,128]{1,0:T(8,128)(2,1)S(1)} %shard_map.76.own), channel_id=1, source_target_pairs={{0,2},{1,3},{2,0},{3,1},{4,6},{5,7},{6,4},{7,5},{8,10},{9,11},{10,... | collective-permute-start | bytes 196616 | tf_op jit(solution)/shard_map/ppermute | solution.py:20
  2.9 10.4 %collective-permute-start.3 = (bf16[512,128]{1,0:T(8,128)(2,1)S(1)}, bf16[512,128]{1,0:T(8,128)(2,1)S(1)}, u32[]{:S(2)}, u32[]{:S(2)}) collective-permute-start(bf16[512,128]{1,0:T(8,128)(2,1)S(1)} %pad_maximum_fusion.1), channel_id=1, source_target_pairs={{0,4},{1,5},{2,7},{3,6},{4,8},{5,9},{6,11},{7,10},{8,12},{9,13},{1... | collective-permute-start | bytes 393224 | tf_op jit(solution)/shard_map/ppermute | solution.py:20
  5.8 8.1 %collective-permute-start.2 = (bf16[512,128]{1,0:T(8,128)(2,1)S(1)}, bf16[512,128]{1,0:T(8,128)(2,1)S(1)}, u32[]{:S(2)}, u32[]{:S(2)}) collective-permute-start(bf16[512,128]{1,0:T(8,128)(2,1)S(1)} %pad_maximum_fusion.1), channel_id=1, source_target_pairs={{0,8},{1,9},{2,11},{3,10},{4,12},{5,13},{6,15},{7,14},{8,16},{9,17... | collective-permute-start | bytes 393224 | tf_op jit(solution)/shard_map/ppermute | solution.py:20
  7.4 4.5 %collective-permute-start.1 = (bf16[256,128]{1,0:T(8,128)(2,1)S(1)}, bf16[256,128]{1,0:T(8,128)(2,1)S(1)}, u32[]{:S(2)}, u32[]{:S(2)}) collective-permute-start(bf16[256,128]{1,0:T(8,128)(2,1)S(1)} %shard_map.76.own), channel_id=1, source_target_pairs={{0,1},{1,0},{2,3},{3,2},{4,5},{5,4},{6,7},{7,6},{8,9},{9,8},{10,11... | collective-permute-start | bytes 196616 | tf_op jit(solution)/shard_map/ppermute | solution.py:20
  13.9 1.8 %collective-permute-start.4 = (bf16[1024,128]{1,0:T(8,128)(2,1)S(1)}, bf16[1024,128]{1,0:T(8,128)(2,1)S(1)}, u32[]{:S(2)}, u32[]{:S(2)}) collective-permute-start(bf16[1024,128]{1,0:T(8,128)(2,1)S(1)} %pad_maximum_fusion), channel_id=1, source_target_pairs={{0,2},{1,3},{2,0},{3,1},{4,6},{5,7},{6,4},{7,5},{8,10},{9,11},{10,... | collective-permute-start | bytes 786440 | tf_op jit(solution)/shard_map/ppermute | solution.py:20
  17.9 1.7 %collective-permute-start.5 = (bf16[1280,128]{1,0:T(8,128)(2,1)S(1)}, bf16[1280,128]{1,0:T(8,128)(2,1)S(1)}, u32[]{:S(2)}, u32[]{:S(2)}) collective-permute-start(bf16[1280,128]{1,0:T(8,128)(2,1)S(1)} %get-tuple-element.47), channel_id=1, source_target_pairs={{0,2},{1,3},{2,0},{3,1},{4,6},{5,7},{6,4},{7,5},{8,10},{9,11},{10,... | collective-permute-start | bytes 983048 | tf_op jit(solution)/shard_map/ppermute | solution.py:20
  19.8 10.0 %collective-permute-start.6 = (bf16[512,128]{1,0:T(8,128)(2,1)S(1)}, bf16[512,128]{1,0:T(8,128)(2,1)S(1)}, u32[]{:S(2)}, u32[]{:S(2)}) collective-permute-start(bf16[512,128]{1,0:T(8,128)(2,1)S(1)} %pad_maximum_fusion.2), channel_id=1, source_target_pairs={{0,24},{1,25},{2,27},{3,26},{4,28},{5,29},{6,31},{7,30},{8,0},{9,1... | collective-permute-start | bytes 393224 | tf_op jit(solution)/shard_map/ppermute | solution.py:20
  21.6 8.2 %collective-permute-start.7 = (bf16[512,128]{1,0:T(8,128)(2,1)S(1)}, bf16[512,128]{1,0:T(8,128)(2,1)S(1)}, u32[]{:S(2)}, u32[]{:S(2)}) collective-permute-start(bf16[512,128]{1,0:T(8,128)(2,1)S(1)} %fusion), channel_id=1, source_target_pairs={{0,28},{1,29},{2,31},{3,30},{4,0},{5,1},{6,3},{7,2},{8,4},{9,5},{1... | collective-permute-start | bytes 393224 | tf_op jit(solution)/shard_map/ppermute | solution.py:20
  24.0 5.8 %collective-permute-start.8 = (bf16[256,128]{1,0:T(8,128)(2,1)S(1)}, bf16[256,128]{1,0:T(8,128)(2,1)S(1)}, u32[]{:S(2)}, u32[]{:S(2)}) collective-permute-start(bf16[256,128]{1,0:T(8,128)(2,1)S(1)} %get-tuple-element.55), channel_id=1, source_target_pairs={{0,1},{1,0},{2,3},{3,2},{4,5},{5,4},{6,7},{7,6},{8,9},{9,8},{10,11... | collective-permute-start | bytes 196616 | tf_op jit(solution)/shard_map/ppermute | solution.py:20
  29.9 1.3 %collective-permute-start.9 = (bf16[256,128]{1,0:T(8,128)(2,1)S(1)}, bf16[256,128]{1,0:T(8,128)(2,1)S(1)}, u32[]{:S(2)}, u32[]{:S(2)}) collective-permute-start(bf16[256,128]{1,0:T(8,128)(2,1)S(1)} %slice.64), channel_id=1, source_target_pairs={{0,2},{1,3},{2,0},{3,1},{4,6},{5,7},{6,4},{7,5},{8,10},{9,11},{10,... | collective-permute-start | bytes 196616 | tf_op jit(solution)/shard_map/ppermute | solution.py:20

commit v4 on v3

--- a/solution.py
+++ b/solution.py
@@ -29,11 +29,13 @@
 
 
 def ahead(steps, at, count):
-    return ((at + steps) % count) ^ ((at >> 1) & 1)
+    after = at + steps
+    return after ^ ((at >> 1) & 1) if after < count else after - count
 
 
 def behind(steps, at, count):
-    return ((at ^ ((at >> 1) & 1)) - steps) % count
+    before = at - steps
+    return before ^ ((at >> 1) & 1) if before >= 0 else before + count
 
 
 def own_slots(at):
@@ -243,60 +245,97 @@
     return start
 
 
-def score_blocks(ids, blocks, start, me, q_rows, do_rows, bias, p_ref, dp_ref):
+def by_reach(me, choices, body):
+    for reached, chosen in zip((me >= 8, (me >= 4) & (me < 8), me < 4), choices):
+
+        @pl.when(reached)
+        def _():
+            body(chosen)
+
+
+def score_blocks(which, ids, blocks, start, me, q_rows, do_rows, bias, p_ref, dp_ref, stats):
+    count = len(blocks)
+    for b in range(count):
+        if b not in which:
+            stats[b : b + 1, :] = jnp.full((1, stats.shape[1]), NEG, jnp.float32)
+            for kind in (1, 2):
+                at = kind * count + b
+                stats[at : at + 1, :] = jnp.zeros((1, stats.shape[1]), jnp.float32)
+    if not which:
+        return
     rows, head_dim = q_rows.shape
     tokens = bias.shape[1]
     factor = math.log2(math.e) / math.sqrt(head_dim)
     position = me * tokens + lax.broadcasted_iota(jnp.int32, (1, tokens), 1)
-    spans = [slice(b * tokens, (b + 1) * tokens) for b in range(len(blocks))]
-    for span, at in zip(spans, ids):
+    spans = [slice(b * tokens, (b + 1) * tokens) for b in which]
+    blocks = [blocks[b] for b in which]
+    for span, at in zip(spans, [ids[b] for b in which]):
         key_at = at * tokens + lax.broadcasted_iota(jnp.int32, (tokens, tokens), 0)
         seen = (key_at >= start) & (key_at <= position)
         bias[span, :] = jnp.where(seen, 0.0, NEG)
     width = 2 * tokens
-    stats = []
+    parts = [[] for _ in blocks]
     for pair in range(rows // width):
         cols = slice(pair * width, (pair + 1) * width)
         qp, dop = q_rows[cols, :], do_rows[cols, :]
-        peak = jnp.full((8, width), NEG, jnp.float32)
-        for span, (keys, values) in zip(spans, blocks):
-            scores = lax.dot_general(
-                keys(), qp, LANES_CONTRACT, preferred_element_type=jnp.float32
-            )
+        for b, (span, found) in enumerate(zip(spans, parts)):
+            if b % 4 == 0:
+                group = blocks[b : b + 4]
+                keys = jnp.concatenate([block[0]() for block in group], axis=0)
+                values = jnp.concatenate([block[1]() for block in group], axis=0)
+                scores_all = lax.dot_general(
+                    keys, qp, LANES_CONTRACT, preferred_element_type=jnp.float32
+                )
+                dp_all = lax.dot_general(
+                    values, dop, LANES_CONTRACT, preferred_element_type=jnp.float32
+                )
+            at = slice(b % 4 * tokens, (b % 4 + 1) * tokens)
+            scores, dp = scores_all[at], dp_all[at]
             off = bias[span, :]
             t = scores * factor + jnp.concatenate([off, off], axis=1)
-            p_ref[span, cols] = t
-            peak = jnp.maximum(peak, jnp.max(t.reshape(tokens // 8, 8, width), axis=0))
-        peak = jnp.max(peak, axis=0, keepdims=True)
-        total = jnp.zeros((8, width), jnp.float32)
-        moment = jnp.zeros((8, width), jnp.float32)
-        for span, (keys, values) in zip(spans, blocks):
-            p = jnp.exp2(p_ref[span, cols] - peak)
-            dp = lax.dot_general(
-                values(), dop, LANES_CONTRACT, preferred_element_type=jnp.float32
-            )
+            peak = jnp.max(t, axis=0, keepdims=True)
+            p = jnp.exp2(t - peak)
             p_ref[span, cols] = p
             dp_ref[span, cols] = dp
-            total = total + jnp.sum(p.reshape(tokens // 8, 8, width), axis=0)
-            moment = moment + jnp.sum((p * dp).reshape(tokens // 8, 8, width), axis=0)
-        stats.append(
-            (
-                peak,
-                jnp.sum(total, axis=0, keepdims=True),
-                jnp.sum(moment, axis=0, keepdims=True),
-            )
-        )
-    return [jnp.concatenate(parts, axis=1) for parts in zip(*stats)]
-
-
-def grad_block(p_ref, dp_ref, span, share, delta, q_rows, do_rows, ds_ref, ds_span):
-    p = p_ref[span, :] * share
-    low = p.astype(jnp.bfloat16)
-    ds = (p * (dp_ref[span, :] - delta)).astype(jnp.bfloat16)
-    ds_ref[ds_span, :] = ds
-    dk = jnp.dot(ds, q_rows[...], preferred_element_type=jnp.float32)
-    dv = jnp.dot(low, do_rows[...], preferred_element_type=jnp.float32)
-    return dk, dv
+            total = jnp.sum(p, axis=0, keepdims=True)
+            found.append((peak, total, jnp.sum(p * dp, axis=0, keepdims=True)))
+    for b, found in zip(which, parts):
+        for kind, values in enumerate(zip(*found)):
+            at = kind * count + b
+            stats[at : at + 1, :] = jnp.concatenate(values, axis=1)
+
+
+def get_stats(ref, n):
+    return [[ref[kind * n + b : kind * n + b + 1, :] for kind in range(3)] for b in range(n)]
+
+
+def grad_blocks(which, reads, delta, q_rows, do_rows, ds_ref, put):
+    head_dim = q_rows.shape[1]
+    tokens = ds_ref.shape[0] // len(reads)
+    for b in range(len(reads)):
+        if b not in which:
+            nothing = jnp.zeros((tokens, head_dim), jnp.float32)
+            put(b, nothing, nothing)
+    for start in range(0, len(which), 4):
+        lows, all_ds = [], []
+        for b in which[start : start + 4]:
+            weights, dprobs, share = reads[b]
+            p = weights() * share
+            lows.append(p.astype(jnp.bfloat16))
+            ds = (p * (dprobs() - delta)).astype(jnp.bfloat16)
+            ds_ref[b * tokens : (b + 1) * tokens, :] = ds
+            all_ds.append(ds)
+        low, ds = jnp.concatenate(lows, axis=0), jnp.concatenate(all_ds, axis=0)
+        dk = jnp.dot(ds, q_rows[...], preferred_element_type=jnp.float32)
+        dv = jnp.dot(low, do_rows[...], preferred_element_type=jnp.float32)
+        for i, b in enumerate(which[start : start + 4]):
+            span = slice(i * tokens, (i + 1) * tokens)
+            put(b, dk[span], dv[span])
+
+
+def reads_of(p_ref, dp_ref, i, tokens, share):
+    span = slice(i * tokens, (i + 1) * tokens)
+    return (lambda: p_ref[span, :]), (lambda: dp_ref[span, :]), share
 
 
 def block_of(ref, i, tokens):
@@ -325,7 +364,7 @@
 
 
 def near_kernel(
-    docs, doc_hbm, q_hbm, do_hbm, own, partner,
+    docs, doc_hbm, q_hbm, do_hbm, own, partner, by_x,
     p_out, dp_out, stats, q_rows, do_rows, starts,
     bias, doc_ref, sems,
 ):
@@ -350,23 +389,27 @@
     position = me * tokens + lax.broadcasted_iota(jnp.int32, (1, tokens), 1)
     start = document_starts(doc_ref, docs, position)
     starts[0:1, :] = start
-    peak, total, moment = score_blocks(
-        [me, me ^ 2],
-        [block_of(own, 0, tokens), block_of(partner, 0, tokens)],
-        start, me, q_rows, do_rows, bias, p_out, dp_out,
-    )
-    stats[0:1, :], stats[1:2, :], stats[2:3, :] = peak, total, moment
-
-
-def direct_kernel(q_rows, do_rows, starts, by_x, by_8, by_4, p_out, dp_out, stats, bias):
+    score_blocks(
+        (0, 1, 2),
+        [me, me ^ 2, me ^ 1],
+        [block_of(ref, 0, tokens) for ref in (own, partner, by_x)],
+        start, me, q_rows, do_rows, bias, p_out, dp_out, stats,
+    )
+
+
+def direct_kernel(q_rows, do_rows, starts, by_8, by_4, p_out, dp_out, stats, bias):
     me = own_position()
     tokens = starts.shape[1]
-    peak, total, moment = score_blocks(
-        own_slots(me),
-        [block_of(by_x, 0, tokens)] + [block_of(ref, i, tokens) for ref in (by_8, by_4) for i in range(2)],
-        starts[0:1, :], me, q_rows, do_rows, bias, p_out, dp_out,
-    )
-    stats[0:1, :], stats[1:2, :], stats[2:3, :] = peak, total, moment
+    by_reach(
+        me,
+        ((0, 1, 2, 3), (2, 3), ()),
+        lambda which: score_blocks(
+            which,
+            own_slots(me)[1:],
+            [block_of(ref, i, tokens) for ref in (by_8, by_4) for i in range(2)],
+            starts[0:1, :], me, q_rows, do_rows, bias, p_out, dp_out, stats,
+        ),
+    )
 
 
 def fetched_ids(me):
@@ -375,63 +418,86 @@
 
 
 def fetched_kernel(
-    q_rows, do_rows, starts, fetched, p_near, dp_near, stats_near, stats_direct,
-    give, ds_out, shares, bias, p_buf, dp_buf,
+    q_rows, do_rows, starts, fetched, stats_near, stats_direct,
+    give, ds_out, shares, bias, p_buf, dp_buf, stats,
+):
+    by_reach(
+        own_position(),
+        ((0, 1, 2, 3), (0, 2, 3), (0,)),
+        lambda which: fetched_blocks(
+            which, q_rows, do_rows, starts, fetched, stats_near, stats_direct,
+            give, ds_out, shares, bias, p_buf, dp_buf, stats,
+        ),
+    )
+
+
+def fetched_blocks(
+    which, q_rows, do_rows, starts, fetched, stats_near, stats_direct,
+    give, ds_out, shares, bias, p_buf, dp_buf, stats,
 ):
     me = own_position()
     tokens = starts.shape[1]
-    ids = fetched_ids(me)
-    peak, total, moment = score_blocks(
-        ids,
+    score_blocks(
+        which,
+        fetched_ids(me),
         [block_of(fetched, i, tokens) for i in range(4)],
-        starts[0:1, :], me, q_rows, do_rows, bias, p_buf, dp_buf,
-    )
-    parts = [(ref[0:1, :], ref[1:2, :], ref[2:3, :]) for ref in (stats_near, stats_direct)]
-    parts.append((peak, total, moment))
-    top = jnp.maximum(jnp.maximum(parts[0][0], parts[1][0]), peak)
+        starts[0:1, :], me, q_rows, do_rows, bias, p_buf, dp_buf, stats,
+    )
+    parts = get_stats(stats_near, 3) + get_stats(stats_direct, 4) + get_stats(stats, 4)
+    top = functools.reduce(jnp.maximum, [part[0] for part in parts])
     factors = [jnp.exp2(part[0] - top) for part in parts]
     one = 1.0 / sum(f * part[1] for f, part in zip(factors, parts))
     delta = sum(f * part[2] for f, part in zip(factors, parts)) * one
     shared = [f * one for f in factors]
-    shares[0:1, :], shares[1:2, :], shares[2:3, :] = shared[0], shared[1], delta
-    for i in range(4):
-        span = slice(i * tokens, (i + 1) * tokens)
-        put_block(give, 1 + i, *grad_block(p_buf, dp_buf, span, shared[2], delta, q_rows, do_rows, ds_out, span))
-    put_block(
-        give, 0,
-        *grad_block(
-            p_near, dp_near, slice(tokens, 2 * tokens), shared[0], delta, q_rows, do_rows,
-            ds_out, slice(4 * tokens, 5 * tokens),
-        ),
-    )
-
-
-def keep_kernel(q_rows, do_rows, p_ref, dp_ref, shares, keep, ds_out):
-    tokens = p_ref.shape[0] // 5
-    share, delta = shares[1:2, :], shares[2:3, :]
-    for i in range(5):
-        span = slice(i * tokens, (i + 1) * tokens)
-        put_block(keep, i, *grad_block(p_ref, dp_ref, span, share, delta, q_rows, do_rows, ds_out, span))
+    for n in range(7):
+        shares[n : n + 1, :] = shared[n]
+    shares[7:8, :] = delta
+    reads = [reads_of(p_buf, dp_buf, i, tokens, shared[7 + i]) for i in range(4)]
+    grad_blocks(which, reads, delta, q_rows, do_rows, ds_out, functools.partial(put_block, give))
+
+
+def keep_kernel(q_rows, do_rows, p_near, dp_near, p_direct, dp_direct, shares, keep, ds_out):
+    tokens = p_near.shape[0] // 3
+    delta = shares[7:8, :]
+    places = [(p_near, dp_near, 2, 2)] + [(p_direct, dp_direct, 3 + i, i) for i in range(4)]
+    reads = [
+        reads_of(p_ref, dp_ref, i, tokens, shares[part : part + 1, :]) for p_ref, dp_ref, part, i in places
+    ]
+    by_reach(
+        own_position(),
+        ((0, 1, 2, 3, 4), (0, 3, 4), (0,)),
+        lambda which: grad_blocks(which, reads, delta, q_rows, do_rows, ds_out, functools.partial(put_block, keep)),
+    )
 
 
 def query_kernel(
-    q_rows, do_rows, p_ref, dp_ref, shares, ds_fetched, ds_direct, fetched, partner, by_x, by_8, by_4, own,
-    dq_ref, mine, ds_own,
+    q_rows, do_rows, p_ref, dp_ref, shares, ds_fetched, ds_direct, fetched, partner, by_x, by_8, by_4, own, back_x,
+    dq_ref, mine, partners, ds_near,
 ):
     tokens = dq_ref.shape[0]
     head_dim = own.shape[1]
     scale = 1.0 / math.sqrt(head_dim)
-    span = slice(0, tokens)
-    put_block(
-        mine, 0, *grad_block(p_ref, dp_ref, span, shares[0:1, :], shares[2:3, :], q_rows, do_rows, ds_own, span)
-    )
+    reads = [reads_of(p_ref, dp_ref, n, tokens, shares[n : n + 1, :]) for n in range(2)]
+    grad_blocks(
+        (0, 1), reads, shares[7:8, :], q_rows, do_rows, ds_near,
+        lambda n, dk, dv: put_block((mine, partners)[n], 0, dk, dv),
+    )
+    mine[...] += back_x[...].astype(jnp.float32)
     where = [(ds_fetched, i, block_of(fetched, i, tokens)) for i in range(4)]
-    where.append((ds_fetched, 4, block_of(partner, 0, tokens)))
     direct = [(by_x, 0)] + [(ref, i) for ref in (by_8, by_4) for i in range(2)]
     where += [(ds_direct, n, block_of(ref, i, tokens)) for n, (ref, i) in enumerate(direct)]
-    where.append((ds_own, 0, block_of(own, 0, tokens)))
-    width = 2 * tokens
-    for pair in range(q_rows.shape[0] // width):
+    where += [(ds_near, n, block_of(ref, 0, tokens)) for n, ref in enumerate((own, partner))]
+    by_reach(
+        own_position(),
+        (range(11), (0, 2, 3, 4, 7, 8, 9, 10), (0, 4, 9, 10)),
+        lambda which: query_blocks([where[n] for n in which], dq_ref, scale),
+    )
+
+
+def query_blocks(where, dq_ref, scale):
+    tokens, width = dq_ref.shape[0], 2 * dq_ref.shape[0]
+    head_dim = where[0][2][0]().shape[1]
+    for pair in range(dq_ref.shape[1] // (2 * head_dim)):
         cols = slice(pair * width, (pair + 1) * width)
         dq = jnp.zeros((width, head_dim), jnp.float32)
         for ref, n, (keys, values) in where:
@@ -445,13 +511,11 @@
             dq_ref[:, h * head_dim : (h + 1) * head_dim] = dq[i * tokens : (i + 1) * tokens]
 
 
-def result_kernel(mine, given, back_x, far, last, dk_ref, dv_ref):
+def result_kernel(mine, far, last, dk_ref, dv_ref):
     tokens, head_dim = dk_ref.shape
-    high = jnp.float32
     for half, (ref, scale) in enumerate(((dk_ref, 1.0 / math.sqrt(head_dim)), (dv_ref, 1.0))):
         span = slice(half * tokens, (half + 1) * tokens)
-        sums = mine[span, :] + given[span, :].astype(high) + back_x[span, :].astype(high)
-        sums = sums + far[span, :] + last[span, :].astype(high)
+        sums = mine[span, :] + far[span, :] + last[span, :].astype(jnp.float32)
         ref[...] = (sums * scale).astype(ref.dtype)
 
 
@@ -482,7 +546,7 @@
     second = (own_position() >> 1) & 1
 
     def part(n):
-        return [((n * tokens, rows), high)] * 2 + [((8, rows), high)], [((n * tokens, tokens), high)]
+        return [((n * tokens, rows), high)] * 2 + [((16, rows), high)], [((n * tokens, tokens), high)]
 
     (own,) = local_call(
         pack_kernel, [((block, head_dim), low)], [pltpu.SemaphoreType.DMA((2,))], [keys, values], 0, far=2
@@ -492,7 +556,7 @@
     both = jnp.concatenate([own, partner], axis=0)
     by_4 = permuted(both, functools.partial(ahead, 4))
     by_8 = permuted(both, functools.partial(ahead, 8))
-    outs, scratch = part(2)
+    outs, scratch = part(3)
     p_near, dp_near, stats_near, q_rows, do_rows, starts = local_call(
         functools.partial(near_kernel, docs),
         outs + [((rows, head_dim), low)] * 2 + [((8, tokens), jnp.int32)],
@@ -501,60 +565,62 @@
             pltpu.SMEM(doc_lengths.shape, jnp.int32),
             pltpu.SemaphoreType.DMA((2 * (rows // tokens) + 1,)),
         ],
-        [doc_lengths, queries, grad_out, own, partner],
-        4,
+        [doc_lengths, queries, grad_out, own, partner, by_x],
+        40,
         far=3,
     )
-    by_x, by_8, by_4, stats_near = lax.optimization_barrier((by_x, by_8, by_4, stats_near))
+    by_8, by_4, stats_near = lax.optimization_barrier((by_8, by_4, stats_near))
     offered = jnp.where(second == 0, by_x, by_8[:block])
     fetched = permuted(jnp.concatenate([offered, by_8[block:], by_4], axis=0), across_core)
     p_direct, dp_direct, stats_direct = local_call(
-        direct_kernel, *part(5), [q_rows, do_rows, starts, by_x, by_8, by_4], 10
+        direct_kernel, *part(4), [q_rows, do_rows, starts, by_8, by_4], 8
     )
     give, ds_fetched, shares = local_call(
         fetched_kernel,
-        [((5 * block, head_dim), low), ((5 * tokens, rows), low), ((8, rows), high)],
-        part(4)[1] + [((4 * tokens, rows), high)] * 2,
-        [q_rows, do_rows, starts, fetched, p_near, dp_near, stats_near, stats_direct],
-        18,
+        [((4 * block, head_dim), low), ((4 * tokens, rows), low), ((8, rows), high)],
+        part(4)[1] + [((4 * tokens, rows), high)] * 2 + [((16, rows), high)],
+        [q_rows, do_rows, starts, fetched, stats_near, stats_direct],
+        16,
     )
     given = permuted(give, across_core)
     keep, ds_direct = local_call(
         keep_kernel,
         [((5 * block, head_dim), high), ((5 * tokens, rows), low)],
         [],
-        [q_rows, do_rows, p_direct, dp_direct, shares],
+        [q_rows, do_rows, p_near, dp_near, p_direct, dp_direct, shares],
         10,
     )
     back = given.astype(high)
-    swapped = back[block : 2 * block]
+    swapped = back[:block]
     total_x = (keep[:block] + jnp.where(second == 0, swapped, 0.0)).astype(low)
     total_8 = jnp.concatenate(
         [
             keep[block : 2 * block] + jnp.where(second == 0, 0.0, swapped),
-            keep[2 * block : 3 * block] + back[2 * block : 3 * block],
+            keep[2 * block : 3 * block] + back[block : 2 * block],
         ],
         axis=0,
     ).astype(low)
-    total_4 = (keep[3 * block :] + back[3 * block :]).astype(low)
+    total_4 = (keep[3 * block :] + back[2 * block :]).astype(low)
     back_4 = permuted(total_4, functools.partial(behind, 4))
     back_8 = permuted(total_8, functools.partial(behind, 8))
     back_x = permuted(total_x, across_x)
-    grad_queries, mine = local_call(
+    grad_queries, mine, partners = local_call(
         query_kernel,
-        [(queries.shape, low), ((block, head_dim), high)],
-        [((tokens, rows), low)],
-        [q_rows, do_rows, p_near, dp_near, shares, ds_fetched, ds_direct, fetched, partner, by_x, by_8, by_4, own],
-        13,
-    )
-    back_8, back_4, back_x, mine = lax.optimization_barrier((back_8, back_4, back_x, mine))
+        [(queries.shape, low)] + [((block, head_dim), high)] * 2,
+        [((2 * tokens, rows), low)],
+        [
+            q_rows, do_rows, p_near, dp_near, shares, ds_fetched, ds_direct,
+            fetched, partner, by_x, by_8, by_4, own, back_x,
+        ],
+        40,
+    )
     far = back_8.astype(high) + back_4.astype(high)
-    last = permuted(far[block:].astype(low), across_core)
+    last = permuted((far[block:] + partners).astype(low), across_core)
     grad_keys, grad_values = local_call(
         result_kernel,
         [((tokens, head_dim), low)] * 2,
         [],
-        [mine, given[:block], back_x, far, last],
+        [mine, far, last],
         0,
     )
     return grad_queries, grad_keys, grad_values

time: 32.1 us -> 31.1 us (0.969)
  Pallas kernels: 9.45 us -> 5.99 us
  waiting for transfers between devices: 8.62 us -> 10.6 us
  starting transfers between devices: 12.8 us -> 13.2 us
    pallas_call x7, Pallas kernels: 9.45 us -> 5.99 us  [local_call(): pl.pallas_call(kernel, out_shape=[jax.ShapeDtypeStruct(shape, kind) for s...]
    ppermute x10, waiting for transfers between devices: 8.62 us -> 10.6 us  [permuted(): lax.ppermute(value, AXES, [(at, target(at, count)) for at in range(count)])]
    ppermute x10, starting transfers between devices: 12.8 us -> 13.2 us  [permuted(): lax.ppermute(value, AXES, [(at, target(at, count)) for at in range(count)])]
  transfers between devices with their start and end apart: 10 -> 10, of which waited for: 7 -> 6; matrix products, arithmetic and copies ran while one was open for 0% -> 0% of each run, Pallas kernels for 18% -> 13%
where the time goes in v4:
time: 31.1 us; the launch traced here: 30.7 us
  starting transfers between devices  13.2 us (42%)
  waiting for transfers between devices  10.6 us (34%)
  Pallas kernels  5.99 us (19%)
  between operations  0.74 us (2%)
    ppermute x10, starting transfers between devices, permuted(): lax.ppermute(value, AXES, [(at, target(at, count)) for at in range(count)])  13.2 us
    ppermute x10, waiting for transfers between devices, permuted(): lax.ppermute(value, AXES, [(at, target(at, count)) for at in range(count)])  10.6 us
    pallas_call x7, Pallas kernels, local_call(): pl.pallas_call(kernel, out_shape=[jax.ShapeDtypeStruct(shape, kind) for s...  5.99 us
  transfers between devices with their start and end apart: 10, of which 6 were waited for; matrix products, arithmetic and copies ran while one was open for 0% of the time, Pallas kernels for 13%

profile of v4, /device:TPU:0, one launch (start us, length us, event | category | flops | bytes accessed | tf_op | source)
XLA Modules:
  0.0 30.7 jit_solution(8008920829645283081)
XLA Ops:
  0.6 0.8 %shard_map.76.own = bf16[256,128]{1,0:T(8,128)(2,1)S(1)} custom-call(bf16[128,128]{1,0:T(8,128)(2,1)} %keys.1, bf16[128,128]{1,0:T(8,128)(2,1)} %values.1), custom_call_target="tpu_custom_call" | custom-call | tf_op jit(solution)/shard_map/pallas_call | solution.py:525
  1.4 0.5 %collective-permute-start = (bf16[256,128]{1,0:T(8,128)(2,1)S(1)}, bf16[256,128]{1,0:T(8,128)(2,1)S(1)}, u32[]{:S(2)}, u32[]{:S(2)}) collective-permute-start(bf16[256,128]{1,0:T(8,128)(2,1)S(1)} %shard_map.76.own), channel_id=1, source_target_pairs={{0,2},{1,3},{2,0},{3,1},{4,6},{5,7},{6,4},{7,5},{8,10},{9,11},{10,... | collective-permute-start | bytes 196616 | tf_op jit(solution)/shard_map/ppermute | solution.py:20
  1.9 2.6 %collective-permute-start.1 = (bf16[256,128]{1,0:T(8,128)(2,1)S(1)}, bf16[256,128]{1,0:T(8,128)(2,1)S(1)}, u32[]{:S(2)}, u32[]{:S(2)}) collective-permute-start(bf16[256,128]{1,0:T(8,128)(2,1)S(1)} %shard_map.76.own), channel_id=1, source_target_pairs={{0,1},{1,0},{2,3},{3,2},{4,5},{5,4},{6,7},{7,6},{8,9},{9,8},{10,11... | collective-permute-start | bytes 196616 | tf_op jit(solution)/shard_map/ppermute | solution.py:20
  4.5 0.0 collective-permute-done.partner
  4.5 1.6 %collective-permute-start.3 = (bf16[512,128]{1,0:T(8,128)(2,1)S(1)}, bf16[512,128]{1,0:T(8,128)(2,1)S(1)}, u32[]{:S(2)}, u32[]{:S(2)}) collective-permute-start(bf16[512,128]{1,0:T(8,128)(2,1)S(1)} %pad_maximum_fusion.1), channel_id=1, source_target_pairs={{0,4},{1,5},{2,7},{3,6},{4,8},{5,9},{6,11},{7,10},{8,12},{9,13},{1... | collective-permute-start | bytes 393224 | tf_op jit(solution)/shard_map/ppermute | solution.py:20
  6.1 1.6 %collective-permute-start.2 = (bf16[512,128]{1,0:T(8,128)(2,1)S(1)}, bf16[512,128]{1,0:T(8,128)(2,1)S(1)}, u32[]{:S(2)}, u32[]{:S(2)}) collective-permute-start(bf16[512,128]{1,0:T(8,128)(2,1)S(1)} %pad_maximum_fusion.1), channel_id=1, source_target_pairs={{0,8},{1,9},{2,11},{3,10},{4,12},{5,13},{6,15},{7,14},{8,16},{9,17... | collective-permute-start | bytes 393224 | tf_op jit(solution)/shard_map/ppermute | solution.py:20
  7.7 0.0 collective-permute-done.1.by_x
  7.7 1.9 %shard_map.77 = (f32[384,1024]{1,0:T(8,128)S(1)}, f32[384,1024]{1,0:T(8,128)S(1)}, f32[16,1024]{1,0:T(8,128)S(1)}, bf16[1024,128]{1,0:T(8,128)(2,1)S(1)}, bf16[1...) custom-call(s32[16]{0:T(128)} %doc_hbm.1, bf16[128,1024]{1,0:T(8,128)(2,1)} %q_hbm.1, bf16[128,1024]{1,0:T(8,128)(2,1)} %do_hbm.1, ...), custom_call_target="tpu_custom_call" | custom-call | flops 1342177280 | bytes 20971520 | tf_op jit(solution)/shard_map/pallas_call | solution.py:525
  9.6 4.0 %collective-permute-done.3.by_4 = bf16[512,128]{1,0:T(8,128)(2,1)S(1)} collective-permute-done((bf16[512,128]{1,0:T(8,128)(2,1)S(1)}, bf16[512,128]{1,0:T(8,128)(2,1)S(1)}, u32[]{:S(2)}, u32[]{:S(2)}) %collective-permute-start.3) | collective-permute-done | bytes 131104 | tf_op jit(solution)/shard_map/ppermute | solution.py:20
  13.6 0.2 collective-permute-done.2.by_8
  13.9 0.1 collective-permute-start.4
  14.0 1.5 %collective-permute-done.4.fetched = bf16[1024,128]{1,0:T(8,128)(2,1)S(1)} collective-permute-done((bf16[1024,128]{1,0:T(8,128)(2,1)S(1)}, bf16[1024,128]{1,0:T(8,128)(2,1)S(1)}, u32[]{:S(2)}, u32[]{:S(2)}) %collective-permute-start.4) | collective-permute-done | bytes 262176 | tf_op jit(solution)/shard_map/ppermute | solution.py:20
  15.5 0.7 %shard_map.79 = (bf16[1024,128]{1,0:T(8,128)(2,1)S(1)}, bf16[512,1024]{1,0:T(8,128)(2,1)S(1)}, f32[8,1024]{1,0:T(8,128)S(1)}) custom-call(bf16[1024,128]{1,0:T(8,128)(2,1)S(1)} %get-tuple-element.25.q_rows, bf16[1024,128]{1,0:T(8,128)(2,1)S(1)} %get-tuple-element.26.do_rows, s32[8,128]{1,0:T(8,128)S(1)} %get-tuple-element.29.starts, ...), custom_call_target="tpu_custom_call" | custom-call | flops 536870912 | bytes 8388608 | tf_op jit(solution)/shard_map/pallas_call | solution.py:525
  16.2 0.2 collective-permute-start.5
  16.4 0.3 %shard_map.80 = (f32[1280,128]{1,0:T(8,128)S(1)}, bf16[640,1024]{1,0:T(8,128)(2,1)S(1)}) custom-call(bf16[1024,128]{1,0:T(8,128)(2,1)S(1)} %get-tuple-element.25.q_rows, bf16[1024,128]{1,0:T(8,128)(2,1)S(1)} %get-tuple-element.26.do_rows, f32[384,1024]{1,0:T(8,128)S(1)} %get-tuple-element.27.p_near.p_ref, f32[384,1024]{1,0:T(8,128)S(1)} %get-tuple-element.28.dp_near.dp_ref, ...), custom_call_target="tpu_custom_call" | custom-call | flops 335544320 | bytes 5242880 | tf_op jit(solution)/shard_map/pallas_call | solution.py:525
  16.7 1.1 %collective-permute-done.5 = bf16[1024,128]{1,0:T(8,128)(2,1)S(1)} collective-permute-done((bf16[1024,128]{1,0:T(8,128)(2,1)S(1)}, bf16[1024,128]{1,0:T(8,128)(2,1)S(1)}, u32[]{:S(2)}, u32[]{:S(2)}) %collective-permute-start.5) | collective-permute-done | bytes 262176 | tf_op jit(solution)/shard_map/ppermute | solution.py:20
  17.9 1.0 %collective-permute-start.6 = (bf16[256,128]{1,0:T(8,128)(2,1)S(1)}, bf16[256,128]{1,0:T(8,128)(2,1)S(1)}, u32[]{:S(2)}, u32[]{:S(2)}) collective-permute-start(bf16[256,128]{1,0:T(8,128)(2,1)S(1)} %get-tuple-element.49), channel_id=1, source_target_pairs={{0,1},{1,0},{2,3},{3,2},{4,5},{5,4},{6,7},{7,6},{8,9},{9,8},{10,11... | collective-permute-start | bytes 196616 | tf_op jit(solution)/shard_map/ppermute | solution.py:20
  18.9 3.3 %collective-permute-start.7 = (bf16[512,128]{1,0:T(8,128)(2,1)S(1)}, bf16[512,128]{1,0:T(8,128)(2,1)S(1)}, u32[]{:S(2)}, u32[]{:S(2)}) collective-permute-start(bf16[512,128]{1,0:T(8,128)(2,1)S(1)} %pad_maximum_fusion.2), channel_id=1, source_target_pairs={{0,24},{1,25},{2,26},{3,27},{4,28},{5,29},{6,30},{7,31},{8,0},{9,1... | collective-permute-start | bytes 393224 | tf_op jit(solution)/shard_map/ppermute | solution.py:20
  22.2 2.3 %collective-permute-start.8 = (bf16[512,128]{1,0:T(8,128)(2,1)S(1)}, bf16[512,128]{1,0:T(8,128)(2,1)S(1)}, u32[]{:S(2)}, u32[]{:S(2)}) collective-permute-start(bf16[512,128]{1,0:T(8,128)(2,1)S(1)} %fusion), channel_id=1, source_target_pairs={{0,28},{1,29},{2,30},{3,31},{4,0},{5,1},{6,3},{7,2},{8,4},{9,5},{1... | collective-permute-start | bytes 393224 | tf_op jit(solution)/shard_map/ppermute | solution.py:20
  24.5 0.0 collective-permute-done.6.back_x
  24.5 1.6 %shard_map.81 = (bf16[128,1024]{1,0:T(8,128)(2,1)}, f32[256,128]{1,0:T(8,128)S(1)}, f32[256,128]{1,0:T(8,128)S(1)}) custom-call(bf16[1024,128]{1,0:T(8,128)(2,1)S(1)} %get-tuple-element.25.q_rows, bf16[1024,128]{1,0:T(8,128)(2,1)S(1)} %get-tuple-element.26.do_rows, f32[384,1024]{1,0:T(8,128)S(1)} %get-tuple-element.27.p_near.p_ref, ...), custom_call_target="tpu_custom_call" | custom-call | flops 1342177280 | bytes 20971520 | tf_op jit(solution)/shard_map/pallas_call | solution.py:525
  26.2 0.0 collective-permute-done.7
  26.2 2.5 %collective-permute-done.8 = bf16[512,128]{1,0:T(8,128)(2,1)S(1)} collective-permute-done((bf16[512,128]{1,0:T(8,128)(2,1)S(1)}, bf16[512,128]{1,0:T(8,128)(2,1)S(1)}, u32[]{:S(2)}, u32[]{:S(2)}) %collective-permute-start.8) | collective-permute-done | bytes 131104 | tf_op jit(solution)/shard_map/ppermute | solution.py:20
  28.8 0.1 collective-permute-start.9
  28.9 1.2 %collective-permute-done.9.last = bf16[256,128]{1,0:T(8,128)(2,1)S(1)} collective-permute-done((bf16[256,128]{1,0:T(8,128)(2,1)S(1)}, bf16[256,128]{1,0:T(8,128)(2,1)S(1)}, u32[]{:S(2)}, u32[]{:S(2)}) %collective-permute-start.9) | collective-permute-done | bytes 65568 | tf_op jit(solution)/shard_map/ppermute | solution.py:20
  30.1 0.6 %shard_map.82 = (bf16[128,128]{1,0:T(8,128)(2,1)}, bf16[128,128]{1,0:T(8,128)(2,1)}) custom-call(f32[256,128]{1,0:T(8,128)S(1)} %get-tuple-element.43.mine, f32[512,128]{1,0:T(8,128)S(1)} %convert_add_fusion.far, bf16[256,128]{1,0:T(8,128)(2,1)S(1)} %collective-permute-done.9.last), custom_call_target="tpu_custom_call" | custom-call | tf_op jit(solution)/shard_map/pallas_call | solution.py:525
  (10 shorter events, 0.2 us)
Async XLA Ops:
  1.4 3.1 %collective-permute-start = (bf16[256,128]{1,0:T(8,128)(2,1)S(1)}, bf16[256,128]{1,0:T(8,128)(2,1)S(1)}, u32[]{:S(2)}, u32[]{:S(2)}) collective-permute-start(bf16[256,128]{1,0:T(8,128)(2,1)S(1)} %shard_map.76.own), channel_id=1, source_target_pairs={{0,2},{1,3},{2,0},{3,1},{4,6},{5,7},{6,4},{7,5},{8,10},{9,11},{10,... | collective-permute-start | bytes 196616 | tf_op jit(solution)/shard_map/ppermute | solution.py:20
  1.9 5.7 %collective-permute-start.1 = (bf16[256,128]{1,0:T(8,128)(2,1)S(1)}, bf16[256,128]{1,0:T(8,128)(2,1)S(1)}, u32[]{:S(2)}, u32[]{:S(2)}) collective-permute-start(bf16[256,128]{1,0:T(8,128)(2,1)S(1)} %shard_map.76.own), channel_id=1, source_target_pairs={{0,1},{1,0},{2,3},{3,2},{4,5},{5,4},{6,7},{7,6},{8,9},{9,8},{10,11... | collective-permute-start | bytes 196616 | tf_op jit(solution)/shard_map/ppermute | solution.py:20
  4.5 9.1 %collective-permute-start.3 = (bf16[512,128]{1,0:T(8,128)(2,1)S(1)}, bf16[512,128]{1,0:T(8,128)(2,1)S(1)}, u32[]{:S(2)}, u32[]{:S(2)}) collective-permute-start(bf16[512,128]{1,0:T(8,128)(2,1)S(1)} %pad_maximum_fusion.1), channel_id=1, source_target_pairs={{0,4},{1,5},{2,7},{3,6},{4,8},{5,9},{6,11},{7,10},{8,12},{9,13},{1... | collective-permute-start | bytes 393224 | tf_op jit(solution)/shard_map/ppermute | solution.py:20
  6.1 7.7 %collective-permute-start.2 = (bf16[512,128]{1,0:T(8,128)(2,1)S(1)}, bf16[512,128]{1,0:T(8,128)(2,1)S(1)}, u32[]{:S(2)}, u32[]{:S(2)}) collective-permute-start(bf16[512,128]{1,0:T(8,128)(2,1)S(1)} %pad_maximum_fusion.1), channel_id=1, source_target_pairs={{0,8},{1,9},{2,11},{3,10},{4,12},{5,13},{6,15},{7,14},{8,16},{9,17... | collective-permute-start | bytes 393224 | tf_op jit(solution)/shard_map/ppermute | solution.py:20
  13.9 1.6 %collective-permute-start.4 = (bf16[1024,128]{1,0:T(8,128)(2,1)S(1)}, bf16[1024,128]{1,0:T(8,128)(2,1)S(1)}, u32[]{:S(2)}, u32[]{:S(2)}) collective-permute-start(bf16[1024,128]{1,0:T(8,128)(2,1)S(1)} %pad_maximum_fusion), channel_id=1, source_target_pairs={{0,2},{1,3},{2,0},{3,1},{4,6},{5,7},{6,4},{7,5},{8,10},{9,11},{10,... | collective-permute-start | bytes 786440 | tf_op jit(solution)/shard_map/ppermute | solution.py:20
  16.2 1.6 %collective-permute-start.5 = (bf16[1024,128]{1,0:T(8,128)(2,1)S(1)}, bf16[1024,128]{1,0:T(8,128)(2,1)S(1)}, u32[]{:S(2)}, u32[]{:S(2)}) collective-permute-start(bf16[1024,128]{1,0:T(8,128)(2,1)S(1)} %get-tuple-element.41), channel_id=1, source_target_pairs={{0,2},{1,3},{2,0},{3,1},{4,6},{5,7},{6,4},{7,5},{8,10},{9,11},{10,... | collective-permute-start | bytes 786440 | tf_op jit(solution)/shard_map/ppermute | solution.py:20
  17.9 6.6 %collective-permute-start.6 = (bf16[256,128]{1,0:T(8,128)(2,1)S(1)}, bf16[256,128]{1,0:T(8,128)(2,1)S(1)}, u32[]{:S(2)}, u32[]{:S(2)}) collective-permute-start(bf16[256,128]{1,0:T(8,128)(2,1)S(1)} %get-tuple-element.49), channel_id=1, source_target_pairs={{0,1},{1,0},{2,3},{3,2},{4,5},{5,4},{6,7},{7,6},{8,9},{9,8},{10,11... | collective-permute-start | bytes 196616 | tf_op jit(solution)/shard_map/ppermute | solution.py:20
  18.9 7.2 %collective-permute-start.7 = (bf16[512,128]{1,0:T(8,128)(2,1)S(1)}, bf16[512,128]{1,0:T(8,128)(2,1)S(1)}, u32[]{:S(2)}, u32[]{:S(2)}) collective-permute-start(bf16[512,128]{1,0:T(8,128)(2,1)S(1)} %pad_maximum_fusion.2), channel_id=1, source_target_pairs={{0,24},{1,25},{2,26},{3,27},{4,28},{5,29},{6,30},{7,31},{8,0},{9,1... | collective-permute-start | bytes 393224 | tf_op jit(solution)/shard_map/ppermute | solution.py:20
  22.2 6.5 %collective-permute-start.8 = (bf16[512,128]{1,0:T(8,128)(2,1)S(1)}, bf16[512,128]{1,0:T(8,128)(2,1)S(1)}, u32[]{:S(2)}, u32[]{:S(2)}) collective-permute-start(bf16[512,128]{1,0:T(8,128)(2,1)S(1)} %fusion), channel_id=1, source_target_pairs={{0,28},{1,29},{2,30},{3,31},{4,0},{5,1},{6,3},{7,2},{8,4},{9,5},{1... | collective-permute-start | bytes 393224 | tf_op jit(solution)/shard_map/ppermute | solution.py:20
  28.8 1.3 %collective-permute-start.9 = (bf16[256,128]{1,0:T(8,128)(2,1)S(1)}, bf16[256,128]{1,0:T(8,128)(2,1)S(1)}, u32[]{:S(2)}, u32[]{:S(2)}) collective-permute-start(bf16[256,128]{1,0:T(8,128)(2,1)S(1)} %fusion.1), channel_id=1, source_target_pairs={{0,2},{1,3},{2,0},{3,1},{4,6},{5,7},{6,4},{7,5},{8,10},{9,11},{10,... | collective-permute-start | bytes 196616 | tf_op jit(solution)/shard_map/ppermute | solution.py:20

commit v5 on v4

--- a/solution.py
+++ b/solution.py
@@ -555,7 +555,7 @@
     by_x = permuted(own, across_x)
     both = jnp.concatenate([own, partner], axis=0)
     by_4 = permuted(both, functools.partial(ahead, 4))
-    by_8 = permuted(both, functools.partial(ahead, 8))
+    by_8 = jnp.concatenate([permuted(own, functools.partial(ahead, 8)), permuted(partner, functools.partial(ahead, 8))], axis=0)
     outs, scratch = part(3)
     p_near, dp_near, stats_near, q_rows, do_rows, starts = local_call(
         functools.partial(near_kernel, docs),

time: 31.1 us -> 30.2 us (0.971)
  waiting for transfers between devices: 10.6 us -> 8.9 us
  starting transfers between devices: 13.2 us -> 14 us
    ppermute x10 -> x11, waiting for transfers between devices: 10.6 us -> 8.9 us  [permuted(): lax.ppermute(value, AXES, [(at, target(at, count)) for at in range(count)])]
    ppermute x10 -> x11, starting transfers between devices: 13.2 us -> 14 us  [permuted(): lax.ppermute(value, AXES, [(at, target(at, count)) for at in range(count)])]
  transfers between devices with their start and end apart: 10 -> 11, of which waited for: 6 -> 7; matrix products, arithmetic and copies ran while one was open for 0% -> 0% of each run, Pallas kernels for 13% -> 13%
where the time goes in v5:
time: 30.2 us; the launch traced here: 29.9 us
  starting transfers between devices  14 us (46%)
  waiting for transfers between devices  8.9 us (29%)
  Pallas kernels  6.05 us (20%)
  between operations  0.75 us (2%)
    ppermute x11, starting transfers between devices, permuted(): lax.ppermute(value, AXES, [(at, target(at, count)) for at in range(count)])  14 us
    ppermute x11, waiting for transfers between devices, permuted(): lax.ppermute(value, AXES, [(at, target(at, count)) for at in range(count)])  8.9 us
    pallas_call x7, Pallas kernels, local_call(): pl.pallas_call(kernel, out_shape=[jax.ShapeDtypeStruct(shape, kind) for s...  6.05 us
  transfers between devices with their start and end apart: 11, of which 7 were waited for; matrix products, arithmetic and copies ran while one was open for 0% of the time, Pallas kernels for 13%

profile of v5, /device:TPU:0, one launch (start us, length us, event | category | flops | bytes accessed | tf_op | source)
XLA Modules:
  0.0 29.9 jit_solution(5736232346368001121)
XLA Ops:
  0.6 0.8 %shard_map.76.own = bf16[256,128]{1,0:T(8,128)(2,1)S(1)} custom-call(bf16[128,128]{1,0:T(8,128)(2,1)} %keys.1, bf16[128,128]{1,0:T(8,128)(2,1)} %values.1), custom_call_target="tpu_custom_call" | custom-call | tf_op jit(solution)/shard_map/pallas_call | solution.py:525
  1.4 0.5 %collective-permute-start = (bf16[256,128]{1,0:T(8,128)(2,1)S(1)}, bf16[256,128]{1,0:T(8,128)(2,1)S(1)}, u32[]{:S(2)}, u32[]{:S(2)}) collective-permute-start(bf16[256,128]{1,0:T(8,128)(2,1)S(1)} %shard_map.76.own), channel_id=1, source_target_pairs={{0,2},{1,3},{2,0},{3,1},{4,6},{5,7},{6,4},{7,5},{8,10},{9,11},{10,... | collective-permute-start | bytes 196616 | tf_op jit(solution)/shard_map/ppermute | solution.py:20
  1.9 2.6 %collective-permute-start.2 = (bf16[256,128]{1,0:T(8,128)(2,1)S(1)}, bf16[256,128]{1,0:T(8,128)(2,1)S(1)}, u32[]{:S(2)}, u32[]{:S(2)}) collective-permute-start(bf16[256,128]{1,0:T(8,128)(2,1)S(1)} %shard_map.76.own), channel_id=1, source_target_pairs={{0,8},{1,9},{2,11},{3,10},{4,12},{5,13},{6,15},{7,14},{8,16},{9,17... | collective-permute-start | bytes 196616 | tf_op jit(solution)/shard_map/ppermute | solution.py:20
  4.6 1.5 %collective-permute-start.1 = (bf16[256,128]{1,0:T(8,128)(2,1)S(1)}, bf16[256,128]{1,0:T(8,128)(2,1)S(1)}, u32[]{:S(2)}, u32[]{:S(2)}) collective-permute-start(bf16[256,128]{1,0:T(8,128)(2,1)S(1)} %shard_map.76.own), channel_id=1, source_target_pairs={{0,1},{1,0},{2,3},{3,2},{4,5},{5,4},{6,7},{7,6},{8,9},{9,8},{10,11... | collective-permute-start | bytes 196616 | tf_op jit(solution)/shard_map/ppermute | solution.py:20
  6.1 0.0 collective-permute-done.partner
  6.1 1.6 %collective-permute-start.4 = (bf16[512,128]{1,0:T(8,128)(2,1)S(1)}, bf16[512,128]{1,0:T(8,128)(2,1)S(1)}, u32[]{:S(2)}, u32[]{:S(2)}) collective-permute-start(bf16[512,128]{1,0:T(8,128)(2,1)S(1)} %pad_maximum_fusion.2), channel_id=1, source_target_pairs={{0,4},{1,5},{2,7},{3,6},{4,8},{5,9},{6,11},{7,10},{8,12},{9,13},{1... | collective-permute-start | bytes 393224 | tf_op jit(solution)/shard_map/ppermute | solution.py:20
  7.7 1.6 %collective-permute-start.3 = (bf16[256,128]{1,0:T(8,128)(2,1)S(1)}, bf16[256,128]{1,0:T(8,128)(2,1)S(1)}, u32[]{:S(2)}, u32[]{:S(2)}) collective-permute-start(bf16[256,128]{1,0:T(8,128)(2,1)S(1)} %collective-permute-done.partner), channel_id=1, source_target_pairs={{0,8},{1,9},{2,11},{3,10},{4,12},{5,13},{6,15},{7,14},{8,16},{9,17... | collective-permute-start | bytes 196616 | tf_op jit(solution)/shard_map/ppermute | solution.py:20
  9.2 0.2 collective-permute-done.1.by_x
  9.4 1.9 %shard_map.77 = (f32[384,1024]{1,0:T(8,128)S(1)}, f32[384,1024]{1,0:T(8,128)S(1)}, f32[16,1024]{1,0:T(8,128)S(1)}, bf16[1024,128]{1,0:T(8,128)(2,1)S(1)}, bf16[1...) custom-call(s32[16]{0:T(128)} %doc_hbm.1, bf16[128,1024]{1,0:T(8,128)(2,1)} %q_hbm.1, bf16[128,1024]{1,0:T(8,128)(2,1)} %do_hbm.1, ...), custom_call_target="tpu_custom_call" | custom-call | flops 1342177280 | bytes 20971520 | tf_op jit(solution)/shard_map/pallas_call | solution.py:525
  11.3 0.0 collective-permute-done.2
  11.3 2.6 %collective-permute-done.3 = bf16[256,128]{1,0:T(8,128)(2,1)S(1)} collective-permute-done((bf16[256,128]{1,0:T(8,128)(2,1)S(1)}, bf16[256,128]{1,0:T(8,128)(2,1)S(1)}, u32[]{:S(2)}, u32[]{:S(2)}) %collective-permute-start.3) | collective-permute-done | bytes 65568 | tf_op jit(solution)/shard_map/ppermute | solution.py:20
  14.0 0.7 %collective-permute-done.4.by_4 = bf16[512,128]{1,0:T(8,128)(2,1)S(1)} collective-permute-done((bf16[512,128]{1,0:T(8,128)(2,1)S(1)}, bf16[512,128]{1,0:T(8,128)(2,1)S(1)}, u32[]{:S(2)}, u32[]{:S(2)}) %collective-permute-start.4) | collective-permute-done | bytes 131104 | tf_op jit(solution)/shard_map/ppermute | solution.py:20
  14.7 0.1 collective-permute-start.5
  14.8 1.5 %collective-permute-done.5.fetched = bf16[1024,128]{1,0:T(8,128)(2,1)S(1)} collective-permute-done((bf16[1024,128]{1,0:T(8,128)(2,1)S(1)}, bf16[1024,128]{1,0:T(8,128)(2,1)S(1)}, u32[]{:S(2)}, u32[]{:S(2)}) %collective-permute-start.5) | collective-permute-done | bytes 262176 | tf_op jit(solution)/shard_map/ppermute | solution.py:20
  16.3 0.7 %shard_map.79 = (bf16[1024,128]{1,0:T(8,128)(2,1)S(1)}, bf16[512,1024]{1,0:T(8,128)(2,1)S(1)}, f32[8,1024]{1,0:T(8,128)S(1)}) custom-call(bf16[1024,128]{1,0:T(8,128)(2,1)S(1)} %get-tuple-element.25.q_rows, bf16[1024,128]{1,0:T(8,128)(2,1)S(1)} %get-tuple-element.26.do_rows, s32[8,128]{1,0:T(8,128)S(1)} %get-tuple-element.29.starts, ...), custom_call_target="tpu_custom_call" | custom-call | flops 536870912 | bytes 8388608 | tf_op jit(solution)/shard_map/pallas_call | solution.py:525
  17.0 0.2 collective-permute-start.6
  17.3 0.3 %shard_map.80 = (f32[1280,128]{1,0:T(8,128)S(1)}, bf16[640,1024]{1,0:T(8,128)(2,1)S(1)}) custom-call(bf16[1024,128]{1,0:T(8,128)(2,1)S(1)} %get-tuple-element.25.q_rows, bf16[1024,128]{1,0:T(8,128)(2,1)S(1)} %get-tuple-element.26.do_rows, f32[384,1024]{1,0:T(8,128)S(1)} %get-tuple-element.27.p_near.p_ref, f32[384,1024]{1,0:T(8,128)S(1)} %get-tuple-element.28.dp_near.dp_ref, ...), custom_call_target="tpu_custom_call" | custom-call | flops 335544320 | bytes 5242880 | tf_op jit(solution)/shard_map/pallas_call | solution.py:525
  17.6 1.1 %collective-permute-done.6 = bf16[1024,128]{1,0:T(8,128)(2,1)S(1)} collective-permute-done((bf16[1024,128]{1,0:T(8,128)(2,1)S(1)}, bf16[1024,128]{1,0:T(8,128)(2,1)S(1)}, u32[]{:S(2)}, u32[]{:S(2)}) %collective-permute-start.6) | collective-permute-done | bytes 262176 | tf_op jit(solution)/shard_map/ppermute | solution.py:20
  18.8 1.1 %collective-permute-start.7 = (bf16[256,128]{1,0:T(8,128)(2,1)S(1)}, bf16[256,128]{1,0:T(8,128)(2,1)S(1)}, u32[]{:S(2)}, u32[]{:S(2)}) collective-permute-start(bf16[256,128]{1,0:T(8,128)(2,1)S(1)} %get-tuple-element.49), channel_id=1, source_target_pairs={{0,1},{1,0},{2,3},{3,2},{4,5},{5,4},{6,7},{7,6},{8,9},{9,8},{10,11... | collective-permute-start | bytes 196616 | tf_op jit(solution)/shard_map/ppermute | solution.py:20
  19.9 2.0 %collective-permute-start.8 = (bf16[512,128]{1,0:T(8,128)(2,1)S(1)}, bf16[512,128]{1,0:T(8,128)(2,1)S(1)}, u32[]{:S(2)}, u32[]{:S(2)}) collective-permute-start(bf16[512,128]{1,0:T(8,128)(2,1)S(1)} %pad_maximum_fusion.3), channel_id=1, source_target_pairs={{0,24},{1,25},{2,26},{3,27},{4,28},{5,29},{6,30},{7,31},{8,0},{9,1... | collective-permute-start | bytes 393224 | tf_op jit(solution)/shard_map/ppermute | solution.py:20
  21.9 2.8 %collective-permute-start.9 = (bf16[512,128]{1,0:T(8,128)(2,1)S(1)}, bf16[512,128]{1,0:T(8,128)(2,1)S(1)}, u32[]{:S(2)}, u32[]{:S(2)}) collective-permute-start(bf16[512,128]{1,0:T(8,128)(2,1)S(1)} %fusion), channel_id=1, source_target_pairs={{0,28},{1,29},{2,30},{3,31},{4,0},{5,1},{6,3},{7,2},{8,4},{9,5},{1... | collective-permute-start | bytes 393224 | tf_op jit(solution)/shard_map/ppermute | solution.py:20
  24.6 0.0 collective-permute-done.7.back_x
  24.6 1.7 %shard_map.81 = (bf16[128,1024]{1,0:T(8,128)(2,1)}, f32[256,128]{1,0:T(8,128)S(1)}, f32[256,128]{1,0:T(8,128)S(1)}) custom-call(bf16[1024,128]{1,0:T(8,128)(2,1)S(1)} %get-tuple-element.25.q_rows, bf16[1024,128]{1,0:T(8,128)(2,1)S(1)} %get-tuple-element.26.do_rows, f32[384,1024]{1,0:T(8,128)S(1)} %get-tuple-element.27.p_near.p_ref, ...), custom_call_target="tpu_custom_call" | custom-call | flops 1342177280 | bytes 20971520 | tf_op jit(solution)/shard_map/pallas_call | solution.py:525
  26.3 0.0 collective-permute-done.8
  26.3 1.6 %collective-permute-done.9 = bf16[512,128]{1,0:T(8,128)(2,1)S(1)} collective-permute-done((bf16[512,128]{1,0:T(8,128)(2,1)S(1)}, bf16[512,128]{1,0:T(8,128)(2,1)S(1)}, u32[]{:S(2)}, u32[]{:S(2)}) %collective-permute-start.9) | collective-permute-done | bytes 131104 | tf_op jit(solution)/shard_map/ppermute | solution.py:20
  27.9 0.1 collective-permute-start.10
  28.0 1.2 %collective-permute-done.10.last = bf16[256,128]{1,0:T(8,128)(2,1)S(1)} collective-permute-done((bf16[256,128]{1,0:T(8,128)(2,1)S(1)}, bf16[256,128]{1,0:T(8,128)(2,1)S(1)}, u32[]{:S(2)}, u32[]{:S(2)}) %collective-permute-start.10) | collective-permute-done | bytes 65568 | tf_op jit(solution)/shard_map/ppermute | solution.py:20
  29.3 0.6 %shard_map.82 = (bf16[128,128]{1,0:T(8,128)(2,1)}, bf16[128,128]{1,0:T(8,128)(2,1)}) custom-call(f32[256,128]{1,0:T(8,128)S(1)} %get-tuple-element.43.mine, f32[512,128]{1,0:T(8,128)S(1)} %convert_add_fusion.far, bf16[256,128]{1,0:T(8,128)(2,1)S(1)} %collective-permute-done.10.last), custom_call_target="tpu_custom_call" | custom-call | tf_op jit(solution)/shard_map/pallas_call | solution.py:525
  (11 shorter events, 0.2 us)
Async XLA Ops:
  1.4 4.6 %collective-permute-start = (bf16[256,128]{1,0:T(8,128)(2,1)S(1)}, bf16[256,128]{1,0:T(8,128)(2,1)S(1)}, u32[]{:S(2)}, u32[]{:S(2)}) collective-permute-start(bf16[256,128]{1,0:T(8,128)(2,1)S(1)} %shard_map.76.own), channel_id=1, source_target_pairs={{0,2},{1,3},{2,0},{3,1},{4,6},{5,7},{6,4},{7,5},{8,10},{9,11},{10,... | collective-permute-start | bytes 196616 | tf_op jit(solution)/shard_map/ppermute | solution.py:20
  1.9 9.4 %collective-permute-start.2 = (bf16[256,128]{1,0:T(8,128)(2,1)S(1)}, bf16[256,128]{1,0:T(8,128)(2,1)S(1)}, u32[]{:S(2)}, u32[]{:S(2)}) collective-permute-start(bf16[256,128]{1,0:T(8,128)(2,1)S(1)} %shard_map.76.own), channel_id=1, source_target_pairs={{0,8},{1,9},{2,11},{3,10},{4,12},{5,13},{6,15},{7,14},{8,16},{9,17... | collective-permute-start | bytes 196616 | tf_op jit(solution)/shard_map/ppermute | solution.py:20
  4.6 4.8 %collective-permute-start.1 = (bf16[256,128]{1,0:T(8,128)(2,1)S(1)}, bf16[256,128]{1,0:T(8,128)(2,1)S(1)}, u32[]{:S(2)}, u32[]{:S(2)}) collective-permute-start(bf16[256,128]{1,0:T(8,128)(2,1)S(1)} %shard_map.76.own), channel_id=1, source_target_pairs={{0,1},{1,0},{2,3},{3,2},{4,5},{5,4},{6,7},{7,6},{8,9},{9,8},{10,11... | collective-permute-start | bytes 196616 | tf_op jit(solution)/shard_map/ppermute | solution.py:20
  6.1 8.6 %collective-permute-start.4 = (bf16[512,128]{1,0:T(8,128)(2,1)S(1)}, bf16[512,128]{1,0:T(8,128)(2,1)S(1)}, u32[]{:S(2)}, u32[]{:S(2)}) collective-permute-start(bf16[512,128]{1,0:T(8,128)(2,1)S(1)} %pad_maximum_fusion.2), channel_id=1, source_target_pairs={{0,4},{1,5},{2,7},{3,6},{4,8},{5,9},{6,11},{7,10},{8,12},{9,13},{1... | collective-permute-start | bytes 393224 | tf_op jit(solution)/shard_map/ppermute | solution.py:20
  7.7 6.3 %collective-permute-start.3 = (bf16[256,128]{1,0:T(8,128)(2,1)S(1)}, bf16[256,128]{1,0:T(8,128)(2,1)S(1)}, u32[]{:S(2)}, u32[]{:S(2)}) collective-permute-start(bf16[256,128]{1,0:T(8,128)(2,1)S(1)} %collective-permute-done.partner), channel_id=1, source_target_pairs={{0,8},{1,9},{2,11},{3,10},{4,12},{5,13},{6,15},{7,14},{8,16},{9,17... | collective-permute-start | bytes 196616 | tf_op jit(solution)/shard_map/ppermute | solution.py:20
  14.7 1.6 %collective-permute-start.5 = (bf16[1024,128]{1,0:T(8,128)(2,1)S(1)}, bf16[1024,128]{1,0:T(8,128)(2,1)S(1)}, u32[]{:S(2)}, u32[]{:S(2)}) collective-permute-start(bf16[1024,128]{1,0:T(8,128)(2,1)S(1)} %pad_maximum_fusion), channel_id=1, source_target_pairs={{0,2},{1,3},{2,0},{3,1},{4,6},{5,7},{6,4},{7,5},{8,10},{9,11},{10,... | collective-permute-start | bytes 786440 | tf_op jit(solution)/shard_map/ppermute | solution.py:20
  17.0 1.6 %collective-permute-start.6 = (bf16[1024,128]{1,0:T(8,128)(2,1)S(1)}, bf16[1024,128]{1,0:T(8,128)(2,1)S(1)}, u32[]{:S(2)}, u32[]{:S(2)}) collective-permute-start(bf16[1024,128]{1,0:T(8,128)(2,1)S(1)} %get-tuple-element.41), channel_id=1, source_target_pairs={{0,2},{1,3},{2,0},{3,1},{4,6},{5,7},{6,4},{7,5},{8,10},{9,11},{10,... | collective-permute-start | bytes 786440 | tf_op jit(solution)/shard_map/ppermute | solution.py:20
  18.8 5.9 %collective-permute-start.7 = (bf16[256,128]{1,0:T(8,128)(2,1)S(1)}, bf16[256,128]{1,0:T(8,128)(2,1)S(1)}, u32[]{:S(2)}, u32[]{:S(2)}) collective-permute-start(bf16[256,128]{1,0:T(8,128)(2,1)S(1)} %get-tuple-element.49), channel_id=1, source_target_pairs={{0,1},{1,0},{2,3},{3,2},{4,5},{5,4},{6,7},{7,6},{8,9},{9,8},{10,11... | collective-permute-start | bytes 196616 | tf_op jit(solution)/shard_map/ppermute | solution.py:20
  19.9 6.4 %collective-permute-start.8 = (bf16[512,128]{1,0:T(8,128)(2,1)S(1)}, bf16[512,128]{1,0:T(8,128)(2,1)S(1)}, u32[]{:S(2)}, u32[]{:S(2)}) collective-permute-start(bf16[512,128]{1,0:T(8,128)(2,1)S(1)} %pad_maximum_fusion.3), channel_id=1, source_target_pairs={{0,24},{1,25},{2,26},{3,27},{4,28},{5,29},{6,30},{7,31},{8,0},{9,1... | collective-permute-start | bytes 393224 | tf_op jit(solution)/shard_map/ppermute | solution.py:20
  21.9 6.0 %collective-permute-start.9 = (bf16[512,128]{1,0:T(8,128)(2,1)S(1)}, bf16[512,128]{1,0:T(8,128)(2,1)S(1)}, u32[]{:S(2)}, u32[]{:S(2)}) collective-permute-start(bf16[512,128]{1,0:T(8,128)(2,1)S(1)} %fusion), channel_id=1, source_target_pairs={{0,28},{1,29},{2,30},{3,31},{4,0},{5,1},{6,3},{7,2},{8,4},{9,5},{1... | collective-permute-start | bytes 393224 | tf_op jit(solution)/shard_map/ppermute | solution.py:20
  27.9 1.3 %collective-permute-start.10 = (bf16[256,128]{1,0:T(8,128)(2,1)S(1)}, bf16[256,128]{1,0:T(8,128)(2,1)S(1)}, u32[]{:S(2)}, u32[]{:S(2)}) collective-permute-start(bf16[256,128]{1,0:T(8,128)(2,1)S(1)} %fusion.1), channel_id=1, source_target_pairs={{0,2},{1,3},{2,0},{3,1},{4,6},{5,7},{6,4},{7,5},{8,10},{9,11},{10,... | collective-permute-start | bytes 196616 | tf_op jit(solution)/shard_map/ppermute | solution.py:20
